TPU v7x, 32 devices: a whole 2x2x4 slice. The times are simulated.
32 devices in a mesh: dp: 8 (over y, x, core), seq: 4 (over z).
Axes of the slice: x: 2, y: 2, z: 4, core: 2. Of those that a mesh axis runs over, the one named last changes fastest.
Arguments:
- tokens: bfloat16 [8, 2048, 768], P('dp', 'seq'), may hold values from -6 to 6
- cell_lengths: int32 [8, 8], P('dp'), may hold values from 0 to 2048, as said below
- ln1_gain: float32 [768], replicated, may hold values from 0.25 to 1.75
- ln1_shift: float32 [768], replicated, may hold values from -3 to 3
- w_qkv: bfloat16 [768, 2304], replicated, may hold values from -0.21875 to 0.21875
- b_query: float32 [768], replicated, may hold values from -3 to 3
- b_value: float32 [768], replicated, may hold values from -3 to 3
- w_out: bfloat16 [768, 768], replicated, may hold values from -2.5 to 2.5
- b_out: float32 [768], replicated, may hold values from -3 to 3
- ln2_gain: float32 [768], replicated, may hold values from 0.25 to 1.75
- ln2_shift: float32 [768], replicated, may hold values from -3 to 3
- w_up: bfloat16 [768, 3072], replicated, may hold values from -0.21875 to 0.21875
- b_up: float32 [3072], replicated, may hold values from -3 to 3
- w_down: bfloat16 [3072, 768], replicated, may hold values from -0.109375 to 0.109375
- b_down: float32 [768], replicated, may hold values from -3 to 3
- cotangent: bfloat16 [8, 2048, 768], P('dp', 'seq'), may hold values from -6 to 6
Outputs:
- layer_out: bfloat16 [8, 2048, 768], P('dp', 'seq')
- tokens_grad: bfloat16 [8, 2048, 768], P('dp', 'seq')
- ln1_gain_grad: float32 [768], P('dp')
- ln1_shift_grad: float32 [768], P('dp')
- w_qkv_grad: float32 [768, 2304], P('dp')
- b_query_grad: float32 [768], P('dp')
- b_value_grad: float32 [768], P('dp')
- w_out_grad: float32 [768, 768], P('dp')
- b_out_grad: float32 [768], P('dp')
- ln2_gain_grad: float32 [768], P('dp')
- ln2_shift_grad: float32 [768], P('dp')
- w_up_grad: float32 [768, 3072], P('dp')
- b_up_grad: float32 [3072], P('dp')
- w_down_grad: float32 [3072, 768], P('dp')
- b_down_grad: float32 [768], P('dp')
Inputs may be any that keep to these rules, and one draw needn't show every extreme that they name: `cell_lengths`: each row lists, in slot order, the lengths of the cells packed into one bucket of 2048 slots, and sums to 2048; an entry of 0 is an unused cell place.
All inputs are finite; a program needn't handle non-finite values.
Results may differ from a plain program's by a relative error of at most 0.015.
Values may be sent and summed in bfloat16 or wider, within the bound.
A program may use at most 192 MiB of HBM per device.

v0:
```python
from functools import partial

import jax
import jax.numpy as jnp
from jax import lax
from jax.sharding import PartitionSpec as P

HEADS = 12
HEAD = 64


EPS = 1e-05
ROOT_HALF = 0.7071067811865476


def normalize(values, gain, shift):
    average = jnp.mean(values, axis=-1, keepdims=True)
    centred = values - average
    variance = jnp.mean(centred * centred, axis=-1, keepdims=True)
    return centred * lax.rsqrt(variance + EPS) * gain + shift


def gelu_exact(values):
    return 0.5 * values * (1.0 + jax.scipy.special.erf(values * ROOT_HALF))


def segments_of(lengths, slot_count):
    cell_ends = jnp.cumsum(lengths, axis=-1)
    places = jnp.arange(slot_count, dtype=jnp.int32)
    return jnp.sum((places[:, None] >= cell_ends[..., None, :]).astype(jnp.int32), axis=-1)


def attend_heads(packed, segment, scaling):
    queries = packed[:, :, 0, :, :HEAD]
    key_part = packed[:, :, 0, :, HEAD : 2 * HEAD]
    value_part = packed[:, :, 0, :, 2 * HEAD :]
    bucket_count, slot_count, head_count = queries.shape[:3]
    block_rows = min(512, slot_count)

    def one_block(block_index):
        block_start = block_index * block_rows
        q_block = lax.dynamic_slice_in_dim(queries, block_start, block_rows, 1)
        seg_block = lax.dynamic_slice_in_dim(segment, block_start, block_rows, 1)
        scores = (
            jnp.einsum("bqhe,bkhe->bhqk", q_block, key_part, preferred_element_type=jnp.float32)
            * scaling
        )
        allowed = seg_block[:, None, :, None] == segment[:, None, None, :]
        scores = jnp.where(allowed, scores, -1e30)
        highest = jnp.max(scores, axis=-1, keepdims=True)
        raised = jnp.exp(scores - highest)
        totals = jnp.sum(raised, axis=-1, keepdims=True)
        weights = (raised / totals).astype(jnp.bfloat16)
        mixture = jnp.einsum(
            "bhqk,bkhe->bqhe", weights, value_part, preferred_element_type=jnp.float32
        )
        return (mixture.astype(jnp.bfloat16), (highest + jnp.log(totals))[..., 0])

    mixture, log_total = lax.map(one_block, jnp.arange(slot_count // block_rows))
    mixture = jnp.moveaxis(mixture, 0, 1).reshape(bucket_count, slot_count, head_count, HEAD)
    log_total = jnp.transpose(log_total, (1, 0, 3, 2)).reshape(bucket_count, slot_count, head_count)
    return (mixture[:, :, None], log_total[:, :, None])


def attend_back(heads_qkv, log_total, d_mixture, segment, scaling):
    queries = heads_qkv[..., :HEAD]
    key_part = heads_qkv[..., HEAD : 2 * HEAD]
    value_part = heads_qkv[..., 2 * HEAD :]
    slot_count = queries.shape[1]
    block_rows = min(512, slot_count)

    def one_block(carry, block_index):
        key_grad, value_grad = carry
        block_start = block_index * block_rows
        q_block = lax.dynamic_slice_in_dim(queries, block_start, block_rows, 1)
        seg_block = lax.dynamic_slice_in_dim(segment, block_start, block_rows, 1)
        lse_block = lax.dynamic_slice_in_dim(log_total, block_start, block_rows, 1)
        grad_block = lax.dynamic_slice_in_dim(d_mixture, block_start, block_rows, 1)
        scores = (
            jnp.einsum("bqhe,bkhe->bhqk", q_block, key_part, preferred_element_type=jnp.float32)
            * scaling
        )
        allowed = seg_block[:, None, :, None] == segment[:, None, None, :]
        scores = jnp.where(allowed, scores, -1e30)
        probs = jnp.exp(scores - jnp.transpose(lse_block, (0, 2, 1))[..., None])
        weights = probs.astype(jnp.bfloat16)
        value_grad = value_grad + jnp.einsum(
            "bhqk,bqhe->bkhe", weights, grad_block, preferred_element_type=jnp.float32
        )
        d_probs = jnp.einsum(
            "bqhe,bkhe->bhqk", grad_block, value_part, preferred_element_type=jnp.float32
        )
        inner = jnp.sum(probs * d_probs, axis=-1, keepdims=True)
        d_scores = (probs * (d_probs - inner)).astype(jnp.bfloat16)
        query_grad = (
            jnp.einsum("bhqk,bkhe->bqhe", d_scores, key_part, preferred_element_type=jnp.float32)
            * scaling
        )
        key_grad = (
            key_grad
            + jnp.einsum("bhqk,bqhe->bkhe", d_scores, q_block, preferred_element_type=jnp.float32)
            * scaling
        )
        return ((key_grad, value_grad), query_grad)

    zero_grad = jnp.zeros(key_part.shape, jnp.float32)
    (key_grad, value_grad), query_grad = lax.scan(
        one_block, (zero_grad, zero_grad), jnp.arange(slot_count // block_rows)
    )
    query_grad = jnp.moveaxis(query_grad, 0, 1).reshape(key_part.shape)
    return jnp.concatenate([query_grad, key_grad, value_grad], axis=-1).astype(jnp.bfloat16)


def local(
    tokens,
    cell_lengths,
    ln1_gain,
    ln1_shift,
    w_qkv,
    b_query,
    b_value,
    w_out,
    b_out,
    ln2_gain,
    ln2_shift,
    w_up,
    b_up,
    w_down,
    b_down,
    cotangent,
):
    bucket_count, local_slots, width = tokens.shape
    seq_count = lax.axis_size("seq")
    slot_count = local_slots * seq_count
    head_local = HEADS // seq_count
    scaling = HEAD ** (-0.5)
    row_count = bucket_count * local_slots
    segment = segments_of(cell_lengths, slot_count)
    flat_tokens = tokens.reshape(row_count, width).astype(jnp.float32)
    normed_one = normalize(flat_tokens, ln1_gain, ln1_shift).astype(jnp.bfloat16)
    bias_all = jnp.stack(
        [
            b_query.reshape(HEADS, HEAD),
            jnp.zeros((HEADS, HEAD), jnp.float32),
            b_value.reshape(HEADS, HEAD),
        ],
        axis=1,
    ).reshape(3 * width)

    def project_heads():
        projected = jnp.dot(normed_one, w_qkv, preferred_element_type=jnp.float32) + bias_all
        return projected.astype(jnp.bfloat16).reshape(
            bucket_count, local_slots, seq_count, head_local, 3 * HEAD
        )

    attend = partial(attend_heads, segment=segment, scaling=scaling)
    received = attend(
        lax.all_to_all(project_heads(), "seq", split_axis=2, concat_axis=1, tiled=True)
    )
    mixture = received[0].reshape(bucket_count, slot_count, 1, head_local * HEAD)
    log_total = received[1][:, :, 0]
    attended = lax.all_to_all(mixture, "seq", split_axis=1, concat_axis=2, tiled=True).reshape(
        row_count, width
    )
    middle = flat_tokens + jnp.dot(attended, w_out, preferred_element_type=jnp.float32) + b_out
    normed_two = normalize(middle, ln2_gain, ln2_shift).astype(jnp.bfloat16)
    upper = jnp.dot(normed_two, w_up, preferred_element_type=jnp.float32) + b_up
    hidden = gelu_exact(upper).astype(jnp.bfloat16)
    layer_out = middle + jnp.dot(hidden, w_down, preferred_element_type=jnp.float32) + b_down
    layer_out = layer_out.astype(jnp.bfloat16).reshape(tokens.shape)
    d_output = cotangent.reshape(row_count, width)
    g_w_down = jnp.dot(hidden.T, d_output, preferred_element_type=jnp.float32)
    g_b_down = jnp.sum(d_output, axis=0, dtype=jnp.float32)
    d_hidden = jnp.dot(d_output, w_down.T, preferred_element_type=jnp.float32)
    gelu_pull = jax.vjp(gelu_exact, upper)[1]
    d_upper = gelu_pull(d_hidden)[0].astype(jnp.bfloat16)
    g_w_up = jnp.dot(normed_two.T, d_upper, preferred_element_type=jnp.float32)
    g_b_up = jnp.sum(d_upper, axis=0, dtype=jnp.float32)
    d_normed_two = jnp.dot(d_upper, w_up.T, preferred_element_type=jnp.float32)
    second_pull = jax.vjp(normalize, middle, ln2_gain, ln2_shift)[1]
    d_middle, g_ln2_gain, g_ln2_shift = second_pull(d_normed_two)
    d_middle = d_middle + d_output.astype(jnp.float32)
    d_branch = d_middle.astype(jnp.bfloat16)
    g_w_out = jnp.dot(attended.T, d_branch, preferred_element_type=jnp.float32)
    g_b_out = jnp.sum(d_branch, axis=0, dtype=jnp.float32)
    d_attended = jnp.dot(d_branch, w_out.T, preferred_element_type=jnp.float32).astype(jnp.bfloat16)
    d_attended = d_attended.reshape(bucket_count, local_slots, seq_count, head_local * HEAD)
    d_mixture = lax.all_to_all(d_attended, "seq", split_axis=2, concat_axis=1, tiled=True)
    d_mixture = d_mixture.reshape(bucket_count, slot_count, head_local, HEAD)
    heads_qkv = lax.all_to_all(project_heads(), "seq", split_axis=2, concat_axis=1, tiled=True)
    heads_qkv = heads_qkv[:, :, 0]
    d_projected = attend_back(heads_qkv, log_total, d_mixture, segment, scaling)
    d_projected = lax.all_to_all(
        d_projected[:, :, None], "seq", split_axis=1, concat_axis=2, tiled=True
    )
    d_projected = d_projected.reshape(row_count, 3 * width)
    g_w_qkv = jnp.dot(normed_one.T, d_projected, preferred_element_type=jnp.float32)
    bias_sums = jnp.sum(d_projected, axis=0, dtype=jnp.float32).reshape(HEADS, 3, HEAD)
    g_b_query = bias_sums[:, 0].reshape(width)
    g_b_value = bias_sums[:, 2].reshape(width)
    d_normed_one = jnp.dot(d_projected, w_qkv.T, preferred_element_type=jnp.float32)
    first_pull = jax.vjp(normalize, flat_tokens, ln1_gain, ln1_shift)[1]
    d_tokens, g_ln1_gain, g_ln1_shift = first_pull(d_normed_one)
    tokens_grad = (d_tokens + d_middle).astype(jnp.bfloat16).reshape(tokens.shape)
    shares = (
        lax.psum_scatter(g_ln1_gain, "dp", scatter_dimension=0, tiled=True),
        lax.psum_scatter(g_ln1_shift, "dp", scatter_dimension=0, tiled=True),
        lax.psum_scatter(g_w_qkv, "dp", scatter_dimension=0, tiled=True),
        lax.psum_scatter(g_b_query, "dp", scatter_dimension=0, tiled=True),
        lax.psum_scatter(g_b_value, "dp", scatter_dimension=0, tiled=True),
        lax.psum_scatter(g_w_out, "dp", scatter_dimension=0, tiled=True),
        lax.psum_scatter(g_b_out, "dp", scatter_dimension=0, tiled=True),
        lax.psum_scatter(g_ln2_gain, "dp", scatter_dimension=0, tiled=True),
        lax.psum_scatter(g_ln2_shift, "dp", scatter_dimension=0, tiled=True),
        lax.psum_scatter(g_w_up, "dp", scatter_dimension=0, tiled=True),
        lax.psum_scatter(g_b_up, "dp", scatter_dimension=0, tiled=True),
        lax.psum_scatter(g_w_down, "dp", scatter_dimension=0, tiled=True),
        lax.psum_scatter(g_b_down, "dp", scatter_dimension=0, tiled=True),
    )
    summed = (
        lax.psum(shares[0].astype(jnp.bfloat16), "seq").astype(jnp.float32),
        lax.psum(shares[1].astype(jnp.bfloat16), "seq").astype(jnp.float32),
        lax.psum(shares[2].astype(jnp.bfloat16), "seq").astype(jnp.float32),
        lax.psum(shares[3].astype(jnp.bfloat16), "seq").astype(jnp.float32),
        lax.psum(shares[4].astype(jnp.bfloat16), "seq").astype(jnp.float32),
        lax.psum(shares[5].astype(jnp.bfloat16), "seq").astype(jnp.float32),
        lax.psum(shares[6].astype(jnp.bfloat16), "seq").astype(jnp.float32),
        lax.psum(shares[7].astype(jnp.bfloat16), "seq").astype(jnp.float32),
        lax.psum(shares[8].astype(jnp.bfloat16), "seq").astype(jnp.float32),
        lax.psum(shares[9].astype(jnp.bfloat16), "seq").astype(jnp.float32),
        lax.psum(shares[10].astype(jnp.bfloat16), "seq").astype(jnp.float32),
        lax.psum(shares[11].astype(jnp.bfloat16), "seq").astype(jnp.float32),
        lax.psum(shares[12].astype(jnp.bfloat16), "seq").astype(jnp.float32),
    )
    return (
        layer_out,
        tokens_grad,
        summed[0],
        summed[1],
        summed[2],
        summed[3],
        summed[4],
        summed[5],
        summed[6],
        summed[7],
        summed[8],
        summed[9],
        summed[10],
        summed[11],
        summed[12],
    )


def solution(mesh):
    placed = (
        P("dp", "seq", None),
        P("dp", None),
        P(),
        P(),
        P(),
        P(),
        P(),
        P(),
        P(),
        P(),
        P(),
        P(),
        P(),
        P(),
        P(),
        P("dp", "seq", None),
    )
    return jax.shard_map(
        local,
        mesh=mesh,
        in_specs=placed,
        out_specs=(
            P("dp", "seq", None),
            P("dp", "seq", None),
            P("dp"),
            P("dp"),
            P("dp", None),
            P("dp"),
            P("dp"),
            P("dp", None),
            P("dp"),
            P("dp"),
            P("dp"),
            P("dp", None),
            P("dp"),
            P("dp", None),
            P("dp"),
        ),
        check_vma=False,
    )
```

profile of v0, /device:TPU:0, one launch (start us, length us, event | category | flops | bytes accessed | tf_op | source)
XLA Modules:
  0.0 792.1 jit_solution(12877956960057919228)
XLA Ops:
  31.7 53.4 %all-to-all-done = bf16[1,512,4,3,192]{1,4,3,0,2:T(8,128)(2,1)} async-done(((bf16[1,512,4,3,192]{1,4,3,0,2:T(8,128)(2,1)}), bf16[1,512,4,3,192]{1,4,3,0,2:T(8,128)(2,1)}, u32[]{:S(2)}, u32[]{:S(2)}) %all-to-all-start) | async-done | bytes 2359328 | tf_op jit(solution)/shard_map/all_to_all | solution.py:158
  88.5 100.2 %while.27 = (s32[]{:T(128)}, bf16[4,1,512,3,64]{2,4,3,1,0:T(8,128)(2,1)}, f32[4,1,3,512]{3,2,1,0:T(4,128)}, s32[4]{0:T(128)S(1)}, s32[1,2048]{1,0:T(1,128)S(1)},...) while((s32[]{:T(128)}, ...), condition=%wide.region_7.8_spmd, body=%wide.region_4.7_spmd.sunk | while | flops 844200448 | bytes 47121616 | solution.py:59
  90.4 8.3 %fusion.135 = (f32[3,512]{1,0:T(4,128)S(1)}, f32[3,512,2048]{2,1,0:T(8,128)}) fusion(pred[512,2048]{1,0:T(8,128)(4,1)S(1)} %broadcast_compare_fusion.4, bf16[1,2048,3,64]{1,3,2,0:T(8,128)(2,1)} %get-tuple-element.406, bf16[1,2048,3,64]{1,3,2,0:T(8,128)(2,1)} %get-tuple-element.405, s32[]{:T(128)S(6)} %select_n.60), kind=kOutput, calls=%fused_computation.3.clone.1 | convolution fusion | flops 412088832 | bytes 14620676 | tf_op jit(solution)/shard_map/while/body/eval_jaxpr/bqhe,bkhe->bhqk/dot_general | solution.py:45
  98.8 6.8 fusion.136
  106.2 7.4 fusion.137
  115.5 8.3 %fusion.135 = (f32[3,512]{1,0:T(4,128)S(1)}, f32[3,512,2048]{2,1,0:T(8,128)}) fusion(pred[512,2048]{1,0:T(8,128)(4,1)S(1)} %broadcast_compare_fusion.4, bf16[1,2048,3,64]{1,3,2,0:T(8,128)(2,1)} %get-tuple-element.406, bf16[1,2048,3,64]{1,3,2,0:T(8,128)(2,1)} %get-tuple-element.405, s32[]{:T(128)S(6)} %select_n.60), kind=kOutput, calls=%fused_computation.3.clone.1 | convolution fusion | flops 412088832 | bytes 14620676 | tf_op jit(solution)/shard_map/while/body/eval_jaxpr/bqhe,bkhe->bhqk/dot_general | solution.py:45
  123.8 6.8 fusion.136
  131.3 7.4 fusion.137
  140.5 8.3 %fusion.135 = (f32[3,512]{1,0:T(4,128)S(1)}, f32[3,512,2048]{2,1,0:T(8,128)}) fusion(pred[512,2048]{1,0:T(8,128)(4,1)S(1)} %broadcast_compare_fusion.4, bf16[1,2048,3,64]{1,3,2,0:T(8,128)(2,1)} %get-tuple-element.406, bf16[1,2048,3,64]{1,3,2,0:T(8,128)(2,1)} %get-tuple-element.405, s32[]{:T(128)S(6)} %select_n.60), kind=kOutput, calls=%fused_computation.3.clone.1 | convolution fusion | flops 412088832 | bytes 14620676 | tf_op jit(solution)/shard_map/while/body/eval_jaxpr/bqhe,bkhe->bhqk/dot_general | solution.py:45
  156.3 7.4 fusion.137
  165.6 8.3 %fusion.135 = (f32[3,512]{1,0:T(4,128)S(1)}, f32[3,512,2048]{2,1,0:T(8,128)}) fusion(pred[512,2048]{1,0:T(8,128)(4,1)S(1)} %broadcast_compare_fusion.4, bf16[1,2048,3,64]{1,3,2,0:T(8,128)(2,1)} %get-tuple-element.406, bf16[1,2048,3,64]{1,3,2,0:T(8,128)(2,1)} %get-tuple-element.405, s32[]{:T(128)S(6)} %select_n.60), kind=kOutput, calls=%fused_computation.3.clone.1 | convolution fusion | flops 412088832 | bytes 14620676 | tf_op jit(solution)/shard_map/while/body/eval_jaxpr/bqhe,bkhe->bhqk/dot_general | solution.py:45
  181.4 7.4 fusion.137
  200.5 13.6 %reduce.14 = bf16[2048,192]{1,0:T(8,128)(2,1)} reduce(bf16[2048,1,1,192]{3,2,1,0:T(2,128)(2,1)} %bitcast.259, bf16[]{:T(256)} %broadcast.297), dimensions={1,2}, to_apply=%bitcast.174.reduce_sub_computation | reduce | bytes 1572866
  218.1 24.1 %all_to_all.68 = bf16[4,2,49152]{2,1,0:T(2,128)(2,1)} all-to-all(bf16[4,2,49152]{2,1,0:T(2,128)(2,1)} %reshape.479), channel_id=1, replica_groups=mesh['dp'=8,'seq'=4] {'seq'}, dimensions={0} | all-to-all | bytes 1572864 | tf_op jit(solution)/shard_map/all_to_all | solution.py:162
  259.2 7.2 multiply_convert_fusion.1
  282.3 9.0 %fusion.90 = f32[768,3072]{1,0:T(8,128)} fusion(bf16[512,3072]{1,0:T(8,128)(2,1)} %copy-done.42, f32[512,768]{1,0:T(8,128)} %copy-done.9, f32[768]{0:T(1024)} %param.30, f32[768]{0:T(1024)} %param.29, f32[512]{0:T(512)} %copy-done.32, f32[512]{0:T(512)S(1)} %broadcast_multiply_fusion), kind=kOutput, calls=%fused_computation.144 | convolution fusion | flops 2417885184 | bytes 14166016 | tf_op jit(solution)/shard_map/dot_general | solution.py:177
  326.8 175.4 %while.28 = (s32[]{:T(128)}, f32[1,2048,3,64]{1,3,2,0:T(8,128)}, f32[1,2048,3,64]{1,3,2,0:T(8,128)}, bf16[4,1,512,3,64]{2,4,3,1,0:T(8,128)(2,1)}, s32[4]{0:T(128...) while((s32[]{:T(128)}, f32[1,2048,3,64]{1,3,2,0:T(8,128)}, ...), condition=%wide.region_14.15_spmd.clone, body=%wide.region_12.14_spmd.clone.sunk | while | flops 2063563264 | bytes 220652432 | solution.py:107
  333.4 10.7 %multiply_reduce_fusion.5 = (f32[3,512]{1,0:T(4,128)S(1)}, f32[3,512,2048]{2,1,0:T(8,128)}) fusion(f32[3,512,2048]{2,1,0:T(8,128)S(1)} %fusion.146, f32[3,512]{1,0:T(4,128)S(1)} %dynamic-slice_bitcast_fusion.2, pred[512,2048]{1,0:T(8,128)(4,1)S(1)} %broadcast_compare_fusion.5, bf16[1,2048,3,64]{1,3,2,0:T(8,128)(2,1)S(1)} %copy-done.5, ...), kind=kOutput, calls=%fused_computation.21.clone.1 | convolution fusion | flops 418380288 | bytes 27209732 | tf_op jit(solution)/shard_map/while/body/eval_jaxpr/bqhe,bkhe->bhqk/dot_general | solution.py:90
  345.0 9.7 %multiply_convert_fusion.3 = bf16[3,512,2048]{2,1,0:T(8,128)(2,1)} fusion(f32[3,512,2048]{2,1,0:T(8,128)} %get-tuple-element.374, f32[3,512,2048]{2,1,0:T(8,128)S(1)} %fusion.146, f32[3,512]{1,0:T(4,128)S(1)} %get-tuple-element.375, f32[3,512]{1,0:T(4,128)S(1)} %dynamic-slice_bitcast_fusion.2, pred[512,2048]{1,0:T(8,128)(4,1)S(1)} %broadcast_compare_fusion.5), kind=kLoop, calls=%fused_computation.20.clone.1 | loop fusion | flops 18874368 | bytes 32518144 | tf_op jit(solution)/shard_map/while/body/eval_jaxpr/convert_element_type | solution.py:94
  379.0 8.1 %multiply_reduce_fusion.5 = (f32[3,512]{1,0:T(4,128)S(1)}, f32[3,512,2048]{2,1,0:T(8,128)}) fusion(f32[3,512,2048]{2,1,0:T(8,128)S(1)} %fusion.146, f32[3,512]{1,0:T(4,128)S(1)} %dynamic-slice_bitcast_fusion.2, pred[512,2048]{1,0:T(8,128)(4,1)S(1)} %broadcast_compare_fusion.5, bf16[1,2048,3,64]{1,3,2,0:T(8,128)(2,1)S(1)} %copy-done.5, ...), kind=kOutput, calls=%fused_computation.21.clone.1 | convolution fusion | flops 418380288 | bytes 27209732 | tf_op jit(solution)/shard_map/while/body/eval_jaxpr/bqhe,bkhe->bhqk/dot_general | solution.py:90
  387.1 10.3 %multiply_convert_fusion.3 = bf16[3,512,2048]{2,1,0:T(8,128)(2,1)} fusion(f32[3,512,2048]{2,1,0:T(8,128)} %get-tuple-element.374, f32[3,512,2048]{2,1,0:T(8,128)S(1)} %fusion.146, f32[3,512]{1,0:T(4,128)S(1)} %get-tuple-element.375, f32[3,512]{1,0:T(4,128)S(1)} %dynamic-slice_bitcast_fusion.2, pred[512,2048]{1,0:T(8,128)(4,1)S(1)} %broadcast_compare_fusion.5), kind=kLoop, calls=%fused_computation.20.clone.1 | loop fusion | flops 18874368 | bytes 32518144 | tf_op jit(solution)/shard_map/while/body/eval_jaxpr/convert_element_type | solution.py:94
  422.7 8.1 %multiply_reduce_fusion.5 = (f32[3,512]{1,0:T(4,128)S(1)}, f32[3,512,2048]{2,1,0:T(8,128)}) fusion(f32[3,512,2048]{2,1,0:T(8,128)S(1)} %fusion.146, f32[3,512]{1,0:T(4,128)S(1)} %dynamic-slice_bitcast_fusion.2, pred[512,2048]{1,0:T(8,128)(4,1)S(1)} %broadcast_compare_fusion.5, bf16[1,2048,3,64]{1,3,2,0:T(8,128)(2,1)S(1)} %copy-done.5, ...), kind=kOutput, calls=%fused_computation.21.clone.1 | convolution fusion | flops 418380288 | bytes 27209732 | tf_op jit(solution)/shard_map/while/body/eval_jaxpr/bqhe,bkhe->bhqk/dot_general | solution.py:90
  430.9 9.2 %multiply_convert_fusion.3 = bf16[3,512,2048]{2,1,0:T(8,128)(2,1)} fusion(f32[3,512,2048]{2,1,0:T(8,128)} %get-tuple-element.374, f32[3,512,2048]{2,1,0:T(8,128)S(1)} %fusion.146, f32[3,512]{1,0:T(4,128)S(1)} %get-tuple-element.375, f32[3,512]{1,0:T(4,128)S(1)} %dynamic-slice_bitcast_fusion.2, pred[512,2048]{1,0:T(8,128)(4,1)S(1)} %broadcast_compare_fusion.5), kind=kLoop, calls=%fused_computation.20.clone.1 | loop fusion | flops 18874368 | bytes 32518144 | tf_op jit(solution)/shard_map/while/body/eval_jaxpr/convert_element_type | solution.py:94
  465.7 8.1 %multiply_reduce_fusion.5 = (f32[3,512]{1,0:T(4,128)S(1)}, f32[3,512,2048]{2,1,0:T(8,128)}) fusion(f32[3,512,2048]{2,1,0:T(8,128)S(1)} %fusion.146, f32[3,512]{1,0:T(4,128)S(1)} %dynamic-slice_bitcast_fusion.2, pred[512,2048]{1,0:T(8,128)(4,1)S(1)} %broadcast_compare_fusion.5, bf16[1,2048,3,64]{1,3,2,0:T(8,128)(2,1)S(1)} %copy-done.5, ...), kind=kOutput, calls=%fused_computation.21.clone.1 | convolution fusion | flops 418380288 | bytes 27209732 | tf_op jit(solution)/shard_map/while/body/eval_jaxpr/bqhe,bkhe->bhqk/dot_general | solution.py:90
  473.8 9.8 %multiply_convert_fusion.3 = bf16[3,512,2048]{2,1,0:T(8,128)(2,1)} fusion(f32[3,512,2048]{2,1,0:T(8,128)} %get-tuple-element.374, f32[3,512,2048]{2,1,0:T(8,128)S(1)} %fusion.146, f32[3,512]{1,0:T(4,128)S(1)} %get-tuple-element.375, f32[3,512]{1,0:T(4,128)S(1)} %dynamic-slice_bitcast_fusion.2, pred[512,2048]{1,0:T(8,128)(4,1)S(1)} %broadcast_compare_fusion.5), kind=kLoop, calls=%fused_computation.20.clone.1 | loop fusion | flops 18874368 | bytes 32518144 | tf_op jit(solution)/shard_map/while/body/eval_jaxpr/convert_element_type | solution.py:94
  511.5 6.9 copy.105
  518.4 98.8 %all_to_all.69 = bf16[1,2048,1,3,192]{4,3,2,0,1:T(4,128)(2,1)} all-to-all(bf16[1,2048,1,3,192]{4,3,2,0,1:T(4,128)(2,1)} %copy.105), channel_id=1, replica_groups=mesh['dp'=8,'seq'=4] {'seq'}, dimensions={1} | all-to-all | bytes 4718592 | tf_op jit(solution)/shard_map/all_to_all | solution.py:193
  617.3 7.4 copy.109
  636.2 7.8 fusion.66
  655.6 42.9 %reduce-scatter.5.cloned.1.call-done = f32[96,2304]{1,0:T(8,128)} async-done(((f32[768,2304]{1,0:T(8,128)}), f32[96,2304]{1,0:T(8,128)}) %reduce-scatter.5.cloned.1.call-update) | async-done | bytes 884752 | tf_op jit(solution)/shard_map/reduce_scatter | solution.py:208
  710.2 26.3 %all-reduce.9 = (bf16[768]{0:T(1024)(128)(2,1)}, bf16[768]{0:T(1024)(128)(2,1)}, bf16[768]{0:T(1024)(128)(2,1)}, bf16[768]{0:T(1024)(128)(2,1)}, bf16[768]{0:T(1...) all-reduce(f32[768]{0:T(1024)} %get-tuple-element.160, ...), channel_id=2, replica_groups=mesh['dp'=8,'seq'=4] {'dp'}, use_global_device_ids=true, to_apply=%region_18.19.clone | all-reduce | flops 9216 | bytes 55296
  747.8 13.1 %all-reduce.10 = (bf16[96]{0:T(256)(128)(2,1)}, bf16[96]{0:T(256)(128)(2,1)}, bf16[96]{0:T(256)(128)(2,1)}, bf16[96]{0:T(256)(128)(2,1)}, bf16[96]{0:T(256)(128)...) all-reduce(bf16[96]{0:T(256)(128)(2,1)} %dynamic-slice.35, ...), channel_id=1, replica_groups=mesh['dp'=8,'seq'=4] {'seq'}, use_global_device_ids=true, to_apply=%region_19.20 | all-reduce | flops 1152 | bytes 4608 | tf_op jit(solution)/shard_map/psum | solution.py:221
  (293 shorter events, 309.3 us)
Async XLA Ops:
  7.2 8.6 %copy-start = (bf16[768,2304]{1,0:T(8,128)(2,1)S(1)}, bf16[768,2304]{1,0:T(8,128)(2,1)}, u32[]{:S(2)}) copy-start(bf16[768,2304]{1,0:T(8,128)(2,1)} %param.24) | copy-start | bytes 10616836
  8.7 11.8 %copy-start.19 = (f32[512]{0:T(512)}, f32[512]{0:T(512)S(1)}, u32[]{:S(2)}) copy-start(f32[512]{0:T(512)S(1)} %broadcast_multiply_fusion.1) | copy-start | bytes 6148
  10.8 9.7 %copy-start.22 = (f32[512]{0:T(512)}, f32[512]{0:T(512)S(1)}, u32[]{:S(2)}) copy-start(f32[512]{0:T(512)S(1)} %fusion.87) | copy-start | bytes 6148
  24.7 60.4 %all-to-all-start = ((bf16[1,512,4,3,192]{1,4,3,0,2:T(8,128)(2,1)}), bf16[1,512,4,3,192]{1,4,3,0,2:T(8,128)(2,1)}, u32[]{:S(2)}, u32[]{:S(2)}) async-start(bf16[1,512,4,3,192]{1,4,3,0,2:T(8,128)(2,1)} %bitcast.257), calls=%async_computation | async-start | bytes 4718592 | tf_op jit(solution)/shard_map/all_to_all | solution.py:158
  31.2 612.8 %reduce-scatter.7.cloned.1.call-start = ((), (), s32[]{:S(2)}) async-start(), calls=%async_computation.9 | async-start | bytes 2654208 | tf_op jit(solution)/shard_map/reduce_scatter | solution.py:211
  98.8 7.5 copy-start.16
  123.8 7.5 copy-start.16
  246.3 10.0 %copy-start.35 = (f32[768]{0:T(1024)S(1)}, f32[768]{0:T(1024)}, u32[]{:S(2)}) copy-start(f32[768]{0:T(1024)} %param.28) | copy-start | bytes 9220
  258.8 17.1 %copy-start.9 = (f32[512,768]{1,0:T(8,128)}, f32[512,768]{1,0:T(8,128)S(1)}, u32[]{:S(2)}) copy-start(f32[512,768]{1,0:T(8,128)S(1)} %get-tuple-element.243) | copy-start | bytes 4718596
  258.8 7.6 slice-start.2
  259.2 16.8 %copy-start.32 = (f32[512]{0:T(512)}, f32[512]{0:T(512)S(1)}, u32[]{:S(2)}) copy-start(f32[512]{0:T(512)S(1)} %fusion.88) | copy-start | bytes 6148
  259.2 13.2 %slice-start = ((s8[4718592]{0:T(1024)(128)(4,1)}), s8[4194304]{0:T(1024)(128)(4,1)S(1)}, s32[]{:S(2)}) async-start(s8[4718592]{0:T(1024)(128)(4,1)} %bitcast.273), calls=%async_computation.13 | async-start | bytes 8388608
  281.9 369.4 %reduce-scatter.9.cloned.1.call-start = ((), (), s32[]{:S(2)}) async-start(), calls=%async_computation.10 | async-start | bytes 10616832 | tf_op jit(solution)/shard_map/reduce_scatter | solution.py:215
  297.0 23.9 %all-to-all-start.2 = ((bf16[1,512,4,192]{1,3,0,2:T(8,128)(2,1)}), bf16[1,512,4,192]{1,3,0,2:T(8,128)(2,1)}, u32[]{:S(2)}, u32[]{:S(2)}) async-start(bf16[1,512,4,192]{1,3,0,2:T(8,128)(2,1)} %bitcast.261), calls=%async_computation.2 | async-start | bytes 1572864 | tf_op jit(solution)/shard_map/all_to_all | solution.py:188
  301.2 352.2 %reduce-scatter.11.cloned.1.call-start = ((), (), s32[]{:S(2)}) async-start(), calls=%async_computation.11 | async-start | bytes 10616832 | tf_op jit(solution)/shard_map/reduce_scatter | solution.py:217
  320.8 377.6 %reduce-scatter.5.cloned.1.call-start = ((), (), s32[]{:S(2)}) async-start(), calls=%async_computation.8 | async-start | bytes 7962624 | tf_op jit(solution)/shard_map/reduce_scatter | solution.py:208
  332.0 12.6 %copy-start.1 = (f32[3,512,2048]{2,1,0:T(8,128)}, f32[3,512,2048]{2,1,0:T(8,128)S(1)}, u32[]{:S(2)}) copy-start(f32[3,512,2048]{2,1,0:T(8,128)S(1)} %fusion.146) | copy-start | bytes 37748740 | tf_op jit(solution)/shard_map/while
  332.7 12.3 %copy-start.3 = (pred[512,2048]{1,0:T(8,128)(4,1)}, pred[512,2048]{1,0:T(8,128)(4,1)S(1)}, u32[]{:S(2)}) copy-start(pred[512,2048]{1,0:T(8,128)(4,1)S(1)} %broadcast_compare_fusion.5) | copy-start | bytes 3145732 | tf_op jit(solution)/shard_map/while
  354.8 12.1 %copy-start.2 = (f32[3,512,2048]{2,1,0:T(8,128)S(1)}, f32[3,512,2048]{2,1,0:T(8,128)}, u32[]{:S(2)}) copy-start(f32[3,512,2048]{2,1,0:T(8,128)} %copy-done.1) | copy-start | bytes 37748740 | tf_op jit(solution)/shard_map/while
  377.6 9.6 %copy-start.1 = (f32[3,512,2048]{2,1,0:T(8,128)}, f32[3,512,2048]{2,1,0:T(8,128)S(1)}, u32[]{:S(2)}) copy-start(f32[3,512,2048]{2,1,0:T(8,128)S(1)} %fusion.146) | copy-start | bytes 37748740 | tf_op jit(solution)/shard_map/while
  378.2 8.9 %copy-start.3 = (pred[512,2048]{1,0:T(8,128)(4,1)}, pred[512,2048]{1,0:T(8,128)(4,1)S(1)}, u32[]{:S(2)}) copy-start(pred[512,2048]{1,0:T(8,128)(4,1)S(1)} %broadcast_compare_fusion.5) | copy-start | bytes 3145732 | tf_op jit(solution)/shard_map/while
  397.4 12.4 %copy-start.2 = (f32[3,512,2048]{2,1,0:T(8,128)S(1)}, f32[3,512,2048]{2,1,0:T(8,128)}, u32[]{:S(2)}) copy-start(f32[3,512,2048]{2,1,0:T(8,128)} %copy-done.1) | copy-start | bytes 37748740 | tf_op jit(solution)/shard_map/while
  421.3 9.6 %copy-start.1 = (f32[3,512,2048]{2,1,0:T(8,128)}, f32[3,512,2048]{2,1,0:T(8,128)S(1)}, u32[]{:S(2)}) copy-start(f32[3,512,2048]{2,1,0:T(8,128)S(1)} %fusion.146) | copy-start | bytes 37748740 | tf_op jit(solution)/shard_map/while
  422.0 8.9 %copy-start.3 = (pred[512,2048]{1,0:T(8,128)(4,1)}, pred[512,2048]{1,0:T(8,128)(4,1)S(1)}, u32[]{:S(2)}) copy-start(pred[512,2048]{1,0:T(8,128)(4,1)S(1)} %broadcast_compare_fusion.5) | copy-start | bytes 3145732 | tf_op jit(solution)/shard_map/while
  440.1 12.8 %copy-start.2 = (f32[3,512,2048]{2,1,0:T(8,128)S(1)}, f32[3,512,2048]{2,1,0:T(8,128)}, u32[]{:S(2)}) copy-start(f32[3,512,2048]{2,1,0:T(8,128)} %copy-done.1) | copy-start | bytes 37748740 | tf_op jit(solution)/shard_map/while
  464.2 9.5 %copy-start.1 = (f32[3,512,2048]{2,1,0:T(8,128)}, f32[3,512,2048]{2,1,0:T(8,128)S(1)}, u32[]{:S(2)}) copy-start(f32[3,512,2048]{2,1,0:T(8,128)S(1)} %fusion.146) | copy-start | bytes 37748740 | tf_op jit(solution)/shard_map/while
  464.9 8.9 %copy-start.3 = (pred[512,2048]{1,0:T(8,128)(4,1)}, pred[512,2048]{1,0:T(8,128)(4,1)S(1)}, u32[]{:S(2)}) copy-start(pred[512,2048]{1,0:T(8,128)(4,1)S(1)} %broadcast_compare_fusion.5) | copy-start | bytes 3145732 | tf_op jit(solution)/shard_map/while
  483.6 12.2 %copy-start.2 = (f32[3,512,2048]{2,1,0:T(8,128)S(1)}, f32[3,512,2048]{2,1,0:T(8,128)}, u32[]{:S(2)}) copy-start(f32[3,512,2048]{2,1,0:T(8,128)} %copy-done.1) | copy-start | bytes 37748740 | tf_op jit(solution)/shard_map/while
  633.6 145.6 %all-reduce.14.cloned.1.call-start = ((), (), s32[]{:S(2)}) async-start(), calls=%async_computation.12 | async-start | bytes 3538944 | tf_op jit(solution)/shard_map/psum | solution.py:223
  653.4 50.5 %copy-start.21 = (f32[512]{0:T(512)S(1)}, f32[512]{0:T(512)}, u32[]{:S(2)}) copy-start(f32[512]{0:T(512)} %copy-done.19) | copy-start | bytes 6148
  653.4 50.5 %copy-start.30 = (f32[768]{0:T(1024)S(1)}, f32[768]{0:T(1024)}, u32[]{:S(2)}) copy-start(f32[768]{0:T(1024)} %param.22) | copy-start | bytes 9220
  708.7 63.3 %copy-start.28 = (f32[512]{0:T(512)S(1)}, f32[512]{0:T(512)}, u32[]{:S(2)}) copy-start(f32[512]{0:T(512)} %copy-done.27) | copy-start | bytes 6148
  (40 other events, 168.8 us)
Sparse Core Ops, SparseCore 0:
  282.0 41.5 reduce-scatter.6
  327.5 76.4 reduce-scatter.8
  408.0 76.4 reduce-scatter.10
  633.8 64.6 reduce-scatter.4
  702.1 77.1 all-reduce.13
where the time goes:
time: 799 us; the launch traced here: 792 us
  matrix products  246 us (31%)
  blocking collectives  162 us (20%)
  other arithmetic  132 us (17%)
  local copies, waits for them, and re-layouts  119 us (15%)
  waiting for transfers between devices  99.7 us (12%)
  between operations  15.8 us (2%)
  starting transfers between devices  11.4 us (1%)
    all_to_all x1, blocking collectives, local(): lax.all_to_all(d_projected[:, :, None], 'seq', split_axis=1, concat_axis=...  98.8 us
    all_to_all x1, waiting for transfers between devices, local(): lax.all_to_all(project_heads(), 'seq', split_axis=2, concat_axis=1, tiled...  53.4 us
    dot_general x8, matrix products, one_block(): jnp.einsum('bqhe,bkhe->bhqk', q_block, key_part, preferred_element_type=j...  46 us
    reduce_scatter x1, waiting for transfers between devices, local(): lax.psum_scatter(g_w_qkv, 'dp', scatter_dimension=0, tiled=True)  42.9 us
    convert_element_type x4, other arithmetic, one_block(): d_scores = (probs * (d_probs - inner)).astype(jnp.bfloat16)  39.1 us
    dot_general x4, matrix products, one_block(): jnp.einsum('bqhe,bkhe->bhqk', grad_block, value_part, preferred_element_t...  35 us
    dot_general x4, matrix products, one_block(): jnp.einsum('bhqk,bkhe->bqhe', weights, value_part, preferred_element_type...  29.5 us
    reduce_sum x4, other arithmetic, one_block(): totals = jnp.sum(raised, axis=-1, keepdims=True)  27.3 us
  transfers between devices with their start and end apart: 7, of which 3 were waited for; matrix products, arithmetic and copies ran while one was open for 38% of the time, Pallas kernels for 0%

commit v1 on v0

v1 whole, which is shorter than its diff:
```python
from functools import partial

import jax
import jax.numpy as jnp
from jax import lax
from jax.experimental import pallas as pl
from jax.experimental.pallas import tpu as pltpu
from jax.sharding import PartitionSpec as P

HEADS = 12
HEAD = 64
PAIRS = 6
EPS = 1e-05
ROOT_HALF = 0.7071067811865476
BIG = 1e30
MESH = pl.DeviceIdType.MESH
F32 = jnp.float32
BF = jnp.bfloat16
MIB = 1024 * 1024


def normalize(values, gain, shift):
    average = jnp.mean(values, axis=-1, keepdims=True)
    centred = values - average
    variance = jnp.mean(centred * centred, axis=-1, keepdims=True)
    return centred * lax.rsqrt(variance + EPS) * gain + shift


def gelu_exact(values):
    return 0.5 * values * (1.0 + jax.scipy.special.erf(values * ROOT_HALF))


def mm(a, b):
    return jnp.dot(a, b, preferred_element_type=F32)


def mm_nt(a, b):
    return lax.dot_general(a, b, (((1,), (1,)), ((), ())), preferred_element_type=F32)


def cell_bounds(lens_ref, index):
    start = jnp.zeros(index.shape, jnp.int32)
    end = jnp.zeros(index.shape, jnp.int32)
    at = jnp.int32(0)
    for c in range(lens_ref.shape[1]):
        after = at + lens_ref[0, c]
        start = jnp.where(index == c, at, start)
        end = jnp.where(index == c, after, end)
        at = after
    return start, end


def key_codes(lens_ref, block, rows):
    lane = lax.broadcasted_iota(jnp.int32, (1, 128), 1) % 64
    start, end = cell_bounds(lens_ref, lane)
    ones = ((lane >= 8) & (lane < 11)).astype(F32)
    slot = lax.broadcasted_iota(jnp.int32, (rows, 128), 0) + block * rows
    hot = jnp.where((slot >= start) & (slot < end), 1.0, 0.0)
    return (hot + ones).astype(BF)


def query_codes(lens_ref, block, rows):
    cell = lax.broadcasted_iota(jnp.int32, (64, 1), 0)
    start, end = cell_bounds(lens_ref, cell)
    slot = lax.broadcasted_iota(jnp.int32, (64, rows), 1) + block * rows
    inside = (slot >= start) & (slot < end)
    return jnp.where(inside | (cell >= 8), 0.0, -BIG)


def lane_halves():
    lane = lax.broadcasted_iota(jnp.int32, (1, 128), 1)
    low = jnp.where(lane < 64, 1.0, 0.0).astype(BF)
    high = jnp.where(lane < 64, 0.0, 1.0).astype(BF)
    return low, high


def sort_weights(w_ref, wp):
    depth = w_ref.shape[0]
    lane = lax.broadcasted_iota(jnp.int32, (depth, 128), 1)
    low = lane < 64
    for i in range(PAIRS):
        t0, t1, t2 = (w_ref[:, 384 * i + 128 * j : 384 * i + 128 * (j + 1)].astype(F32) for j in range(3))
        at = slice(128 * i, 128 * (i + 1))
        wp[0, :, at] = jnp.where(low, t0, t1).astype(BF)
        wp[1, :, at] = pltpu.roll(jnp.where(low, t2, t0), 64, 1).astype(BF)
        wp[2, :, at] = jnp.where(low, t1, t2).astype(BF)


def gather_kernel(
    tok, lens, gain, shift, w, bq, bv,
    kn_o, vn_o, kt_o, xt_o, qn_o, qt_o, wp_o, att_f, att_o, lse_o,
    xg, wp, kn, vn, kt, xt, qn, qt, qta, vta, acc, top, send, recv, out_sem,
):
    rows, width = tok.shape
    seq = lax.axis_size("seq")
    me = lax.axis_index("seq")
    has_left, has_right = me > 0, me < seq - 1

    barrier = pltpu.get_barrier_semaphore()

    @pl.when(has_left)
    def _():
        pl.semaphore_signal(barrier, inc=1, device_id={"seq": me - 1}, device_id_type=MESH)

    @pl.when(has_right)
    def _():
        pl.semaphore_signal(barrier, inc=1, device_id={"seq": me + 1}, device_id_type=MESH)

    xg[me] = normalize(tok[...].astype(F32), gain[...], shift[...]).astype(BF)

    @pl.when(has_left & has_right)
    def _():
        pl.semaphore_wait(barrier, 2)

    @pl.when(~(has_left & has_right))
    def _():
        pl.semaphore_wait(barrier, 1)

    def copy(way, hop, block):
        return pltpu.make_async_remote_copy(
            src_ref=xg.at[block],
            dst_ref=xg.at[block],
            send_sem=send.at[way, hop],
            recv_sem=recv.at[way, hop],
            device_id={"seq": me - 1 if way == 0 else me + 1},
            device_id_type=MESH,
        )

    def can_send(way):
        return has_left if way == 0 else has_right

    def holds(way, hop):
        return me + hop < seq if way == 0 else me - hop >= 0

    def block_of(way, hop):
        return me + hop if way == 0 else me - hop

    for way in range(2):
        @pl.when(can_send(way))
        def _():
            copy(way, 0, me).start()

    sort_weights(w, wp)
    keep_w = pltpu.make_async_copy(wp, wp_o, out_sem.at[0])
    keep_w.start()
    codes = query_codes(lens, me, rows).astype(BF)
    q = ((mm(xg[me], wp[0]) + bq[...]).astype(BF).astype(F32) * (HEAD**-0.5)).astype(BF)
    for i in range(PAIRS):
        pair = q[:, 128 * i : 128 * (i + 1)]
        qn[i] = pair
        turned = pair.T
        qt[i] = turned
        qta[2 * i, :64] = turned[:64]
        qta[2 * i, 64:] = codes
        qta[2 * i + 1, :64] = codes
        qta[2 * i + 1, 64:] = turned[64:]
    keep_q = pltpu.make_async_copy(qn, qn_o, out_sem.at[1])
    keep_q.start()
    keep_qt = pltpu.make_async_copy(qt, qt_o, out_sem.at[2])
    keep_qt.start()
    row16 = lax.broadcasted_iota(jnp.int32, (16, rows), 0)
    for h in range(HEADS):
        vta[h, 64:] = jnp.where(row16 == 0, 1.0, 0.0).astype(BF)
    acc[...] = jnp.zeros_like(acc)
    top[...] = jnp.full_like(top, -3e38)
    low, high = lane_halves()
    at_end = (me == 0) | (me == seq - 1)

    def keeps(block, step):
        return [
            pltpu.make_async_copy(kn.at[block], kn_o.at[block], out_sem.at[3 + 4 * step]),
            pltpu.make_async_copy(vn.at[block], vn_o.at[block], out_sem.at[4 + 4 * step]),
            pltpu.make_async_copy(kt.at[block], kt_o.at[block], out_sem.at[5 + 4 * step]),
            pltpu.make_async_copy(xt.at[block], xt_o.at[block], out_sem.at[6 + 4 * step]),
        ]

    def block_at(step):
        from_end = jnp.where(me == 0, step, seq - 1 - step)
        from_mid = jnp.where(step == 0, me, jnp.where(step == 1, me + 1, jnp.where(step == 2, me - 1, jnp.where(me == 1, seq - 1, 0))))
        return jnp.where(at_end, from_end, from_mid)

    def one_step(step, carry):
        for hop in range(1, 4):
            due = step == jnp.where(at_end, hop, 2 * hop - 1)
            for way in range(2):
                @pl.when(due & holds(way, hop))
                def _():
                    copy(way, hop - 1, block_of(way, hop)).wait_recv()

                    @pl.when(can_send(way))
                    def _():
                        copy(way, hop, block_of(way, hop)).start()

        block = block_at(step)
        x = xg[block]
        keys = mm(x, wp[1]).astype(BF)
        values = (mm(x, wp[2]) + bv[...]).astype(BF)
        hot = key_codes(lens, block, rows)
        hot_low, hot_high = hot * low, hot * high
        xt[block] = x.T
        for i in range(PAIRS):
            at = slice(128 * i, 128 * (i + 1))
            kn[block, i] = keys[:, at]
            kt[block, i] = keys[:, at].T
            vn[block, i] = values[:, at]
            turned = values[:, at].T
            vta[2 * i, :64] = turned[:64]
            vta[2 * i + 1, :64] = turned[64:]
        for c in keeps(block, step):
            c.start()

        def one_pair(i, carry):
            pair = kn[block, i]
            scores = [
                mm(pair * low + hot_high, qta[2 * i]),
                mm(pair * high + hot_low, qta[2 * i + 1]),
            ]
            for j in range(2):
                h = 2 * i + j
                before = top[h]
                now = jnp.maximum(before, jnp.max(scores[j], axis=0, keepdims=True))
                raised = jnp.exp(scores[j] - now).astype(BF)
                top[h] = now
                acc[h] = acc[h] * jnp.exp(before - now) + mm(vta[h], raised)
            return carry

        lax.fori_loop(0, PAIRS, one_pair, 0)
        return carry

    lax.fori_loop(0, seq, one_step, 0)

    lse_o[...] = jnp.zeros_like(lse_o)
    for h in range(HEADS):
        total = acc[h, 64:65]
        lse_o[h : h + 1] = top[h] + jnp.log(total)
        att_f[64 * h : 64 * (h + 1)] = acc[h, :64] / total
    att_o[...] = att_f[...].T.astype(BF)

    for way in range(2):
        for hop in range(3):
            @pl.when(can_send(way) & holds(way, hop))
            def _():
                copy(way, hop, block_of(way, hop)).wait_send()

    keep_w.wait()
    keep_q.wait()
    keep_qt.wait()
    for step in range(4):
        for c in keeps(block_at(step), step):
            c.wait()


def gather_attend(tokens, lens, gain, shift, w, bq, bv, seq):
    rows, width = tokens.shape
    any_spec = pl.BlockSpec(memory_space=pl.ANY)
    vmem = pl.BlockSpec(memory_space=pltpu.VMEM)
    sds = jax.ShapeDtypeStruct
    outs = [
        sds((seq, PAIRS, rows, 128), BF),
        sds((seq, PAIRS, rows, 128), BF),
        sds((seq, PAIRS, 128, rows), BF),
        sds((seq, width, rows), BF),
        sds((PAIRS, rows, 128), BF),
        sds((PAIRS, 128, rows), BF),
        sds((3, width, width), BF),
        sds((width, rows), F32),
        sds((rows, width), BF),
        sds((16, rows), F32),
    ]
    return pl.pallas_call(
        gather_kernel,
        out_shape=outs,
        in_specs=[vmem, pl.BlockSpec(memory_space=pltpu.SMEM)] + [vmem] * 5,
        out_specs=[any_spec] * 7 + [vmem] * 3,
        scratch_shapes=[
            pltpu.VMEM((seq, rows, width), BF),
            pltpu.VMEM((3, width, width), BF),
            pltpu.VMEM((seq, PAIRS, rows, 128), BF),
            pltpu.VMEM((seq, PAIRS, rows, 128), BF),
            pltpu.VMEM((seq, PAIRS, 128, rows), BF),
            pltpu.VMEM((seq, width, rows), BF),
            pltpu.VMEM((PAIRS, rows, 128), BF),
            pltpu.VMEM((PAIRS, 128, rows), BF),
            pltpu.VMEM((HEADS, 128, rows), BF),
            pltpu.VMEM((HEADS, 80, rows), BF),
            pltpu.VMEM((HEADS, 80, rows), F32),
            pltpu.VMEM((HEADS, 1, rows), F32),
            pltpu.SemaphoreType.DMA((2, 4)),
            pltpu.SemaphoreType.DMA((2, 4)),
            pltpu.SemaphoreType.DMA((20,)),
        ],
        compiler_params=pltpu.CompilerParams(
            collective_id=0, has_side_effects=True, vmem_limit_bytes=56 * MIB
        ),
        name="gather_attend",
    )(tokens, lens, gain, shift, w, bq, bv)


def three_parts(values):
    high = values.astype(BF).astype(F32)
    middle = (values - high).astype(BF).astype(F32)
    return high, middle, values - high - middle


def attend_back_kernel(
    kn_h, vn_h, kt_h, xt_h, qn, qt, d_att, d_att_t, delta, lse, wp, lens,
    dx_o, gw_o, gbias_o,
    kn, vn, kt, xt, qta, dta, qh, dh, dqt, gk, gv, dk, dv, in_sem,
):
    rows, width = d_att.shape
    seq = lax.axis_size("seq")
    me = lax.axis_index("seq")

    def block_at(step):
        b0 = jnp.where(me < 2, seq - 1, 0)
        b1 = jnp.where(me < 2, seq - 2, 1)
        b2 = jnp.where(me == 0, 1, jnp.where(me == 1, 0, jnp.where(me == 2, 3, 2)))
        return jnp.where(step == 0, b0, jnp.where(step == 1, b1, jnp.where(step == 2, b2, me)))

    def loads(step):
        block = block_at(step)
        return [
            pltpu.make_async_copy(kn_h.at[block], kn.at[step], in_sem.at[step, 0]),
            pltpu.make_async_copy(vn_h.at[block], vn.at[step], in_sem.at[step, 1]),
            pltpu.make_async_copy(kt_h.at[block], kt.at[step], in_sem.at[step, 2]),
            pltpu.make_async_copy(xt_h.at[block], xt.at[step], in_sem.at[step, 3]),
        ]

    for step in range(4):
        for c in loads(step):
            c.start()

    low, high = lane_halves()
    codes = query_codes(lens, me, rows)
    row64 = lax.broadcasted_iota(jnp.int32, (64, rows), 0)
    for h in range(HEADS):
        i, j = h // 2, h % 2
        own, other = (slice(0, 64), slice(64, 128)) if j == 0 else (slice(64, 128), slice(0, 64))
        extra = codes
        for r, part in enumerate(three_parts(-lse[h : h + 1])):
            extra = jnp.where(row64 == 8 + r, part, extra)
        qta[h, own] = qt[i, own]
        qta[h, other] = extra.astype(BF)
        extra = jnp.zeros((64, rows), F32)
        for r, part in enumerate(three_parts(-delta[h : h + 1])):
            extra = jnp.where(row64 == r, part, extra)
        dta[h, own] = d_att_t[64 * h : 64 * (h + 1)]
        dta[h, other] = extra.astype(BF)
        half = low if j == 0 else high
        qh[h] = qn[i] * half
        dh[h] = d_att[:, 128 * i : 128 * (i + 1)] * half
    dqt[...] = jnp.zeros_like(dqt)
    gk[...] = jnp.zeros_like(gk)
    gv[...] = jnp.zeros_like(gv)
    gbias_o[...] = jnp.zeros_like(gbias_o)
    lane = lax.broadcasted_iota(jnp.int32, (1, 128), 1)
    v_low = jnp.where(lane < 3, 1.0, 0.0).astype(BF)
    v_high = jnp.where((lane >= 64) & (lane < 67), 1.0, 0.0).astype(BF)

    def one_step(step, carry):
        for c in loads(step):
            c.wait()
        block = block_at(step)
        hot = key_codes(lens, block, rows)
        hot_low, hot_high = hot * low, hot * high

        def one_pair(i, carry):
            keys, values = kn[step, i], vn[step, i]
            scores = [
                mm(keys * low + hot_high, qta[2 * i]),
                mm(keys * high + hot_low, qta[2 * i + 1]),
            ]
            slopes = [
                mm(values * low + v_high, dta[2 * i]),
                mm(values * high + v_low, dta[2 * i + 1]),
            ]
            d_keys = jnp.zeros((rows, 128), F32)
            d_values = jnp.zeros((rows, 128), F32)
            for j in range(2):
                h = 2 * i + j
                probs = jnp.exp(scores[j])
                d_scores = (probs * slopes[j]).astype(BF)
                d_values = d_values + mm(probs.astype(BF), dh[h])
                d_keys = d_keys + mm(d_scores, qh[h])
                dqt[h] += mm(kt[step, i, 64 * j : 64 * (j + 1)], d_scores)
            at = pl.ds(pl.multiple_of(i * 128, 128), 128)
            dk[:, at] = d_keys.astype(BF)
            dv[:, at] = d_values.astype(BF)
            return carry

        lax.fori_loop(0, PAIRS, one_pair, 0)
        dx = mm_nt(dk[...], wp[1]) + mm_nt(dv[...], wp[2])
        gk[...] += mm(xt[step], dk[...])
        gv[...] += mm(xt[step], dv[...])
        gbias_o[1:2] += jnp.sum(dv[...].astype(F32), axis=0, keepdims=True)

        @pl.when(step < seq - 1)
        def _():
            dx_o[block] = dx.astype(BF)

        @pl.when(step == seq - 1)
        def _():
            turned = (dqt[...] * (HEAD**-0.5)).reshape(width, rows).T
            dq = turned.astype(BF)
            dx_o[block] = (dx + mm_nt(dq, wp[0])).astype(BF)
            gbias_o[0:1] = jnp.sum(dq.astype(F32), axis=0, keepdims=True)
            gq = mm(xt[step], dq)
            lane_w = lax.broadcasted_iota(jnp.int32, (width, 128), 1)
            lo = lane_w < 64
            for i in range(PAIRS):
                at = slice(128 * i, 128 * (i + 1))
                k_turned = pltpu.roll(gk[:, at], 64, 1)
                t0 = jnp.where(lo, gq[:, at], k_turned)
                t1 = jnp.where(lo, gv[:, at], gq[:, at])
                t2 = jnp.where(lo, k_turned, gv[:, at])
                for j, t in enumerate((t0, t1, t2)):
                    gw_o[:, 384 * i + 128 * j : 384 * i + 128 * (j + 1)] = t.astype(BF)

        return carry

    lax.fori_loop(0, seq, one_step, 0)


def attend_back(kn, vn, kt, xt, qn, qt, d_att, d_att_t, delta, lse, wp, lens):
    seq, _, rows, _ = kn.shape
    width = wp.shape[1]
    any_spec = pl.BlockSpec(memory_space=pl.ANY)
    vmem = pl.BlockSpec(memory_space=pltpu.VMEM)
    sds = jax.ShapeDtypeStruct
    return pl.pallas_call(
        attend_back_kernel,
        out_shape=[
            sds((seq, rows, width), BF),
            sds((width, 3 * width), BF),
            sds((8, width), F32),
        ],
        in_specs=[any_spec] * 4 + [vmem] * 7 + [pl.BlockSpec(memory_space=pltpu.SMEM)],
        out_specs=[vmem] * 3,
        scratch_shapes=[
            pltpu.VMEM((seq, PAIRS, rows, 128), BF),
            pltpu.VMEM((seq, PAIRS, rows, 128), BF),
            pltpu.VMEM((seq, PAIRS, 128, rows), BF),
            pltpu.VMEM((seq, width, rows), BF),
            pltpu.VMEM((HEADS, 128, rows), BF),
            pltpu.VMEM((HEADS, 128, rows), BF),
            pltpu.VMEM((HEADS, rows, 128), BF),
            pltpu.VMEM((HEADS, rows, 128), BF),
            pltpu.VMEM((HEADS, HEAD, rows), F32),
            pltpu.VMEM((width, width), F32),
            pltpu.VMEM((width, width), F32),
            pltpu.VMEM((rows, width), BF),
            pltpu.VMEM((rows, width), BF),
            pltpu.SemaphoreType.DMA((4, 4)),
        ],
        compiler_params=pltpu.CompilerParams(vmem_limit_bytes=58 * MIB),
        name="attend_back",
    )(kn, vn, kt, xt, qn, qt, d_att, d_att_t, delta, lse, wp, lens)


def local(
    tokens, cell_lengths, ln1_gain, ln1_shift, w_qkv, b_query, b_value, w_out, b_out,
    ln2_gain, ln2_shift, w_up, b_up, w_down, b_down, cotangent,
):
    bucket_count, local_slots, width = tokens.shape
    seq_count = lax.axis_size("seq")
    dp_count = lax.axis_size("dp")
    rows = bucket_count * local_slots
    flat = tokens.reshape(rows, width)
    flat_tokens = flat.astype(F32)

    def row(v):
        return v.reshape(1, -1)

    kn, vn, kt, xt, qn, qt, wp, att_t, attended, lse = gather_attend(
        flat, cell_lengths, row(ln1_gain), row(ln1_shift), w_qkv, row(b_query), row(b_value), seq_count
    )
    middle = flat_tokens + mm(attended, w_out) + b_out
    normed_two = normalize(middle, ln2_gain, ln2_shift).astype(BF)
    upper = mm(normed_two, w_up) + b_up
    hidden = gelu_exact(upper).astype(BF)
    layer_out = middle + mm(hidden, w_down) + b_down
    layer_out = layer_out.astype(BF).reshape(tokens.shape)
    d_output = cotangent.reshape(rows, width)
    g_w_down = mm(hidden.T, d_output).astype(BF)
    g_b_down = jnp.sum(d_output, axis=0, dtype=F32)
    d_hidden = mm(d_output, w_down.T)
    gelu_pull = jax.vjp(gelu_exact, upper)[1]
    d_upper = gelu_pull(d_hidden)[0].astype(BF)
    g_w_up = mm(normed_two.T, d_upper).astype(BF)
    g_b_up = jnp.sum(d_upper, axis=0, dtype=F32)
    d_normed_two = mm(d_upper, w_up.T)
    second_pull = jax.vjp(normalize, middle, ln2_gain, ln2_shift)[1]
    d_middle, g_ln2_gain, g_ln2_shift = second_pull(d_normed_two)
    d_middle = d_middle + d_output.astype(F32)
    d_branch = d_middle.astype(BF)
    g_w_out = mm(attended.T, d_branch).astype(BF)
    g_b_out = jnp.sum(d_branch, axis=0, dtype=F32)
    d_att = mm(d_branch, w_out.T).astype(BF)
    d_att_t = d_att.T
    delta = jnp.sum((d_att_t.astype(F32) * att_t).reshape(HEADS, HEAD, rows), axis=1)
    delta = jnp.pad(delta, ((0, 4), (0, 0)))
    dx, g_w_qkv, g_bias = attend_back(kn, vn, kt, xt, qn, qt, d_att, d_att_t, delta, lse, wp, cell_lengths)
    d_normed_one = lax.psum_scatter(dx, "seq", scatter_dimension=0, tiled=True).reshape(rows, width).astype(F32)
    first_pull = jax.vjp(normalize, flat_tokens, ln1_gain, ln1_shift)[1]
    d_tokens, g_ln1_gain, g_ln1_shift = first_pull(d_normed_one)
    tokens_grad = (d_tokens + d_middle).astype(BF).reshape(tokens.shape)

    def summed(g):
        share = lax.psum_scatter(g, "dp", scatter_dimension=0, tiled=True)
        return lax.psum(share, "seq").astype(F32)

    g_w_down, g_w_up, g_w_out, g_w_qkv = summed(g_w_down), summed(g_w_up), summed(g_w_out), summed(g_w_qkv)
    vectors = (g_ln1_gain, g_ln1_shift, g_bias[0], g_bias[1], g_b_out, g_ln2_gain, g_ln2_shift, g_b_up, g_b_down)
    packed = jnp.concatenate([v.reshape(dp_count, -1) for v in vectors], axis=1)
    packed = lax.psum(packed, ("dp", "seq"))
    mine = lax.dynamic_index_in_dim(packed, lax.axis_index("dp"), 0, keepdims=False)
    parts, at = [], 0
    for v in vectors:
        size = v.shape[0] // dp_count
        parts.append(mine[at : at + size])
        at += size
    return (
        layer_out, tokens_grad, parts[0], parts[1], g_w_qkv, parts[2], parts[3], g_w_out, parts[4],
        parts[5], parts[6], g_w_up, parts[7], g_w_down, parts[8],
    )


def solution(mesh):
    token_spec = P("dp", "seq", None)
    vector, matrix = P("dp"), P("dp", None)
    placed = (token_spec, P("dp", None)) + (P(),) * 13 + (token_spec,)
    return jax.shard_map(
        local,
        mesh=mesh,
        in_specs=placed,
        out_specs=(
            token_spec, token_spec, vector, vector, matrix, vector, vector, matrix, vector,
            vector, vector, matrix, vector, matrix, vector,
        ),
        check_vma=False,
    )
```

time: 799 us -> 484 us (0.61)
  matrix products: 246 us -> 44.4 us
  waiting for transfers between devices: 99.7 us -> 227 us
  Pallas kernels: 0 us -> 124 us
  blocking collectives: 162 us -> 44 us
  other arithmetic: 132 us -> 16 us
  local copies, waits for them, and re-layouts: 119 us -> 12.8 us
  starting transfers between devices: 11.4 us -> 0.65 us
    dot_general x40 -> x9, matrix products: 246 us -> 44.4 us  [mm(): return jnp.dot(a, b, preferred_element_type=F32)]
    reduce_scatter x4 -> x5, waiting for transfers between devices: 42.9 us -> 199 us  [the longest x4 136 us: summed(): share = lax.psum_scatter(g, 'dp', scatter_dimension=0, tiled=True)]
    pallas_call x0 -> x2, Pallas kernels: none -> 124 us  [the longest x1 69.2 us: gather_attend(): pl.pallas_call(gather_kernel, out_shape=outs, in_specs=[vmem, pl.BlockSpe...]
    all_to_all x2 -> x0, blocking collectives: 123 us -> none  [the longest x1 98.8 us: local(): lax.all_to_all(d_projected[:, :, None], 'seq', split_axis=1, concat_axis=...]
    convert_element_type x21 -> x4, other arithmetic: 63.6 us -> 5.95 us  [summed(): return lax.psum(share, 'seq').astype(F32)]
    all_to_all x2 -> x0, waiting for transfers between devices: 53.4 us -> none  [the longest x1 53.4 us: local(): lax.all_to_all(project_heads(), 'seq', split_axis=2, concat_axis=1, tiled...]
    psum x1, blocking collectives: 13.1 us -> 44 us  [local(): packed = lax.psum(packed, ('dp', 'seq'))]
    reduce_sum x7 -> x2, other arithmetic: 32.1 us -> 2.08 us  [the longest x1 1.7 us: local(): jnp.sum((d_att_t.astype(F32) * att_t).reshape(HEADS, HEAD, rows), axis=1)]
  transfers between devices with their start and end apart: 7 -> 6, of which waited for: 3 -> 5; matrix products, arithmetic and copies ran while one was open for 38% -> 8% of each run, Pallas kernels for 0% -> 11%
where the time goes in v1:
time: 484 us
  waiting for transfers between devices  227 us (47%)
  Pallas kernels  124 us (26%)
  matrix products  44.4 us (9%)
  blocking collectives  44 us (9%)
  other arithmetic  16 us (3%)
  between operations  14.4 us (3%)
  local copies, waits for them, and re-layouts  12.8 us (3%)
    reduce_scatter x4, waiting for transfers between devices, summed(): share = lax.psum_scatter(g, 'dp', scatter_dimension=0, tiled=True)  136 us
    pallas_call x1, Pallas kernels, gather_attend(): pl.pallas_call(gather_kernel, out_shape=outs, in_specs=[vmem, pl.BlockSpe...  69.2 us
    reduce_scatter x1, waiting for transfers between devices, local(): lax.psum_scatter(dx, 'seq', scatter_dimension=0, tiled=True)  62.5 us
    pallas_call x1, Pallas kernels, attend_back(): pl.pallas_call(attend_back_kernel, out_shape=[sds((seq, rows, width), BF)...  54.8 us
    dot_general x9, matrix products, mm(): return jnp.dot(a, b, preferred_element_type=F32)  44.4 us
    psum x1, blocking collectives, local(): packed = lax.psum(packed, ('dp', 'seq'))  44 us
    psum x1, waiting for transfers between devices, summed(): return lax.psum(share, 'seq').astype(F32)  28.1 us
  transfers between devices with their start and end apart: 6, of which 5 were waited for; matrix products, arithmetic and copies ran while one was open for 8% of the time, Pallas kernels for 11%

profile of v1, /device:TPU:0, one launch (start us, length us, event | category | flops | bytes accessed | tf_op | source)
XLA Modules:
  0.0 483.6 jit_solution(234229082837813361)
XLA Ops:
  7.2 1.4 reshape.161.shift
  8.6 1.3 reshape.162.bq
  9.9 1.3 reshape.163.bv
  11.1 1.3 reshape.160.gain
  12.4 69.2 %gather_attend.1 = (bf16[4,6,512,128]{3,2,1,0:T(8,128)(2,1)}, bf16[4,6,512,128]{3,2,1,0:T(8,128)(2,1)}, bf16[4,6,128,512]{3,2,1,0:T(8,128)(2,1)}, bf16[4,768,512...) custom-call(bf16[512,768]{1,0:T(8,128)(2,1)} %bitcast.82, ...), custom_call_target="tpu_custom_call" | custom-call | tf_op jit(solution)/shard_map/gather_attend/pallas_call | solution.py:270
  81.6 2.2 fusion.25
  84.7 4.9 %multiply_convert_fusion = (bf16[512,3072]{1,0:T(8,128)(2,1)}, f32[512,3072]{1,0:T(8,128)S(1)}) fusion(f32[3072]{0:T(1024)S(1)} %copy-done.21, bf16[768,3072]{1,0:T(8,128)(2,1)S(1)} %copy-done.19, f32[512,768]{1,0:T(8,128)S(1)} %get-tuple-element.70, f32[768]{0:T(1024)S(1)} %copy-done.23, f32[768]{0:T(1024)S(1)} %copy-done.17, f32[512]{0:T(512)S(1)} %fusion.20, ...), kind=kOutput, calls=%fused_computation.2 | convolution fusion | flops 2427322368 | bytes 15751168 | tf_op jit(solution)/shard_map/dot_general | solution.py:34
  89.6 6.0 %convert_reduce_fusion = (f32[3072]{0:T(1024)}, bf16[512,3072]{1,0:T(8,128)(2,1)S(1)}) fusion(bf16[3072,768]{1,0:T(8,128)(2,1)S(1)} %bitcast.86, bf16[1,512,768]{2,1,0:T(8,128)(2,1)S(1)} %copy-done.6, f32[512,3072]{1,0:T(8,128)S(1)} %get-tuple-element.72, f32[3072]{0:T(1024)S(1)} %copy-done.21), kind=kOutput, calls=%fused_computation | convolution fusion | flops 2441081856 | bytes 14966784 | tf_op jit(solution)/shard_map/dot_general | solution.py:34
  95.6 3.5 multiply_reduce_fusion
  101.0 1.8 convolution_convert_fusion.2
  103.1 3.9 convert_multiply_fusion
  107.0 1.7 reduce_sum.147
  109.3 1.2 copy.32.d_att
  110.5 54.8 %attend_back.1 = (bf16[4,512,768]{2,1,0:T(8,128)(2,1)}, bf16[768,2304]{1,0:T(8,128)(2,1)}, f32[8,768]{1,0:T(8,128)}) custom-call(bf16[4,6,512,128]{3,2,1,0:T(8,128)(2,1)} %get-tuple-element.29.kn_h, bf16[4,6,512,128]{3,2,1,0:T(8,128)(2,1)} %get-tuple-element.30.vn_h, bf16[4,6,128,512]{3,2,1,0:T(8,128)(2,1)} %get-tuple-element.31.kt_h, ...), custom_call_target="tpu_custom_call" | custom-call | tf_op jit(solution)/shard_map/attend_back/pallas_call | solution.py:430
  165.4 1.0 copy-done.7
  166.5 6.6 %convolution_convert_fusion = bf16[3072,768]{1,0:T(8,128)(2,1)} fusion(bf16[512,3072]{1,0:T(8,128)(2,1)} %get-tuple-element.71, bf16[1,512,768]{2,1,0:T(8,128)(2,1)S(1)} %copy-done.7), kind=kOutput, calls=%fused_computation.4 | convolution fusion | flops 2418278400 | bytes 8650752 | tf_op jit(solution)/shard_map/dot_general | solution.py:34
  173.8 7.7 %convolution_convert_fusion.1 = bf16[768,3072]{1,0:T(8,128)(2,1)} fusion(bf16[512,3072]{1,0:T(8,128)(2,1)} %copy-done.26, f32[512,768]{1,0:T(8,128)} %copy-done.5, f32[768]{0:T(1024)S(1)} %copy-done.24, f32[768]{0:T(1024)S(1)} %copy-done.18, f32[512]{0:T(512)S(1)} %copy-done.14, f32[512]{0:T(512)S(1)} %broadcast_multiply_fusion.1), kind=kOutput, calls=%fused_computation.5 | convolution fusion | flops 2420244480 | bytes 9447424 | tf_op jit(solution)/shard_map/dot_general | solution.py:34
  183.8 7.8 %fusion.11 = bf16[1,512,768]{2,1,0:T(8,128)(2,1)} fusion(f32[512,768]{1,0:T(8,128)} %copy-done.5, bf16[512,3072]{1,0:T(8,128)(2,1)} %get-tuple-element.71, bf16[3072,768]{1,0:T(8,128)(2,1)} %param.29, f32[768]{0:T(1024)S(1)} %copy-done.25), kind=kOutput, calls=%fused_computation.36 | convolution fusion | flops 2417098752 | bytes 10226688 | tf_op jit(solution)/shard_map/dot_general | solution.py:34
  191.7 21.1 %reduce-scatter.8.cloned.1.call-done = bf16[96,2304]{1,0:T(8,128)(2,1)} async-done(((bf16[768,2304]{1,0:T(8,128)(2,1)}), bf16[96,2304]{1,0:T(8,128)(2,1)}) %reduce-scatter.8.cloned.1.call-update) | async-done | bytes 442384 | tf_op jit(solution)/shard_map/reduce_scatter | solution.py:509
  212.8 57.8 %reduce-scatter.14.cloned.1.call-done = bf16[384,768]{1,0:T(8,128)(2,1)} async-done(((bf16[3072,768]{1,0:T(8,128)(2,1)}), bf16[384,768]{1,0:T(8,128)(2,1)}) %reduce-scatter.14.cloned.1.call-update) | async-done | bytes 589840 | tf_op jit(solution)/shard_map/reduce_scatter | solution.py:509
  270.6 57.2 %reduce-scatter.12.cloned.1.call-done = bf16[96,3072]{1,0:T(8,128)(2,1)} async-done(((bf16[768,3072]{1,0:T(8,128)(2,1)}), bf16[96,3072]{1,0:T(8,128)(2,1)}) %reduce-scatter.12.cloned.1.call-update) | async-done | bytes 589840 | tf_op jit(solution)/shard_map/reduce_scatter | solution.py:509
  327.8 62.5 %reduce-scatter.6.cloned.1.call-done = bf16[1,512,768]{2,1,0:T(8,128)(2,1)} async-done(((bf16[4,512,768]{2,1,0:T(8,128)(2,1)}), bf16[1,512,768]{2,1,0:T(8,128)(2,1)}) %reduce-scatter.6.cloned.1.call-update) | async-done | bytes 786448 | tf_op jit(solution)/shard_map/reduce_scatter | solution.py:503
  390.3 1.4 convert_reduce_fusion.2
  391.7 1.8 fusion.8
  393.5 0.9 fusion.7
  394.6 44.0 %psum.35 = f32[8,1152]{1,0:T(8,128)S(1)} all-reduce(f32[8,1152]{1,0:T(8,128)S(1)} %concatenate.3), channel_id=1, replica_groups=mesh['dp'=8,'seq'=4] {'dp','seq'}, use_global_device_ids=true, to_apply=%region_17.18 | all-reduce | flops 9216 | bytes 73728 | tf_op jit(solution)/shard_map/psum | solution.py:515
  439.9 2.8 fusion.19
  442.7 28.1 %all-reduce.4.cloned.1.call-done = (bf16[96,2304]{1,0:T(8,128)(2,1)}, bf16[96,768]{1,0:T(8,128)(2,1)}, bf16[96,3072]{1,0:T(8,128)(2,1)}, bf16[384,768]{1,0:T(8,128)(2,1)}) async-done(((bf16[96,2304]{1,0:T(8,128)(2,1)}, bf16[96,768]{1,0:T(8,128)(2,1)}, bf16[96,3072]{1,0:T(8,128)(2,1)}, bf16[384,768]{1,0:T(8,128)(2,1)}), (bf16[96,2304]{1,0:T(8,128)(2,1)}, bf16[96,768]{1,0:T(8,128)(2,1)}, ...) | async-done | bytes 1769488 | tf_op jit(solution)/shard_map/psum | solution.py:510
  470.7 1.7 convert_element_type.85
  472.5 2.0 convert_element_type.83
  474.5 1.1 convert_element_type.87
  475.6 1.1 convert_element_type.89
  (96 shorter events, 8.3 us)
Async XLA Ops:
  7.2 74.4 %copy-start = (bf16[768,768]{1,0:T(8,128)(2,1)S(1)}, bf16[768,768]{1,0:T(8,128)(2,1)}, u32[]{:S(2)}) copy-start(bf16[768,768]{1,0:T(8,128)(2,1)} %param.23) | copy-start | bytes 3538948
  7.2 184.5 %reduce-scatter.10.cloned.1.call-start = ((), (), s32[]{:S(2)}) async-start(), calls=%async_computation.7 | async-start | bytes 1327104 | tf_op jit(solution)/shard_map/reduce_scatter | solution.py:509
  12.4 69.2 %copy-start.2 = (bf16[1,512,768]{2,1,0:T(8,128)(2,1)S(1)}, bf16[1,512,768]{2,1,0:T(8,128)(2,1)}, u32[]{:S(2)}) copy-start(bf16[1,512,768]{2,1,0:T(8,128)(2,1)} %param.16) | copy-start | bytes 2359300
  12.4 69.2 %copy-start.22 = (f32[768]{0:T(1024)S(1)}, f32[768]{0:T(1024)}, u32[]{:S(2)}) copy-start(f32[768]{0:T(1024)} %param.24) | copy-start | bytes 9220
  81.6 2.6 copy-start.19
  83.8 15.3 %copy-start.5 = (f32[512,768]{1,0:T(8,128)}, f32[512,768]{1,0:T(8,128)S(1)}, u32[]{:S(2)}) copy-start(f32[512,768]{1,0:T(8,128)S(1)} %get-tuple-element.70) | copy-start | bytes 4718596
  83.8 0.8 copy-start.17
  83.8 0.9 copy-start.21
  83.8 0.9 copy-start.23
  83.8 5.8 %slice-start = ((s8[4718592]{0:T(1024)(128)(4,1)}), s8[4194304]{0:T(1024)(128)(4,1)S(1)}, s32[]{:S(2)}) async-start(s8[4718592]{0:T(1024)(128)(4,1)} %bitcast.85), calls=%async_computation.11 | async-start | bytes 8388608
  84.7 14.4 %copy-start.13 = (f32[512]{0:T(512)}, f32[512]{0:T(512)S(1)}, u32[]{:S(2)}) copy-start(f32[512]{0:T(512)S(1)} %fusion.20) | copy-start | bytes 6148
  84.7 4.9 %copy-start.6 = (bf16[1,512,768]{2,1,0:T(8,128)(2,1)S(1)}, bf16[1,512,768]{2,1,0:T(8,128)(2,1)}, u32[]{:S(2)}) copy-start(bf16[1,512,768]{2,1,0:T(8,128)(2,1)} %param.31) | copy-start | bytes 2359300
  84.7 4.9 %slice-start.1 = ((s8[4718592]{0:T(1024)(128)(4,1)}), s8[524288]{0:T(1024)(128)(4,1)S(1)}, s32[]{:S(2)}) async-start(s8[4718592]{0:T(1024)(128)(4,1)} %bitcast.85), calls=%async_computation.12 | async-start | bytes 1048576
  95.6 3.5 copy-start.26
  99.8 1.3 copy-start.20
  100.2 0.9 copy-start.8
  102.9 109.9 %reduce-scatter.8.cloned.1.call-start = ((), (), s32[]{:S(2)}) async-start(), calls=%async_computation.6 | async-start | bytes 3981312 | tf_op jit(solution)/shard_map/reduce_scatter | solution.py:509
  107.0 2.3 copy-start.4
  165.3 1.1 copy-start.7
  165.4 105.2 %reduce-scatter.14.cloned.1.call-start = ((), (), s32[]{:S(2)}) async-start(), calls=%async_computation.9 | async-start | bytes 5308416 | tf_op jit(solution)/shard_map/reduce_scatter | solution.py:509
  173.1 0.7 copy-start.18
  173.1 0.7 copy-start.24
  173.1 154.6 %reduce-scatter.12.cloned.1.call-start = ((), (), s32[]{:S(2)}) async-start(), calls=%async_computation.8 | async-start | bytes 5308416 | tf_op jit(solution)/shard_map/reduce_scatter | solution.py:509
  181.6 208.7 %reduce-scatter.6.cloned.1.call-start = ((), (), s32[]{:S(2)}) async-start(), calls=%async_computation.5 | async-start | bytes 3932160 | tf_op jit(solution)/shard_map/reduce_scatter | solution.py:503
  181.7 0.8 copy-start.15
  181.7 2.1 copy-start.25
  182.2 288.5 %all-reduce.4.cloned.1.call-start = ((), (), s32[]{:S(2)}) async-start(), calls=%async_computation.10 | async-start | bytes 3538944 | tf_op jit(solution)/shard_map/psum | solution.py:510
  191.7 200.1 %copy-start.11 = (f32[768]{0:T(1024)S(1)}, f32[768]{0:T(1024)}, u32[]{:S(2)}) copy-start(f32[768]{0:T(1024)} %param.18) | copy-start | bytes 9220
  390.3 3.2 copy-start.3
  470.7 3.8 copy-start.10
  472.5 3.2 copy-start.9
  474.5 2.2 copy-start.1
  (3 other events, 2.1 us)
Sparse Core Ops, SparseCore 0:
  103.0 35.8 reduce-scatter.9
  165.5 47.2 reduce-scatter.7
  216.6 53.8 reduce-scatter.13
  273.9 53.8 reduce-scatter.11
  330.0 60.2 reduce-scatter.5
  393.0 77.7 all-reduce.3

commit v2 on v1

--- a/solution.py
+++ b/solution.py
@@ -106,7 +106,7 @@
     def _():
         pl.semaphore_signal(barrier, inc=1, device_id={"seq": me + 1}, device_id_type=MESH)
 
-    xg[me] = normalize(tok[...].astype(F32), gain[...], shift[...]).astype(BF)
+    xg[me] = normalize(tok[...].astype(F32), gain[...].reshape(1, -1), shift[...].reshape(1, -1)).astype(BF)
 
     @pl.when(has_left & has_right)
     def _():
@@ -144,7 +144,7 @@
     keep_w = pltpu.make_async_copy(wp, wp_o, out_sem.at[0])
     keep_w.start()
     codes = query_codes(lens, me, rows).astype(BF)
-    q = ((mm(xg[me], wp[0]) + bq[...]).astype(BF).astype(F32) * (HEAD**-0.5)).astype(BF)
+    q = ((mm(xg[me], wp[0]) + bq[...].reshape(1, -1)).astype(BF).astype(F32) * (HEAD**-0.5)).astype(BF)
     for i in range(PAIRS):
         pair = q[:, 128 * i : 128 * (i + 1)]
         qn[i] = pair
@@ -194,7 +194,7 @@
         block = block_at(step)
         x = xg[block]
         keys = mm(x, wp[1]).astype(BF)
-        values = (mm(x, wp[2]) + bv[...]).astype(BF)
+        values = (mm(x, wp[2]) + bv[...].reshape(1, -1)).astype(BF)
         hot = key_codes(lens, block, rows)
         hot_low, hot_high = hot * low, hot * high
         xt[block] = x.T
@@ -302,14 +302,361 @@
     return high, middle, values - high - middle
 
 
-def attend_back_kernel(
-    kn_h, vn_h, kt_h, xt_h, qn, qt, d_att, d_att_t, delta, lse, wp, lens,
-    dx_o, gw_o, gbias_o,
-    kn, vn, kt, xt, qta, dta, qh, dh, dqt, gk, gv, dk, dv, in_sem,
-):
+def dp_place():
+    dp = lax.axis_index("dp")
+    core, x, y = dp % 2, (dp // 2) % 2, dp // 4
+    return (core, x, y), (dp + 1 - 2 * core, dp + 2 - 4 * x, dp + 4 - 8 * y)
+
+
+class DpSum:
+    def __init__(self, first, stage, one, two, three, send, recv):
+        self.first, self.stage, self.one, self.two, self.three = first, stage, one, two, three
+        (self.core, self.x, self.y), (self.to_core, self.to_x, self.to_y) = dp_place()
+        self.send, self.recv = send, recv
+
+    def copy(self, phase):
+        x_first = self.first == "x"
+        if phase == 0:
+            src, dst, to = self.stage.at[:, :, 1 - self.core], self.one, self.to_core
+        elif phase == 1:
+            src = self.one.at[:, 1 - self.x] if x_first else self.one.at[1 - self.y]
+            dst, to = self.two, self.to_x if x_first else self.to_y
+        else:
+            src = self.two.at[1 - self.y] if x_first else self.two.at[1 - self.x]
+            dst, to = self.three, self.to_y if x_first else self.to_x
+        return pltpu.make_async_remote_copy(
+            src_ref=src, dst_ref=dst, send_sem=self.send.at[phase], recv_sem=self.recv.at[phase],
+            device_id={"dp": to}, device_id_type=MESH,
+        )
+
+    def start(self, phase):
+        self.copy(phase).start()
+
+    def finish(self, phase):
+        self.copy(phase).wait_recv()
+        x_first = self.first == "x"
+        if phase == 0:
+            for y in range(2):
+                for x in range(2):
+                    self.one[y, x] = self.one[y, x] + self.stage[y, x, self.core]
+        elif phase == 1:
+            for other in range(2):
+                kept = self.one[other, self.x] if x_first else self.one[self.y, other]
+                self.two[other] = self.two[other] + kept
+        else:
+            kept = self.two[self.y] if x_first else self.two[self.x]
+            self.three[...] = self.three[...] + kept
+
+    def wait_sends(self, phases):
+        for phase in phases:
+            self.copy(phase).wait_send()
+
+
+class SeqSum:
+    def __init__(self, part, from_end, swapped, total, send, recv):
+        self.part, self.from_end, self.swapped, self.total = part, from_end, swapped, total
+        self.send, self.recv = send, recv
+        me = lax.axis_index("seq")
+        self.end = (me == 0) | (me == 3)
+        self.partner = jnp.where(me < 2, 1 - me, 5 - me)
+        self.other = 3 - me
+
+    def copy(self, phase):
+        src, dst, to = (
+            (self.part, self.from_end, self.partner),
+            (self.part, self.swapped, self.other),
+            (self.total, self.total, self.partner),
+        )[phase]
+        return pltpu.make_async_remote_copy(
+            src_ref=src, dst_ref=dst, send_sem=self.send.at[phase], recv_sem=self.recv.at[phase],
+            device_id={"seq": to}, device_id_type=MESH,
+        )
+
+    def ends_send(self):
+        @pl.when(self.end)
+        def _():
+            self.copy(0).start()
+
+    def middles_swap(self):
+        @pl.when(~self.end)
+        def _():
+            self.copy(0).wait_recv()
+            self.part[...] = self.part[...] + self.from_end[...]
+            self.copy(1).start()
+
+    def middles_send(self):
+        @pl.when(~self.end)
+        def _():
+            self.copy(1).wait_recv()
+            self.total[...] = self.part[...] + self.swapped[...]
+            self.copy(2).start()
+
+    def finish(self):
+        @pl.when(self.end)
+        def _():
+            self.copy(0).wait_send()
+            self.copy(2).wait_recv()
+
+        @pl.when(~self.end)
+        def _():
+            self.copy(1).wait_send()
+            self.copy(2).wait_send()
+
+
+CHUNKS = 3
+GROUPS = 8
+
+
+def chunk_columns(ff, c, d):
+    return (ff // GROUPS) * d + 128 * c
+
+
+def feed_forward_kernel(fast, *refs):
+    (
+        tok, att, att_f, cot, w_out, b_out, gain, shift, b_up, b_down, w_up_h, w_down_h,
+        layer_o, d_mid_o, d_att_o, d_att_t_o, delta_o, vec_o, vec_up_o, gd_o, gu_o, go_o, *refs,
+    ) = refs
+    if fast:
+        d3_o, u3_o, *refs = refs
+    wu, wd, stage_d, stage_u, stage_o, *refs = refs
+    if fast:
+        one_d, one_u, one_o, two_d, two_u, three_d, three_u, send, recv, *refs = refs
+    in_sem, out_sem = refs
+    rows, width = tok.shape
+    ff = w_up_h.shape[1]
+    span = GROUPS * 128
+
+    def loads(c):
+        found = []
+        for d in range(GROUPS):
+            at = pl.ds(chunk_columns(ff, c, d), 128)
+            to = pl.ds(128 * d, 128)
+            found.append(pltpu.make_async_copy(w_up_h.at[:, at], wu.at[c, :, to], in_sem.at[0, c, d]))
+            found.append(pltpu.make_async_copy(w_down_h.at[at], wd.at[c, to], in_sem.at[1, c, d]))
+        return found
+
+    for c in range(CHUNKS):
+        for copy in loads(c):
+            copy.start()
+    if fast:
+        barrier = pltpu.get_barrier_semaphore()
+        for to in dp_place()[1]:
+            pl.semaphore_signal(barrier, inc=1, device_id={"dp": to}, device_id_type=MESH)
+        pl.semaphore_wait(barrier, 3)
+        sums_d = [
+            DpSum("x", stage_d.at[c], one_d.at[c], two_d, three_d, send.at[c], recv.at[c]) for c in range(CHUNKS)
+        ]
+        sums_u = [
+            DpSum("y", stage_u.at[c], one_u.at[c], two_u, three_u, send.at[3 + c], recv.at[3 + c]) for c in range(CHUNKS)
+        ]
+        sum_o = DpSum("x", stage_o, one_o, None, None, send.at[6], recv.at[6])
+
+    def per_row(ref):
+        return ref[...].reshape(1, -1)
+
+    middle = tok[...].astype(F32) + mm(att[...], w_out[...]) + per_row(b_out)
+    average = jnp.mean(middle, axis=-1, keepdims=True)
+    centred = middle - average
+    scale = lax.rsqrt(jnp.mean(centred * centred, axis=-1, keepdims=True) + EPS)
+    unit = centred * scale
+    normed = (unit * per_row(gain) + per_row(shift)).astype(BF)
+    normed_t = normed.T
+    d_out = cot[...]
+    up_bias = b_up[...].reshape(1, -1)
+    total = middle + per_row(b_down)
+    d_normed = jnp.zeros((rows, width), F32)
+    vec_up_o[...] = jnp.zeros_like(vec_up_o)
+    vec_o[...] = jnp.zeros_like(vec_o)
+
+    for c in range(CHUNKS):
+        for copy in loads(c):
+            copy.wait()
+        bias = jnp.concatenate(
+            [up_bias[:, chunk_columns(ff, c, d) : chunk_columns(ff, c, d) + 128] for d in range(GROUPS)], axis=1
+        )
+        upper = mm(normed, wu[c]) + bias
+        cdf = 0.5 * (1.0 + lax.erf(upper * ROOT_HALF))
+        hidden = (upper * cdf).astype(BF)
+        slope = cdf + upper * (jnp.exp(-0.5 * upper * upper) * 0.3989422804014327)
+        d_upper_f = mm_nt(d_out, wd[c]) * slope
+        d_upper = d_upper_f.astype(BF)
+        vec_up_o[c : c + 1] = jnp.sum(d_upper.astype(F32), axis=0, keepdims=True)
+        if fast and c == 1:
+            for unit_sum in (sums_d[0], sums_u[0]):
+                unit_sum.finish(0)
+                unit_sum.start(1)
+        if fast and c == 2:
+            for unit_sum in (sums_d[0], sums_u[0]):
+                unit_sum.finish(1)
+                unit_sum.start(2)
+            for unit_sum in (sums_d[1], sums_u[1]):
+                unit_sum.finish(0)
+        total = total + mm(hidden, wd[c])
+        d_normed = d_normed + mm_nt(d_upper, wu[c])
+        g_down = mm(hidden.T, d_out).astype(BF)
+        g_up = mm(normed_t, d_upper).astype(BF)
+        for d in range(GROUPS):
+            y, x, core = d // 4, (d // 2) % 2, d % 2
+            stage_d[c, y, x, core] = g_down[128 * d : 128 * (d + 1)]
+            stage_u[c, y, x, core] = g_up[96 * d : 96 * (d + 1)]
+        if fast:
+            sums_d[c].start(0)
+            sums_u[c].start(0)
+    layer_o[...] = total.astype(BF)
+    vec_o[3:4] = jnp.sum(d_out.astype(F32), axis=0, keepdims=True)
+    vec_o[1:2] = jnp.sum(d_normed * unit, axis=0, keepdims=True)
+    vec_o[2:3] = jnp.sum(d_normed, axis=0, keepdims=True)
+    scaled = d_normed * per_row(gain)
+    d_middle = d_out.astype(F32) + scale * (
+        scaled
+        - jnp.mean(scaled, axis=-1, keepdims=True)
+        - unit * jnp.mean(scaled * unit, axis=-1, keepdims=True)
+    )
+    d_mid_o[...] = d_middle
+    d_branch = d_middle.astype(BF)
+    vec_o[0:1] = jnp.sum(d_branch.astype(F32), axis=0, keepdims=True)
+    g_out = mm(att_f[...].astype(BF), d_branch).astype(BF)
+    for d in range(GROUPS):
+        stage_o[d // 4, (d // 2) % 2, d % 2] = g_out[96 * d : 96 * (d + 1)]
+    if fast:
+        sum_o.start(0)
+        for unit_sum in (sums_d[2], sums_u[2]):
+            unit_sum.finish(0)
+    d_att = mm_nt(d_branch, w_out[...]).astype(BF)
+    d_att_o[...] = d_att
+    d_att_t = d_att.T
+    d_att_t_o[...] = d_att_t
+    product = d_att_t.astype(F32) * att_f[...]
+    delta_o[...] = jnp.zeros_like(delta_o)
+    for h in range(HEADS):
+        delta_o[h : h + 1] = jnp.sum(product[64 * h : 64 * (h + 1)], axis=0, keepdims=True)
+    if fast:
+        keep = [
+            pltpu.make_async_copy(one_d.at[pl.ds(1, 2)], gd_o, out_sem.at[0]),
+            pltpu.make_async_copy(one_u.at[pl.ds(1, 2)], gu_o, out_sem.at[1]),
+        ]
+        for copy in keep:
+            copy.start()
+        sum_o.finish(0)
+        keep.append(pltpu.make_async_copy(one_o, go_o, out_sem.at[2]))
+        keep[-1].start()
+        for unit_sum in (sums_d[0], sums_u[0]):
+            unit_sum.finish(2)
+        keep.append(pltpu.make_async_copy(three_d, d3_o, out_sem.at[3]))
+        keep.append(pltpu.make_async_copy(three_u, u3_o, out_sem.at[4]))
+        for copy in keep[3:]:
+            copy.start()
+        for c in range(CHUNKS):
+            phases = (0, 1, 2) if c == 0 else (0,)
+            sums_d[c].wait_sends(phases)
+            sums_u[c].wait_sends(phases)
+        sum_o.wait_sends((0,))
+    else:
+        keep = [
+            pltpu.make_async_copy(stage_d, gd_o, out_sem.at[0]),
+            pltpu.make_async_copy(stage_u, gu_o, out_sem.at[1]),
+            pltpu.make_async_copy(stage_o, go_o, out_sem.at[2]),
+        ]
+        for copy in keep:
+            copy.start()
+    for copy in keep:
+        copy.wait()
+
+
+def feed_forward(fast, tokens, att, att_f, cot, w_out, b_out, gain, shift, b_up, b_down, w_up, w_down):
+    rows, width = tokens.shape
+    ff = w_up.shape[1]
+    span = GROUPS * 128
+    part_w, part_o = width // GROUPS, width // GROUPS
+    any_spec = pl.BlockSpec(memory_space=pl.ANY)
+    vmem = pl.BlockSpec(memory_space=pltpu.VMEM)
+    sds = jax.ShapeDtypeStruct
+    cube = (2, 2, 2)
+    outs = [
+        sds((rows, width), BF), sds((rows, width), F32), sds((rows, width), BF), sds((width, rows), BF),
+        sds((16, rows), F32), sds((8, width), F32), sds((8, span), F32),
+    ]
+    out_specs = [vmem] * 7
+    scratch = [
+        pltpu.VMEM((CHUNKS, width, span), BF),
+        pltpu.VMEM((CHUNKS, span, width), BF),
+        pltpu.VMEM((CHUNKS, *cube, 128, width), BF),
+        pltpu.VMEM((CHUNKS, *cube, part_w, span), BF),
+        pltpu.VMEM((*cube, part_o, width), BF),
+    ]
+    if fast:
+        outs += [
+            sds((2, 2, 2, 128, width), BF), sds((2, 2, 2, part_w, span), BF), sds((2, 2, part_o, width), BF),
+            sds((128, width), BF), sds((part_w, span), BF),
+        ]
+        scratch += [
+            pltpu.VMEM((CHUNKS, 2, 2, 128, width), BF),
+            pltpu.VMEM((CHUNKS, 2, 2, part_w, span), BF),
+            pltpu.VMEM((2, 2, part_o, width), BF),
+            pltpu.VMEM((2, 128, width), BF),
+            pltpu.VMEM((2, part_w, span), BF),
+            pltpu.VMEM((128, width), BF),
+            pltpu.VMEM((part_w, span), BF),
+            pltpu.SemaphoreType.DMA((7, 3)),
+            pltpu.SemaphoreType.DMA((7, 3)),
+        ]
+    else:
+        outs += [
+            sds((CHUNKS, *cube, 128, width), BF), sds((CHUNKS, *cube, part_w, span), BF), sds((*cube, part_o, width), BF),
+        ]
+    out_specs += [any_spec] * (len(outs) - 7)
+    scratch += [pltpu.SemaphoreType.DMA((2, CHUNKS, GROUPS)), pltpu.SemaphoreType.DMA((5,))]
+    params = dict(vmem_limit_bytes=58 * MIB)
+    if fast:
+        params.update(collective_id=1, has_side_effects=True)
+    return pl.pallas_call(
+        partial(feed_forward_kernel, fast),
+        out_shape=outs,
+        in_specs=[vmem] * 10 + [any_spec] * 2,
+        out_specs=out_specs,
+        scratch_shapes=scratch,
+        compiler_params=pltpu.CompilerParams(**params),
+        name="feed_forward",
+    )(tokens, att, att_f, cot, w_out, b_out, gain, shift, b_up, b_down, w_up, w_down)
+
+
+def attend_back_kernel(fast, *refs):
+    (
+        kn_h, vn_h, kt_h, xt_h, qn, qt_h, d_att, d_att_t_h, delta, lse, wp_h, lens, tok_h, d_mid_h, gain, vec, vec_up,
+        *refs,
+    ) = refs
+    if fast:
+        one_d_h, one_u_h, one_o_h, d3_h, u3_h, *refs = refs
+    tok_o, *refs = refs
+    if fast:
+        fin_d_o, fin_u_o, fin_o_o, fin_q_o, fin_v_o, *refs = refs
+    else:
+        gw_o, stage_v_o, *refs = refs
+    (
+        kn, vn, kt, xt, qta, dta, dqt, gk, gv, dk, dv, wp, tok, d_mid, dx_own, dxs, rx, stage_q, stage_v, sums,
+        in_sem, load_sem, out_sem, dsend, drecv, *refs,
+    ) = refs
     rows, width = d_att.shape
     seq = lax.axis_size("seq")
     me = lax.axis_index("seq")
+    has_left, has_right = me > 0, me < seq - 1
+    at_end = (me == 0) | (me == seq - 1)
+    part_w = width // GROUPS
+
+    barrier = pltpu.get_barrier_semaphore()
+
+    @pl.when(has_left)
+    def _():
+        pl.semaphore_signal(barrier, inc=1, device_id={"seq": me - 1}, device_id_type=MESH)
+
+    @pl.when(has_right)
+    def _():
+        pl.semaphore_signal(barrier, inc=1, device_id={"seq": me + 1}, device_id_type=MESH)
+
+    if fast:
+        for to in dp_place()[1]:
+            pl.semaphore_signal(barrier, inc=1, device_id={"dp": to}, device_id_type=MESH)
+    greeted = 3 if fast else 0
 
     def block_at(step):
         b0 = jnp.where(me < 2, seq - 1, 0)
@@ -318,54 +665,187 @@
         return jnp.where(step == 0, b0, jnp.where(step == 1, b1, jnp.where(step == 2, b2, me)))
 
     def loads(step):
-        block = block_at(step)
+        block, slot = block_at(step), step % 2
         return [
-            pltpu.make_async_copy(kn_h.at[block], kn.at[step], in_sem.at[step, 0]),
-            pltpu.make_async_copy(vn_h.at[block], vn.at[step], in_sem.at[step, 1]),
-            pltpu.make_async_copy(kt_h.at[block], kt.at[step], in_sem.at[step, 2]),
-            pltpu.make_async_copy(xt_h.at[block], xt.at[step], in_sem.at[step, 3]),
-        ]
-
-    for step in range(4):
-        for c in loads(step):
-            c.start()
+            pltpu.make_async_copy(kn_h.at[block], kn.at[slot], in_sem.at[slot, 0]),
+            pltpu.make_async_copy(vn_h.at[block], vn.at[slot], in_sem.at[slot, 1]),
+            pltpu.make_async_copy(kt_h.at[block], kt.at[slot], in_sem.at[slot, 2]),
+            pltpu.make_async_copy(xt_h.at[block], xt.at[slot], in_sem.at[slot, 3]),
+        ]
+
+    def halves(j):
+        return (slice(0, 64), slice(64, 128)) if j == 0 else (slice(64, 128), slice(0, 64))
+
+    fills = []
+    for h in range(HEADS):
+        own = pl.ds(64 * (h % 2), 64)
+        fills.append(pltpu.make_async_copy(qt_h.at[h // 2, own], qta.at[h, own], load_sem.at[h]))
+        fills.append(pltpu.make_async_copy(d_att_t_h.at[pl.ds(64 * h, 64)], dta.at[h, own], load_sem.at[HEADS + h]))
+    for copy in fills:
+        copy.start()
+    for copy in loads(0):
+        copy.start()
+    late = [
+        pltpu.make_async_copy(wp_h, wp, load_sem.at[24]),
+        pltpu.make_async_copy(tok_h, tok, load_sem.at[25]),
+        pltpu.make_async_copy(d_mid_h, d_mid, load_sem.at[26]),
+    ]
+    for copy in late:
+        copy.start()
+    if fast:
+        (
+            one_d, one_u, one_o, two_d, two_u, two_o, three_d, three_u, three_o,
+            one_q, two_q, three_q, one_v, two_v, three_v,
+            za_d, zx_d, fin_d, za_u, zx_u, fin_u, za_o, zx_o, fin_o, za_q, zx_q, fin_q, za_v, zx_v, fin_v,
+            psend, precv, zsend, zrecv,
+        ) = refs
+        early = [
+            pltpu.make_async_copy(d3_h, three_d.at[0], load_sem.at[27]),
+            pltpu.make_async_copy(u3_h, three_u.at[0], load_sem.at[28]),
+            pltpu.make_async_copy(one_d_h.at[0], one_d.at[0], load_sem.at[29]),
+            pltpu.make_async_copy(one_u_h.at[0], one_u.at[0], load_sem.at[30]),
+            pltpu.make_async_copy(one_d_h.at[1], one_d.at[1], load_sem.at[31]),
+            pltpu.make_async_copy(one_u_h.at[1], one_u.at[1], load_sem.at[32]),
+            pltpu.make_async_copy(one_o_h, one_o, load_sem.at[33]),
+        ]
+        for copy in early:
+            copy.start()
+        rs_d = [DpSum("x", None, one_d.at[c], two_d.at[c], three_d.at[c + 1], psend.at[c], precv.at[c]) for c in range(2)]
+        rs_u = [
+            DpSum("y", None, one_u.at[c], two_u.at[c], three_u.at[c + 1], psend.at[2 + c], precv.at[2 + c])
+            for c in range(2)
+        ]
+        rs_o = DpSum("x", None, one_o, two_o, three_o, psend.at[4], precv.at[4])
+        rs_q = [
+            DpSum("xy"[c], stage_q.at[c], one_q.at[c], two_q.at[c], three_q.at[c], psend.at[5 + c], precv.at[5 + c])
+            for c in range(2)
+        ]
+        rs_v = DpSum("x", stage_v, one_v, two_v, three_v, psend.at[7], precv.at[7])
+        ar_d = [
+            SeqSum(three_d.at[c], za_d.at[c], zx_d.at[c], fin_d.at[c], zsend.at[c], zrecv.at[c]) for c in range(3)
+        ]
+        ar_u = [
+            SeqSum(three_u.at[c], za_u.at[c], zx_u.at[c], fin_u.at[c], zsend.at[3 + c], zrecv.at[3 + c]) for c in range(3)
+        ]
+        ar_o = SeqSum(three_o, za_o, zx_o, fin_o, zsend.at[6], zrecv.at[6])
+        ar_q = [
+            SeqSum(three_q.at[c], za_q.at[c], zx_q.at[c], fin_q.at[c], zsend.at[7 + c], zrecv.at[7 + c]) for c in range(2)
+        ]
+        ar_v = SeqSum(three_v, za_v, zx_v, fin_v, zsend.at[9], zrecv.at[9])
 
     low, high = lane_halves()
     codes = query_codes(lens, me, rows)
     row64 = lax.broadcasted_iota(jnp.int32, (64, rows), 0)
     for h in range(HEADS):
-        i, j = h // 2, h % 2
-        own, other = (slice(0, 64), slice(64, 128)) if j == 0 else (slice(64, 128), slice(0, 64))
+        _, other = halves(h % 2)
         extra = codes
         for r, part in enumerate(three_parts(-lse[h : h + 1])):
             extra = jnp.where(row64 == 8 + r, part, extra)
-        qta[h, own] = qt[i, own]
         qta[h, other] = extra.astype(BF)
         extra = jnp.zeros((64, rows), F32)
         for r, part in enumerate(three_parts(-delta[h : h + 1])):
             extra = jnp.where(row64 == r, part, extra)
-        dta[h, own] = d_att_t[64 * h : 64 * (h + 1)]
         dta[h, other] = extra.astype(BF)
-        half = low if j == 0 else high
-        qh[h] = qn[i] * half
-        dh[h] = d_att[:, 128 * i : 128 * (i + 1)] * half
     dqt[...] = jnp.zeros_like(dqt)
     gk[...] = jnp.zeros_like(gk)
     gv[...] = jnp.zeros_like(gv)
-    gbias_o[...] = jnp.zeros_like(gbias_o)
+    stage_v[...] = jnp.zeros_like(stage_v)
+    sums[...] = jnp.zeros_like(sums)
     lane = lax.broadcasted_iota(jnp.int32, (1, 128), 1)
     v_low = jnp.where(lane < 3, 1.0, 0.0).astype(BF)
     v_high = jnp.where((lane >= 64) & (lane < 67), 1.0, 0.0).astype(BF)
+    for copy in fills:
+        copy.wait()
+
+    @pl.when(at_end)
+    def _():
+        pl.semaphore_wait(barrier, greeted + 1)
+
+    @pl.when(~at_end)
+    def _():
+        pl.semaphore_wait(barrier, greeted + 2)
+
+    def dx_copy(way, block):
+        return pltpu.make_async_remote_copy(
+            src_ref=dxs.at[block], dst_ref=rx.at[block + way],
+            send_sem=dsend.at[way, block], recv_sem=drecv.at[way, block],
+            device_id={"seq": me - 1 if way == 0 else me + 1}, device_id_type=MESH,
+        )
+
+    def relay(way, block):
+        dx_copy(way, block).wait_recv()
+        dxs[block] = dxs[block] + rx[block + way]
+        dx_copy(way, block).start()
+
+    def relay_at(place, way, step):
+        @pl.when(me == place)
+        def _():
+            relay(way, block_at(step))
+
+    def hooks(g):
+        if not fast:
+            return
+
+        def at(when, action):
+            @pl.when(g == when)
+            def _():
+                action()
+
+        def chunk0_out():
+            for copy in early[:4]:
+                copy.wait()
+            ar_d[0].ends_send()
+            ar_u[0].ends_send()
+            rs_d[0].start(1)
+            rs_u[0].start(1)
+
+        def chunk2_out():
+            for copy in early[4:]:
+                copy.wait()
+            rs_d[1].start(1)
+            rs_u[1].start(1)
+
+        def turn(*sums):
+            for unit_sum in sums:
+                unit_sum.finish(1)
+                unit_sum.start(2)
+
+        def close(*sums):
+            for unit_sum in sums:
+                unit_sum.finish(2)
+
+        at(0, chunk0_out)
+        at(2, chunk2_out)
+        at(4, lambda: (ar_d[0].middles_swap(), ar_u[0].middles_swap()))
+        at(5, lambda: turn(rs_d[0], rs_u[0]))
+        at(7, lambda: rs_o.start(1))
+        at(8, lambda: (ar_d[0].middles_send(), ar_u[0].middles_send()))
+        at(9, lambda: close(rs_d[0], rs_u[0]))
+        at(11, lambda: turn(rs_d[1], rs_u[1]))
+        at(14, lambda: close(rs_d[1], rs_u[1]))
+        at(15, lambda: (relay_at(1, 1, 0), relay_at(2, 0, 0)))
+        at(16, lambda: turn(rs_o))
+        at(19, lambda: close(rs_o))
 
     def one_step(step, carry):
-        for c in loads(step):
-            c.wait()
+        slot = step % 2
+        for copy in loads(step):
+            copy.wait()
+
+        @pl.when(step < seq - 1)
+        def _():
+            for copy in loads(step + 1):
+                copy.start()
+
         block = block_at(step)
         hot = key_codes(lens, block, rows)
         hot_low, hot_high = hot * low, hot * high
 
         def one_pair(i, carry):
-            keys, values = kn[step, i], vn[step, i]
+            hooks(step * PAIRS + i)
+            at = pl.ds(pl.multiple_of(i * 128, 128), 128)
+            keys, values = kn[slot, i], vn[slot, i]
+            q_pair, d_pair = qn[i], d_att[:, at]
             scores = [
                 mm(keys * low + hot_high, qta[2 * i]),
                 mm(keys * high + hot_low, qta[2 * i + 1]),
@@ -378,83 +858,274 @@
             d_values = jnp.zeros((rows, 128), F32)
             for j in range(2):
                 h = 2 * i + j
+                half = low if j == 0 else high
                 probs = jnp.exp(scores[j])
                 d_scores = (probs * slopes[j]).astype(BF)
-                d_values = d_values + mm(probs.astype(BF), dh[h])
-                d_keys = d_keys + mm(d_scores, qh[h])
-                dqt[h] += mm(kt[step, i, 64 * j : 64 * (j + 1)], d_scores)
-            at = pl.ds(pl.multiple_of(i * 128, 128), 128)
+                d_values = d_values + mm(probs.astype(BF), d_pair * half)
+                d_keys = d_keys + mm(d_scores, q_pair * half)
+                dqt[h] += mm(kt[slot, i, 64 * j : 64 * (j + 1)], d_scores)
             dk[:, at] = d_keys.astype(BF)
             dv[:, at] = d_values.astype(BF)
             return carry
 
         lax.fori_loop(0, PAIRS, one_pair, 0)
+
+        @pl.when(step == 0)
+        def _():
+            late[0].wait()
+
         dx = mm_nt(dk[...], wp[1]) + mm_nt(dv[...], wp[2])
-        gk[...] += mm(xt[step], dk[...])
-        gv[...] += mm(xt[step], dv[...])
-        gbias_o[1:2] += jnp.sum(dv[...].astype(F32), axis=0, keepdims=True)
 
         @pl.when(step < seq - 1)
         def _():
-            dx_o[block] = dx.astype(BF)
+            dxs[block] = dx.astype(BF)
+
+            @pl.when(me == 0)
+            def _():
+                dx_copy(1, block).start()
+
+            @pl.when(me == seq - 1)
+            def _():
+                dx_copy(0, block).start()
 
         @pl.when(step == seq - 1)
         def _():
-            turned = (dqt[...] * (HEAD**-0.5)).reshape(width, rows).T
-            dq = turned.astype(BF)
-            dx_o[block] = (dx + mm_nt(dq, wp[0])).astype(BF)
-            gbias_o[0:1] = jnp.sum(dq.astype(F32), axis=0, keepdims=True)
-            gq = mm(xt[step], dq)
-            lane_w = lax.broadcasted_iota(jnp.int32, (width, 128), 1)
-            lo = lane_w < 64
-            for i in range(PAIRS):
-                at = slice(128 * i, 128 * (i + 1))
-                k_turned = pltpu.roll(gk[:, at], 64, 1)
-                t0 = jnp.where(lo, gq[:, at], k_turned)
-                t1 = jnp.where(lo, gv[:, at], gq[:, at])
-                t2 = jnp.where(lo, k_turned, gv[:, at])
-                for j, t in enumerate((t0, t1, t2)):
-                    gw_o[:, 384 * i + 128 * j : 384 * i + 128 * (j + 1)] = t.astype(BF)
-
+            dx_own[...] = dx
+
+        gk[...] += mm(xt[slot], dk[...])
+        gv[...] += mm(xt[slot], dv[...])
+        sums[3:4] += jnp.sum(dv[...].astype(F32), axis=0, keepdims=True)
         return carry
 
     lax.fori_loop(0, seq, one_step, 0)
-
-
-def attend_back(kn, vn, kt, xt, qn, qt, d_att, d_att_t, delta, lse, wp, lens):
+    last = (seq - 1) % 2
+    dq = ((dqt[...] * (HEAD**-0.5)).reshape(width, rows).T).astype(BF)
+    dx_own[...] += mm_nt(dq, wp[0])
+    sums[2:3] = jnp.sum(dq.astype(F32), axis=0, keepdims=True)
+    gq = mm(xt[last], dq)
+    lane_w = lax.broadcasted_iota(jnp.int32, (width, 128), 1)
+    lo = lane_w < 64
+    for i in range(PAIRS):
+        at = slice(128 * i, 128 * (i + 1))
+        k_turned = pltpu.roll(gk[:, at], 64, 1)
+        tiles = (
+            jnp.where(lo, gq[:, at], k_turned), jnp.where(lo, gv[:, at], gq[:, at]), jnp.where(lo, k_turned, gv[:, at])
+        )
+        for j, tile in enumerate(tiles):
+            tile = tile.astype(BF)
+            place = 3 * i + j
+            if not fast:
+                gw_o[:, 128 * place : 128 * (place + 1)] = tile
+                continue
+            to = slice(128 * (place % 9), 128 * (place % 9 + 1))
+            for d in range(GROUPS):
+                stage_q[place // 9, d // 4, (d // 2) % 2, d % 2, :, to] = tile[part_w * d : part_w * (d + 1)]
+        if fast and i == 2:
+            rs_q[0].start(0)
+    if fast:
+        rs_q[1].start(0)
+        for unit in (ar_d[1], ar_u[1], ar_d[2], ar_u[2], ar_o):
+            unit.ends_send()
+    relay_at(1, 1, 1)
+    relay_at(2, 0, 1)
+    relay_at(1, 0, 2)
+    relay_at(2, 1, 2)
+    if fast:
+        for unit in rs_q:
+            unit.finish(0)
+            unit.start(1)
+
+    late[1].wait()
+    late[2].wait()
+    for way, there in ((0, has_right), (1, has_left)):
+        @pl.when(there)
+        def _():
+            dx_copy(way, me).wait_recv()
+            dx_own[...] += rx[me + way].astype(F32)
+
+    values = tok[...].astype(F32)
+    centred = values - jnp.mean(values, axis=-1, keepdims=True)
+    scale = lax.rsqrt(jnp.mean(centred * centred, axis=-1, keepdims=True) + EPS)
+    unit_rows = centred * scale
+    d_normed = dx_own[...]
+    sums[0:1] = jnp.sum(d_normed * unit_rows, axis=0, keepdims=True)
+    sums[1:2] = jnp.sum(d_normed, axis=0, keepdims=True)
+    sums[4:8] = vec[0:4]
+    scaled = d_normed * gain[...].reshape(1, -1)
+    tok_o[...] = (
+        d_mid[...]
+        + scale
+        * (
+            scaled
+            - jnp.mean(scaled, axis=-1, keepdims=True)
+            - unit_rows * jnp.mean(scaled * unit_rows, axis=-1, keepdims=True)
+        )
+    ).astype(BF)
+    rows8 = sums[...]
+    for d in range(GROUPS):
+        y, x, core = d // 4, (d // 2) % 2, d % 2
+        stage_v[y, x, core, 0:8, 0:part_w] = rows8[:, part_w * d : part_w * (d + 1)]
+        stage_v[y, x, core, 8 : 8 + CHUNKS] = vec_up[0:CHUNKS, 128 * d : 128 * (d + 1)]
+    if fast:
+        rs_v.start(0)
+        for unit in (ar_d[1], ar_u[1], ar_d[2], ar_u[2], ar_o):
+            unit.middles_swap()
+        rs_v.finish(0)
+        rs_v.start(1)
+        for unit in rs_q:
+            unit.finish(1)
+            unit.start(2)
+        rs_v.finish(1)
+        rs_v.start(2)
+        for unit in (ar_d[1], ar_u[1], ar_d[2], ar_u[2], ar_o):
+            unit.middles_send()
+        rs_v.finish(2)
+        ar_v.ends_send()
+        for unit in rs_q:
+            unit.finish(2)
+        for unit in ar_q:
+            unit.ends_send()
+        ar_v.middles_swap()
+        for unit in ar_q:
+            unit.middles_swap()
+        ar_v.middles_send()
+        for unit in ar_q:
+            unit.middles_send()
+        for unit in (*ar_d, *ar_u, ar_o, ar_v, *ar_q):
+            unit.finish()
+        keep = [
+            pltpu.make_async_copy(src, dst, out_sem.at[k])
+            for k, (src, dst) in enumerate(
+                ((fin_d, fin_d_o), (fin_u, fin_u_o), (fin_o, fin_o_o), (fin_q, fin_q_o), (fin_v, fin_v_o))
+            )
+        ]
+        for copy in keep:
+            copy.start()
+        for unit in (*rs_d, *rs_u, rs_o):
+            unit.wait_sends((1, 2))
+        for unit in (*rs_q, rs_v):
+            unit.wait_sends((0, 1, 2))
+        for copy in keep:
+            copy.wait()
+    else:
+        stage_v_o[...] = stage_v[...]
+
+    for place, first, second in ((0, 1, 1), (1, 1, 0), (2, 0, 1), (3, 0, 0)):
+        @pl.when(me == place)
+        def _():
+            for step, way in enumerate((first, first, second)):
+                dx_copy(way, block_at(step)).wait_send()
+
+
+def attend_back(fast, kn, vn, kt, xt, qn, qt, d_att, d_att_t, delta, lse, wp, lens, tokens, d_mid, gain, vec, vec_up, *ready):
     seq, _, rows, _ = kn.shape
     width = wp.shape[1]
+    span = GROUPS * 128
+    part = width // GROUPS
+    half = 3 * width // 2
     any_spec = pl.BlockSpec(memory_space=pl.ANY)
     vmem = pl.BlockSpec(memory_space=pltpu.VMEM)
     sds = jax.ShapeDtypeStruct
+    cube = (2, 2, 2)
+    outs = [sds((rows, width), BF)]
+    out_specs = [vmem]
+    if fast:
+        outs += [
+            sds((CHUNKS, 128, width), BF), sds((CHUNKS, part, span), BF), sds((part, width), BF),
+            sds((2, part, half), BF), sds((16, 128), F32),
+        ]
+        out_specs += [any_spec] * 5
+    else:
+        outs += [sds((width, 3 * width), BF), sds((*cube, 16, 128), F32)]
+        out_specs += [vmem] * 2
+    scratch = [
+        pltpu.VMEM((2, PAIRS, rows, 128), BF),
+        pltpu.VMEM((2, PAIRS, rows, 128), BF),
+        pltpu.VMEM((2, PAIRS, 128, rows), BF),
+        pltpu.VMEM((2, width, rows), BF),
+        pltpu.VMEM((HEADS, 128, rows), BF),
+        pltpu.VMEM((HEADS, 128, rows), BF),
+        pltpu.VMEM((HEADS, HEAD, rows), F32),
+        pltpu.VMEM((width, width), F32),
+        pltpu.VMEM((width, width), F32),
+        pltpu.VMEM((rows, width), BF),
+        pltpu.VMEM((rows, width), BF),
+        pltpu.VMEM((3, width, width), BF),
+        pltpu.VMEM((rows, width), BF),
+        pltpu.VMEM((rows, width), F32),
+        pltpu.VMEM((rows, width), F32),
+        pltpu.VMEM((seq, rows, width), BF),
+        pltpu.VMEM((seq + 1, rows, width), BF),
+        pltpu.VMEM((2, *cube, part, half) if fast else (8, 128), BF),
+        pltpu.VMEM((*cube, 16, 128), F32),
+        pltpu.VMEM((8, width), F32),
+        pltpu.SemaphoreType.DMA((2, 4)),
+        pltpu.SemaphoreType.DMA((34,)),
+        pltpu.SemaphoreType.DMA((5,)),
+        pltpu.SemaphoreType.DMA((2, 4)),
+        pltpu.SemaphoreType.DMA((2, 4)),
+    ]
+    if fast:
+        d, u, o, q = (128, width), (part, span), (part, width), (part, half)
+        scratch += [
+            pltpu.VMEM(shape, BF)
+            for shape in (
+                (2, 2, 2, *d), (2, 2, 2, *u), (2, 2, *o), (2, 2, *d), (2, 2, *u), (2, *o), (3, *d), (3, *u), o,
+                (2, 2, 2, *q), (2, 2, *q), (2, *q),
+            )
+        ]
+        scratch += [pltpu.VMEM((2, 2, 16, 128), F32), pltpu.VMEM((2, 16, 128), F32), pltpu.VMEM((16, 128), F32)]
+        for shape in ((3, *d), (3, *u), o, (2, *q)):
+            scratch += [pltpu.VMEM(shape, BF)] * 3
+        scratch += [pltpu.VMEM((16, 128), F32)] * 3
+        scratch += [pltpu.SemaphoreType.DMA(shape) for shape in ((8, 3), (8, 3), (10, 3), (10, 3))]
     return pl.pallas_call(
-        attend_back_kernel,
-        out_shape=[
-            sds((seq, rows, width), BF),
-            sds((width, 3 * width), BF),
-            sds((8, width), F32),
-        ],
-        in_specs=[any_spec] * 4 + [vmem] * 7 + [pl.BlockSpec(memory_space=pltpu.SMEM)],
-        out_specs=[vmem] * 3,
-        scratch_shapes=[
-            pltpu.VMEM((seq, PAIRS, rows, 128), BF),
-            pltpu.VMEM((seq, PAIRS, rows, 128), BF),
-            pltpu.VMEM((seq, PAIRS, 128, rows), BF),
-            pltpu.VMEM((seq, width, rows), BF),
-            pltpu.VMEM((HEADS, 128, rows), BF),
-            pltpu.VMEM((HEADS, 128, rows), BF),
-            pltpu.VMEM((HEADS, rows, 128), BF),
-            pltpu.VMEM((HEADS, rows, 128), BF),
-            pltpu.VMEM((HEADS, HEAD, rows), F32),
-            pltpu.VMEM((width, width), F32),
-            pltpu.VMEM((width, width), F32),
-            pltpu.VMEM((rows, width), BF),
-            pltpu.VMEM((rows, width), BF),
-            pltpu.SemaphoreType.DMA((4, 4)),
-        ],
-        compiler_params=pltpu.CompilerParams(vmem_limit_bytes=58 * MIB),
+        partial(attend_back_kernel, fast),
+        out_shape=outs,
+        in_specs=[any_spec] * 4
+        + [vmem, any_spec, vmem, any_spec, vmem, vmem, any_spec, pl.BlockSpec(memory_space=pltpu.SMEM)]
+        + [any_spec] * 2
+        + [vmem] * 3
+        + [any_spec] * len(ready),
+        out_specs=out_specs,
+        scratch_shapes=scratch,
+        compiler_params=pltpu.CompilerParams(
+            collective_id=2, has_side_effects=True, vmem_limit_bytes=62 * MIB
+        ),
         name="attend_back",
-    )(kn, vn, kt, xt, qn, qt, d_att, d_att_t, delta, lse, wp, lens)
+    )(kn, vn, kt, xt, qn, qt, d_att, d_att_t, delta, lse, wp, lens, tokens, d_mid, gain, vec, vec_up, *ready)
+
+
+def unpack_kernel(fin_d, fin_u, fin_o, fin_q, fin_v, down_o, up_o, out_o, qkv_o, *vec_o):
+    chunks, _, _ = fin_d.shape
+    part, span = fin_u.shape[1:]
+    half = fin_q.shape[2]
+    for c in range(chunks):
+        down_o[128 * c : 128 * (c + 1)] = fin_d[c].astype(F32)
+        for d in range(GROUPS):
+            at = chunk_columns(up_o.shape[1], c, d)
+            up_o[:, at : at + 128] = fin_u[c, :, 128 * d : 128 * (d + 1)].astype(F32)
+    out_o[...] = fin_o[...].astype(F32)
+    for c in range(2):
+        qkv_o[:, half * c : half * (c + 1)] = fin_q[c].astype(F32)
+    for r in range(8):
+        vec_o[r][...] = fin_v[r : r + 1, :part].reshape(part)
+    vec_o[8][...] = jnp.concatenate([fin_v[8 + c : 9 + c] for c in range(chunks)], axis=1).reshape(128 * chunks)
+
+
+def unpack(fin_d, fin_u, fin_o, fin_q, fin_v):
+    vmem = pl.BlockSpec(memory_space=pltpu.VMEM)
+    chunks, _, width = fin_d.shape
+    part, span = fin_u.shape[1:]
+    sds = jax.ShapeDtypeStruct
+    outs = [
+        sds((128 * chunks, width), F32), sds((part, span * chunks), F32), sds((part, width), F32),
+        sds((part, 2 * fin_q.shape[2]), F32),
+    ]
+    outs += [sds((part,), F32)] * 8 + [sds((128 * chunks,), F32)]
+    return pl.pallas_call(
+        unpack_kernel, out_shape=outs, in_specs=[vmem] * 5, out_specs=[vmem] * len(outs), name="unpack",
+    )(fin_d, fin_u, fin_o, fin_q, fin_v)
 
 
 def local(
@@ -462,67 +1133,48 @@
     ln2_gain, ln2_shift, w_up, b_up, w_down, b_down, cotangent,
 ):
     bucket_count, local_slots, width = tokens.shape
+    ff = w_up.shape[1]
     seq_count = lax.axis_size("seq")
     dp_count = lax.axis_size("dp")
+    fast = dp_count == GROUPS
     rows = bucket_count * local_slots
     flat = tokens.reshape(rows, width)
-    flat_tokens = flat.astype(F32)
-
-    def row(v):
-        return v.reshape(1, -1)
-
     kn, vn, kt, xt, qn, qt, wp, att_t, attended, lse = gather_attend(
-        flat, cell_lengths, row(ln1_gain), row(ln1_shift), w_qkv, row(b_query), row(b_value), seq_count
+        flat, cell_lengths, ln1_gain, ln1_shift, w_qkv, b_query, b_value, seq_count
     )
-    middle = flat_tokens + mm(attended, w_out) + b_out
-    normed_two = normalize(middle, ln2_gain, ln2_shift).astype(BF)
-    upper = mm(normed_two, w_up) + b_up
-    hidden = gelu_exact(upper).astype(BF)
-    layer_out = middle + mm(hidden, w_down) + b_down
-    layer_out = layer_out.astype(BF).reshape(tokens.shape)
-    d_output = cotangent.reshape(rows, width)
-    g_w_down = mm(hidden.T, d_output).astype(BF)
-    g_b_down = jnp.sum(d_output, axis=0, dtype=F32)
-    d_hidden = mm(d_output, w_down.T)
-    gelu_pull = jax.vjp(gelu_exact, upper)[1]
-    d_upper = gelu_pull(d_hidden)[0].astype(BF)
-    g_w_up = mm(normed_two.T, d_upper).astype(BF)
-    g_b_up = jnp.sum(d_upper, axis=0, dtype=F32)
-    d_normed_two = mm(d_upper, w_up.T)
-    second_pull = jax.vjp(normalize, middle, ln2_gain, ln2_shift)[1]
-    d_middle, g_ln2_gain, g_ln2_shift = second_pull(d_normed_two)
-    d_middle = d_middle + d_output.astype(F32)
-    d_branch = d_middle.astype(BF)
-    g_w_out = mm(attended.T, d_branch).astype(BF)
-    g_b_out = jnp.sum(d_branch, axis=0, dtype=F32)
-    d_att = mm(d_branch, w_out.T).astype(BF)
-    d_att_t = d_att.T
-    delta = jnp.sum((d_att_t.astype(F32) * att_t).reshape(HEADS, HEAD, rows), axis=1)
-    delta = jnp.pad(delta, ((0, 4), (0, 0)))
-    dx, g_w_qkv, g_bias = attend_back(kn, vn, kt, xt, qn, qt, d_att, d_att_t, delta, lse, wp, cell_lengths)
-    d_normed_one = lax.psum_scatter(dx, "seq", scatter_dimension=0, tiled=True).reshape(rows, width).astype(F32)
-    first_pull = jax.vjp(normalize, flat_tokens, ln1_gain, ln1_shift)[1]
-    d_tokens, g_ln1_gain, g_ln1_shift = first_pull(d_normed_one)
-    tokens_grad = (d_tokens + d_middle).astype(BF).reshape(tokens.shape)
-
-    def summed(g):
-        share = lax.psum_scatter(g, "dp", scatter_dimension=0, tiled=True)
-        return lax.psum(share, "seq").astype(F32)
-
-    g_w_down, g_w_up, g_w_out, g_w_qkv = summed(g_w_down), summed(g_w_up), summed(g_w_out), summed(g_w_qkv)
-    vectors = (g_ln1_gain, g_ln1_shift, g_bias[0], g_bias[1], g_b_out, g_ln2_gain, g_ln2_shift, g_b_up, g_b_down)
-    packed = jnp.concatenate([v.reshape(dp_count, -1) for v in vectors], axis=1)
-    packed = lax.psum(packed, ("dp", "seq"))
-    mine = lax.dynamic_index_in_dim(packed, lax.axis_index("dp"), 0, keepdims=False)
-    parts, at = [], 0
-    for v in vectors:
-        size = v.shape[0] // dp_count
-        parts.append(mine[at : at + size])
-        at += size
-    return (
-        layer_out, tokens_grad, parts[0], parts[1], g_w_qkv, parts[2], parts[3], g_w_out, parts[4],
-        parts[5], parts[6], g_w_up, parts[7], g_w_down, parts[8],
+    layer_out, d_mid, d_att, d_att_t, delta, vec, vec_up, *sums = feed_forward(
+        fast, flat, attended, att_t, cotangent.reshape(rows, width), w_out, b_out, ln2_gain, ln2_shift,
+        b_up, b_down, w_up, w_down,
     )
+    tokens_grad, *found = attend_back(
+        fast, kn, vn, kt, xt, qn, qt, d_att, d_att_t, delta, lse, wp, cell_lengths, flat, d_mid, ln1_gain,
+        vec, vec_up, *(sums if fast else ()),
+    )
+    layer_out = layer_out.reshape(tokens.shape)
+    tokens_grad = tokens_grad.reshape(tokens.shape)
+    if fast:
+        down, up, out, qkv, *vectors = unpack(*found)
+    else:
+
+        def summed(g):
+            share = lax.psum_scatter(g, "dp", scatter_dimension=0, tiled=True)
+            return lax.psum(share, "seq").astype(F32)
+
+        g_down, g_up, g_out = sums
+        g_qkv, packed = found
+        g_down = jnp.moveaxis(g_down.reshape(CHUNKS, GROUPS, 128, width), 0, 1).reshape(ff, width)
+        g_up = jnp.transpose(g_up.reshape(CHUNKS, width, GROUPS, 128), (1, 2, 0, 3)).reshape(width, ff)
+        down, up, out, qkv = summed(g_down), summed(g_up), summed(g_out.reshape(width, width)), summed(g_qkv)
+        packed = packed.reshape(GROUPS, 16, 128)
+        vectors = [packed[:, r, : width // GROUPS].reshape(width) for r in range(8)]
+        vectors.append(packed[:, 8 : 8 + CHUNKS].reshape(ff))
+        together = jnp.concatenate([v.reshape(dp_count, -1) for v in vectors], axis=1)
+        together = lax.psum(together, ("dp", "seq"))
+        mine = lax.dynamic_index_in_dim(together, lax.axis_index("dp"), 0, keepdims=False)
+        sizes = [v.shape[0] // dp_count for v in vectors]
+        vectors = [mine[sum(sizes[:k]) : sum(sizes[: k + 1])] for k in range(len(sizes))]
+    g1, s1, bq, bv, bo, g2, s2, bd, bu = vectors
+    return layer_out, tokens_grad, g1, s1, qkv, bq, bv, out, bo, g2, s2, up, bu, down, bd
 
 
 def solution(mesh):

time: 484 us -> 241 us (0.50)
  waiting for transfers between devices: 227 us -> 0 us
  Pallas kernels: 124 us -> 238 us
  matrix products: 44.4 us -> 0 us
  blocking collectives: 44 us -> 0 us
  other arithmetic: 16 us -> 0 us
  between operations: 14.4 us -> 0.7 us
  local copies, waits for them, and re-layouts: 12.8 us -> 1.77 us
    reduce_scatter x5 -> x0, waiting for transfers between devices: 199 us -> none  [the longest x4 136 us: summed(): share = lax.psum_scatter(g, 'dp', scatter_dimension=0, tiled=True)]
    pallas_call x1 -> x3, Pallas kernels: 54.8 us -> 169 us  [the longest x1 130 us: attend_back(): pl.pallas_call(partial(attend_back_kernel, fast), out_shape=outs, in_spec...]
    dot_general x9 -> x0, matrix products: 44.4 us -> none  [mm(): return jnp.dot(a, b, preferred_element_type=F32)]
    psum x1 -> x0, blocking collectives: 44 us -> none  [local(): packed = lax.psum(packed, ('dp', 'seq'))]
    psum x1 -> x0, waiting for transfers between devices: 28.1 us -> none  [summed(): return lax.psum(share, 'seq').astype(F32)]
    reduce_sum x8 -> x0, other arithmetic: 7.26 us -> none  [the longest x2 2.3 us: normalize(): return centred * lax.rsqrt(variance + EPS) * gain + shift]
    convert_element_type x4 -> x0, other arithmetic: 5.95 us -> none  [summed(): return lax.psum(share, 'seq').astype(F32)]
    reshape x11 -> x0, local copies, waits for them, and re-layouts: 5.59 us -> none  [the longest x4 5.15 us: row(): return v.reshape(1, -1)]
  transfers between devices with their start and end apart: 6 -> 0, of which waited for: 5 -> 0; matrix products, arithmetic and copies ran while one was open for 8% -> 0% of each run, Pallas kernels for 11% -> 0%
where the time goes in v2:
time: 241 us
  Pallas kernels  238 us (99%)
    pallas_call x1, Pallas kernels, attend_back(): pl.pallas_call(partial(attend_back_kernel, fast), out_shape=outs, in_spec...  130 us
    pallas_call x1, Pallas kernels, gather_attend(): pl.pallas_call(gather_kernel, out_shape=outs, in_specs=[vmem, pl.BlockSpe...  69.3 us
    pallas_call x1, Pallas kernels, feed_forward(): pl.pallas_call(partial(feed_forward_kernel, fast), out_shape=outs, in_spe...  36 us

profile of v2, /device:TPU:0, one launch (start us, length us, event | category | flops | bytes accessed | tf_op | source)
XLA Modules:
  0.0 240.9 jit_solution(11655969397250358600)
XLA Ops:
  0.6 69.3 %gather_attend.1 = (bf16[4,6,512,128]{3,2,1,0:T(8,128)(2,1)}, bf16[4,6,512,128]{3,2,1,0:T(8,128)(2,1)}, bf16[4,6,128,512]{3,2,1,0:T(8,128)(2,1)}, bf16[4,768,512...) custom-call(bf16[512,768]{1,0:T(8,128)(2,1)} %bitcast.4, ...), custom_call_target="tpu_custom_call" | custom-call | tf_op jit(solution)/shard_map/gather_attend/pallas_call | solution.py:270
  70.0 36.0 %feed_forward.1 = (bf16[512,768]{1,0:T(8,128)(2,1)}, f32[512,768]{1,0:T(8,128)}, bf16[512,768]{1,0:T(8,128)(2,1)}, bf16[768,512]{1,0:T(8,128)(2,1)}, f32[16,512]...) custom-call(bf16[512,768]{1,0:T(8,128)(2,1)} %bitcast.5, ...), custom_call_target="tpu_custom_call" | custom-call | tf_op jit(solution)/shard_map/feed_forward/pallas_call | solution.py:612
  106.0 0.0 copy-start
  106.0 129.7 %attend_back.1 = (bf16[512,768]{1,0:T(8,128)(2,1)}, bf16[3,128,768]{2,1,0:T(8,128)(2,1)}, bf16[3,96,1024]{2,1,0:T(8,128)(2,1)}, bf16[96,768]{1,0:T(8,128)(2,1)},...) custom-call(bf16[4,6,512,128]{3,2,1,0:T(8,128)(2,1)} %get-tuple-element.59.refs_0_, ...), custom_call_target="tpu_custom_call" | custom-call | tf_op jit(solution)/shard_map/attend_back/pallas_call | solution.py:1082
  235.7 0.0 copy-start.1
  235.7 3.4 %unpack.1 = (f32[384,768]{1,0:T(8,128)}, f32[96,3072]{1,0:T(8,128)}, f32[96,768]{1,0:T(8,128)}, f32[96,2304]{1,0:T(8,128)}, f32[96]{0:T(128)}, /*index=5*/f32[96...) custom-call(bf16[3,128,768]{2,1,0:T(8,128)(2,1)} %get-tuple-element., ...), custom_call_target="tpu_custom_call" | custom-call | tf_op jit(solution)/shard_map/unpack/pallas_call | solution.py:1126
  239.1 0.0 copy-done
  239.1 0.9 copy.33
  240.0 0.0 copy-done.1
  240.0 0.9 copy.34
Async XLA Ops:
  106.0 133.2 %copy-start = (bf16[512,768]{1,0:T(8,128)(2,1)S(1)}, bf16[512,768]{1,0:T(8,128)(2,1)}, u32[]{:S(2)}) copy-start(bf16[512,768]{1,0:T(8,128)(2,1)} %get-tuple-element.58) | copy-start | bytes 2359300
  235.7 4.3 %copy-start.1 = (bf16[512,768]{1,0:T(8,128)(2,1)S(1)}, bf16[512,768]{1,0:T(8,128)(2,1)}, u32[]{:S(2)}) copy-start(bf16[512,768]{1,0:T(8,128)(2,1)} %get-tuple-element.78) | copy-start | bytes 2359300

commit v3 on v2

--- a/solution.py
+++ b/solution.py
@@ -87,14 +87,16 @@
 
 
 def gather_kernel(
-    tok, lens, gain, shift, w, bq, bv,
+    tok, lens, gain, shift, w_h, bq, bv,
     kn_o, vn_o, kt_o, xt_o, qn_o, qt_o, wp_o, att_f, att_o, lse_o,
-    xg, wp, kn, vn, kt, xt, qn, qt, qta, vta, acc, top, send, recv, out_sem,
+    xr, w, wp, kn, vn, kt, xt, qn, qt, qta, vta, acc, top, send, recv, in_sem, out_sem,
 ):
     rows, width = tok.shape
+    span = rows // 2
     seq = lax.axis_size("seq")
     me = lax.axis_index("seq")
     has_left, has_right = me > 0, me < seq - 1
+    at_end = (me == 0) | (me == seq - 1)
 
     barrier = pltpu.get_barrier_semaphore()
 
@@ -106,22 +108,26 @@
     def _():
         pl.semaphore_signal(barrier, inc=1, device_id={"seq": me + 1}, device_id_type=MESH)
 
-    xg[me] = normalize(tok[...].astype(F32), gain[...].reshape(1, -1), shift[...].reshape(1, -1)).astype(BF)
-
-    @pl.when(has_left & has_right)
+    own_tokens = pltpu.make_async_copy(tok, xr.at[me], in_sem.at[0])
+    own_tokens.start()
+    weights = pltpu.make_async_copy(w_h, w, in_sem.at[1])
+    weights.start()
+
+    @pl.when(at_end)
+    def _():
+        pl.semaphore_wait(barrier, 1)
+
+    @pl.when(~at_end)
     def _():
         pl.semaphore_wait(barrier, 2)
 
-    @pl.when(~(has_left & has_right))
-    def _():
-        pl.semaphore_wait(barrier, 1)
-
-    def copy(way, hop, block):
+    def copy(way, hop, half, block):
+        at = pl.ds(half * span, span)
         return pltpu.make_async_remote_copy(
-            src_ref=xg.at[block],
-            dst_ref=xg.at[block],
-            send_sem=send.at[way, hop],
-            recv_sem=recv.at[way, hop],
+            src_ref=tok.at[at] if hop == 0 else xr.at[block, at],
+            dst_ref=xr.at[block, at],
+            send_sem=send.at[way, hop, half],
+            recv_sem=recv.at[way, hop, half],
             device_id={"seq": me - 1 if way == 0 else me + 1},
             device_id_type=MESH,
         )
@@ -135,16 +141,28 @@
     def block_of(way, hop):
         return me + hop if way == 0 else me - hop
 
-    for way in range(2):
-        @pl.when(can_send(way))
-        def _():
-            copy(way, 0, me).start()
-
+    for half in range(2):
+        for way in range(2):
+            @pl.when(can_send(way))
+            def _():
+                copy(way, 0, half, me).start()
+
+    def normed(raw):
+        return normalize(raw.astype(F32), gain[...].reshape(1, -1), shift[...].reshape(1, -1)).astype(BF)
+
+    row16 = lax.broadcasted_iota(jnp.int32, (16, span), 0)
+    for h in range(HEADS):
+        vta[h, 64:] = jnp.where(row16 == 0, 1.0, 0.0).astype(BF)
+    acc[...] = jnp.zeros_like(acc)
+    top[...] = jnp.full_like(top, -3e38)
+    codes = query_codes(lens, me, rows).astype(BF)
+    low, high = lane_halves()
+    own_tokens.wait()
+    weights.wait()
     sort_weights(w, wp)
     keep_w = pltpu.make_async_copy(wp, wp_o, out_sem.at[0])
     keep_w.start()
-    codes = query_codes(lens, me, rows).astype(BF)
-    q = ((mm(xg[me], wp[0]) + bq[...].reshape(1, -1)).astype(BF).astype(F32) * (HEAD**-0.5)).astype(BF)
+    q = ((mm(normed(xr[me]), wp[0]) + bq[...].reshape(1, -1)).astype(BF).astype(F32) * (HEAD**-0.5)).astype(BF)
     for i in range(PAIRS):
         pair = q[:, 128 * i : 128 * (i + 1)]
         qn[i] = pair
@@ -158,15 +176,9 @@
     keep_q.start()
     keep_qt = pltpu.make_async_copy(qt, qt_o, out_sem.at[2])
     keep_qt.start()
-    row16 = lax.broadcasted_iota(jnp.int32, (16, rows), 0)
-    for h in range(HEADS):
-        vta[h, 64:] = jnp.where(row16 == 0, 1.0, 0.0).astype(BF)
-    acc[...] = jnp.zeros_like(acc)
-    top[...] = jnp.full_like(top, -3e38)
-    low, high = lane_halves()
-    at_end = (me == 0) | (me == seq - 1)
-
-    def keeps(block, step):
+
+    def keeps(step):
+        block = block_at(step)
         return [
             pltpu.make_async_copy(kn.at[block], kn_o.at[block], out_sem.at[3 + 4 * step]),
             pltpu.make_async_copy(vn.at[block], vn_o.at[block], out_sem.at[4 + 4 * step]),
@@ -179,38 +191,39 @@
         from_mid = jnp.where(step == 0, me, jnp.where(step == 1, me + 1, jnp.where(step == 2, me - 1, jnp.where(me == 1, seq - 1, 0))))
         return jnp.where(at_end, from_end, from_mid)
 
-    def one_step(step, carry):
+    def half_step(turn, carry):
+        step, half = turn // 2, turn % 2
         for hop in range(1, 4):
-            due = step == jnp.where(at_end, hop, 2 * hop - 1)
-            for way in range(2):
-                @pl.when(due & holds(way, hop))
-                def _():
-                    copy(way, hop - 1, block_of(way, hop)).wait_recv()
-
-                    @pl.when(can_send(way))
+            for part in range(2):
+                due = turn == jnp.where(at_end, 2 * hop + part, 4 * hop - 2 + part)
+                for way in range(2):
+                    @pl.when(due & holds(way, hop))
                     def _():
-                        copy(way, hop, block_of(way, hop)).start()
+                        copy(way, hop - 1, part, block_of(way, hop)).wait_recv()
+
+                        @pl.when(can_send(way))
+                        def _():
+                            copy(way, hop, part, block_of(way, hop)).start()
 
         block = block_at(step)
-        x = xg[block]
+        at = pl.ds(pl.multiple_of(half * span, span), span)
+        x = normed(xr[block, at])
         keys = mm(x, wp[1]).astype(BF)
         values = (mm(x, wp[2]) + bv[...].reshape(1, -1)).astype(BF)
-        hot = key_codes(lens, block, rows)
+        hot = key_codes(lens, 2 * block + half, span)
         hot_low, hot_high = hot * low, hot * high
-        xt[block] = x.T
+        xt[block, :, at] = x.T
         for i in range(PAIRS):
-            at = slice(128 * i, 128 * (i + 1))
-            kn[block, i] = keys[:, at]
-            kt[block, i] = keys[:, at].T
-            vn[block, i] = values[:, at]
-            turned = values[:, at].T
+            cut = slice(128 * i, 128 * (i + 1))
+            kn[block, i, at] = keys[:, cut]
+            kt[block, i, :, at] = keys[:, cut].T
+            vn[block, i, at] = values[:, cut]
+            turned = values[:, cut].T
             vta[2 * i, :64] = turned[:64]
             vta[2 * i + 1, :64] = turned[64:]
-        for c in keeps(block, step):
-            c.start()
 
         def one_pair(i, carry):
-            pair = kn[block, i]
+            pair = kn[block, i, at]
             scores = [
                 mm(pair * low + hot_high, qta[2 * i]),
                 mm(pair * high + hot_low, qta[2 * i + 1]),
@@ -225,9 +238,15 @@
             return carry
 
         lax.fori_loop(0, PAIRS, one_pair, 0)
+        for s in range(4):
+            @pl.when(turn == 2 * s + 1)
+            def _():
+                for c in keeps(s):
+                    c.start()
+
         return carry
 
-    lax.fori_loop(0, seq, one_step, 0)
+    lax.fori_loop(0, 2 * seq, half_step, 0)
 
     lse_o[...] = jnp.zeros_like(lse_o)
     for h in range(HEADS):
@@ -238,15 +257,16 @@
 
     for way in range(2):
         for hop in range(3):
-            @pl.when(can_send(way) & holds(way, hop))
-            def _():
-                copy(way, hop, block_of(way, hop)).wait_send()
+            for half in range(2):
+                @pl.when(can_send(way) & holds(way, hop))
+                def _():
+                    copy(way, hop, half, block_of(way, hop)).wait_send()
 
     keep_w.wait()
     keep_q.wait()
     keep_qt.wait()
     for step in range(4):
-        for c in keeps(block_at(step), step):
+        for c in keeps(step):
             c.wait()
 
 
@@ -270,10 +290,11 @@
     return pl.pallas_call(
         gather_kernel,
         out_shape=outs,
-        in_specs=[vmem, pl.BlockSpec(memory_space=pltpu.SMEM)] + [vmem] * 5,
+        in_specs=[any_spec, pl.BlockSpec(memory_space=pltpu.SMEM), vmem, vmem, any_spec, vmem, vmem],
         out_specs=[any_spec] * 7 + [vmem] * 3,
         scratch_shapes=[
             pltpu.VMEM((seq, rows, width), BF),
+            pltpu.VMEM((width, 3 * width), BF),
             pltpu.VMEM((3, width, width), BF),
             pltpu.VMEM((seq, PAIRS, rows, 128), BF),
             pltpu.VMEM((seq, PAIRS, rows, 128), BF),
@@ -282,15 +303,16 @@
             pltpu.VMEM((PAIRS, rows, 128), BF),
             pltpu.VMEM((PAIRS, 128, rows), BF),
             pltpu.VMEM((HEADS, 128, rows), BF),
-            pltpu.VMEM((HEADS, 80, rows), BF),
+            pltpu.VMEM((HEADS, 80, rows // 2), BF),
             pltpu.VMEM((HEADS, 80, rows), F32),
             pltpu.VMEM((HEADS, 1, rows), F32),
-            pltpu.SemaphoreType.DMA((2, 4)),
-            pltpu.SemaphoreType.DMA((2, 4)),
+            pltpu.SemaphoreType.DMA((2, 4, 2)),
+            pltpu.SemaphoreType.DMA((2, 4, 2)),
+            pltpu.SemaphoreType.DMA((2,)),
             pltpu.SemaphoreType.DMA((20,)),
         ],
         compiler_params=pltpu.CompilerParams(
-            collective_id=0, has_side_effects=True, vmem_limit_bytes=56 * MIB
+            collective_id=0, has_side_effects=True, vmem_limit_bytes=58 * MIB
         ),
         name="gather_attend",
     )(tokens, lens, gain, shift, w, bq, bv)
@@ -450,6 +472,9 @@
             DpSum("y", stage_u.at[c], one_u.at[c], two_u, three_u, send.at[3 + c], recv.at[3 + c]) for c in range(CHUNKS)
         ]
         sum_o = DpSum("x", stage_o, one_o, None, None, send.at[6], recv.at[6])
+        kept = [(one_d.at[1], gd_o.at[0]), (one_u.at[1], gu_o.at[0]), (one_d.at[2], gd_o.at[1]), (one_u.at[2], gu_o.at[1])]
+        kept += [(one_o, go_o), (three_d, d3_o), (three_u, u3_o)]
+        keep = [pltpu.make_async_copy(src, dst, out_sem.at[k]) for k, (src, dst) in enumerate(kept)]
 
     def per_row(ref):
         return ref[...].reshape(1, -1)
@@ -486,11 +511,10 @@
                 unit_sum.finish(0)
                 unit_sum.start(1)
         if fast and c == 2:
-            for unit_sum in (sums_d[0], sums_u[0]):
-                unit_sum.finish(1)
-                unit_sum.start(2)
             for unit_sum in (sums_d[1], sums_u[1]):
                 unit_sum.finish(0)
+            for copy in keep[:2]:
+                copy.start()
         total = total + mm(hidden, wd[c])
         d_normed = d_normed + mm_nt(d_upper, wu[c])
         g_down = mm(hidden.T, d_out).astype(BF)
@@ -502,6 +526,10 @@
         if fast:
             sums_d[c].start(0)
             sums_u[c].start(0)
+        if fast and c == 2:
+            for unit_sum in (sums_d[0], sums_u[0]):
+                unit_sum.finish(1)
+                unit_sum.start(2)
     layer_o[...] = total.astype(BF)
     vec_o[3:4] = jnp.sum(d_out.astype(F32), axis=0, keepdims=True)
     vec_o[1:2] = jnp.sum(d_normed * unit, axis=0, keepdims=True)
@@ -522,6 +550,8 @@
         sum_o.start(0)
         for unit_sum in (sums_d[2], sums_u[2]):
             unit_sum.finish(0)
+        for copy in keep[2:4]:
+            copy.start()
     d_att = mm_nt(d_branch, w_out[...]).astype(BF)
     d_att_o[...] = d_att
     d_att_t = d_att.T
@@ -531,20 +561,11 @@
     for h in range(HEADS):
         delta_o[h : h + 1] = jnp.sum(product[64 * h : 64 * (h + 1)], axis=0, keepdims=True)
     if fast:
-        keep = [
-            pltpu.make_async_copy(one_d.at[pl.ds(1, 2)], gd_o, out_sem.at[0]),
-            pltpu.make_async_copy(one_u.at[pl.ds(1, 2)], gu_o, out_sem.at[1]),
-        ]
-        for copy in keep:
-            copy.start()
         sum_o.finish(0)
-        keep.append(pltpu.make_async_copy(one_o, go_o, out_sem.at[2]))
-        keep[-1].start()
+        keep[4].start()
         for unit_sum in (sums_d[0], sums_u[0]):
             unit_sum.finish(2)
-        keep.append(pltpu.make_async_copy(three_d, d3_o, out_sem.at[3]))
-        keep.append(pltpu.make_async_copy(three_u, u3_o, out_sem.at[4]))
-        for copy in keep[3:]:
+        for copy in keep[5:]:
             copy.start()
         for c in range(CHUNKS):
             phases = (0, 1, 2) if c == 0 else (0,)
@@ -605,7 +626,7 @@
             sds((CHUNKS, *cube, 128, width), BF), sds((CHUNKS, *cube, part_w, span), BF), sds((*cube, part_o, width), BF),
         ]
     out_specs += [any_spec] * (len(outs) - 7)
-    scratch += [pltpu.SemaphoreType.DMA((2, CHUNKS, GROUPS)), pltpu.SemaphoreType.DMA((5,))]
+    scratch += [pltpu.SemaphoreType.DMA((2, CHUNKS, GROUPS)), pltpu.SemaphoreType.DMA((7,))]
     params = dict(vmem_limit_bytes=58 * MIB)
     if fast:
         params.update(collective_id=1, has_side_effects=True)
@@ -633,7 +654,7 @@
     else:
         gw_o, stage_v_o, *refs = refs
     (
-        kn, vn, kt, xt, qta, dta, dqt, gk, gv, dk, dv, wp, tok, d_mid, dx_own, dxs, rx, stage_q, stage_v, sums,
+        kn, vn, kt, xt, qta, dta, dqt, gk, gv, dk, dv, dq, wp, tok, d_mid, dx_own, dxs, rx, stage_q, stage_v, sums,
         in_sem, load_sem, out_sem, dsend, drecv, *refs,
     ) = refs
     rows, width = d_att.shape
@@ -672,9 +693,6 @@
             pltpu.make_async_copy(kt_h.at[block], kt.at[slot], in_sem.at[slot, 2]),
             pltpu.make_async_copy(xt_h.at[block], xt.at[slot], in_sem.at[slot, 3]),
         ]
-
-    def halves(j):
-        return (slice(0, 64), slice(64, 128)) if j == 0 else (slice(64, 128), slice(0, 64))
 
     fills = []
     for h in range(HEADS):
@@ -690,8 +708,6 @@
         pltpu.make_async_copy(tok_h, tok, load_sem.at[25]),
         pltpu.make_async_copy(d_mid_h, d_mid, load_sem.at[26]),
     ]
-    for copy in late:
-        copy.start()
     if fast:
         (
             one_d, one_u, one_o, two_d, two_u, two_o, three_d, three_u, three_o,
@@ -708,7 +724,7 @@
             pltpu.make_async_copy(one_u_h.at[1], one_u.at[1], load_sem.at[32]),
             pltpu.make_async_copy(one_o_h, one_o, load_sem.at[33]),
         ]
-        for copy in early:
+        for copy in early[:4]:
             copy.start()
         rs_d = [DpSum("x", None, one_d.at[c], two_d.at[c], three_d.at[c + 1], psend.at[c], precv.at[c]) for c in range(2)]
         rs_u = [
@@ -716,11 +732,17 @@
             for c in range(2)
         ]
         rs_o = DpSum("x", None, one_o, two_o, three_o, psend.at[4], precv.at[4])
-        rs_q = [
-            DpSum("xy"[c], stage_q.at[c], one_q.at[c], two_q.at[c], three_q.at[c], psend.at[5 + c], precv.at[5 + c])
-            for c in range(2)
-        ]
-        rs_v = DpSum("x", stage_v, one_v, two_v, three_v, psend.at[7], precv.at[7])
+
+        def rs_q(tile, first):
+            return DpSum(
+                first, stage_q.at[tile], one_q.at[tile], two_q.at[tile], three_q.at[tile],
+                psend.at[6 + tile], precv.at[6 + tile],
+            )
+
+        def couple(c):
+            return rs_q(2 * c, "x"), rs_q(2 * c + 1, "y")
+
+        rs_v = DpSum("x", stage_v, one_v, two_v, three_v, psend.at[5], precv.at[5])
         ar_d = [
             SeqSum(three_d.at[c], za_d.at[c], zx_d.at[c], fin_d.at[c], zsend.at[c], zrecv.at[c]) for c in range(3)
         ]
@@ -729,26 +751,33 @@
         ]
         ar_o = SeqSum(three_o, za_o, zx_o, fin_o, zsend.at[6], zrecv.at[6])
         ar_q = [
-            SeqSum(three_q.at[c], za_q.at[c], zx_q.at[c], fin_q.at[c], zsend.at[7 + c], zrecv.at[7 + c]) for c in range(2)
-        ]
-        ar_v = SeqSum(three_v, za_v, zx_v, fin_v, zsend.at[9], zrecv.at[9])
-
+            SeqSum(three_q.at[c], za_q.at[c], zx_q.at[c], fin_q.at[c], zsend.at[8 + c], zrecv.at[8 + c])
+            for c in range(PAIRS)
+        ]
+        ar_ff = (ar_d[1], ar_u[1], ar_d[2], ar_u[2], ar_o)
+        ar_v = SeqSum(three_v, za_v, zx_v, fin_v, zsend.at[7], zrecv.at[7])
+
+    late[0].start()
+    if fast:
+        for copy in early[4:]:
+            copy.start()
     low, high = lane_halves()
-    codes = query_codes(lens, me, rows)
-    row64 = lax.broadcasted_iota(jnp.int32, (64, rows), 0)
+    codes = query_codes(lens, me, rows)[:16]
+    row16 = lax.broadcasted_iota(jnp.int32, (16, rows), 0)
+    blank = jnp.zeros((48, rows), BF)
     for h in range(HEADS):
-        _, other = halves(h % 2)
+        first = 64 * (1 - h % 2)
         extra = codes
         for r, part in enumerate(three_parts(-lse[h : h + 1])):
-            extra = jnp.where(row64 == 8 + r, part, extra)
-        qta[h, other] = extra.astype(BF)
-        extra = jnp.zeros((64, rows), F32)
+            extra = jnp.where(row16 == 8 + r, part, extra)
+        qta[h, first : first + 16] = extra.astype(BF)
+        qta[h, first + 16 : first + 64] = blank
+        extra = jnp.zeros((16, rows), F32)
         for r, part in enumerate(three_parts(-delta[h : h + 1])):
-            extra = jnp.where(row64 == r, part, extra)
-        dta[h, other] = extra.astype(BF)
+            extra = jnp.where(row16 == r, part, extra)
+        dta[h, first : first + 16] = extra.astype(BF)
+        dta[h, first + 16 : first + 64] = blank
     dqt[...] = jnp.zeros_like(dqt)
-    gk[...] = jnp.zeros_like(gk)
-    gv[...] = jnp.zeros_like(gv)
     stage_v[...] = jnp.zeros_like(stage_v)
     sums[...] = jnp.zeros_like(sums)
     lane = lax.broadcasted_iota(jnp.int32, (1, 128), 1)
@@ -765,22 +794,48 @@
     def _():
         pl.semaphore_wait(barrier, greeted + 2)
 
-    def dx_copy(way, block):
+    def dx_copy(way, block, half):
+        at = pl.ds(half * (rows // 2), rows // 2)
         return pltpu.make_async_remote_copy(
-            src_ref=dxs.at[block], dst_ref=rx.at[block + way],
-            send_sem=dsend.at[way, block], recv_sem=drecv.at[way, block],
+            src_ref=dxs.at[block, at], dst_ref=rx.at[block + way, at],
+            send_sem=dsend.at[way, block, half], recv_sem=drecv.at[way, block, half],
             device_id={"seq": me - 1 if way == 0 else me + 1}, device_id_type=MESH,
         )
 
-    def relay(way, block):
-        dx_copy(way, block).wait_recv()
-        dxs[block] = dxs[block] + rx[block + way]
-        dx_copy(way, block).start()
-
-    def relay_at(place, way, step):
+    def relay_at(place, way, step, half):
         @pl.when(me == place)
         def _():
-            relay(way, block_at(step))
+            block = block_at(step)
+            at = pl.ds(half * (rows // 2), rows // 2)
+            dx_copy(way, block, half).wait_recv()
+            dxs[block, at] = dxs[block, at] + rx[block + way, at]
+            dx_copy(way, block, half).start()
+
+    def relay_far(step, half):
+        relay_at(1, 1, step, half)
+        relay_at(2, 0, step, half)
+
+    def relay_near(half):
+        relay_at(1, 0, 2, half)
+        relay_at(2, 1, 2, half)
+
+    def send_dx(block, half):
+        @pl.when(me == 0)
+        def _():
+            dx_copy(1, block, half).start()
+
+        @pl.when(me == seq - 1)
+        def _():
+            dx_copy(0, block, half).start()
+
+    def turn(*sums):
+        for unit_sum in sums:
+            unit_sum.finish(1)
+            unit_sum.start(2)
+
+    def close(*sums):
+        for unit_sum in sums:
+            unit_sum.finish(2)
 
     def hooks(g):
         if not fast:
@@ -804,143 +859,208 @@
                 copy.wait()
             rs_d[1].start(1)
             rs_u[1].start(1)
-
-        def turn(*sums):
-            for unit_sum in sums:
-                unit_sum.finish(1)
-                unit_sum.start(2)
-
-        def close(*sums):
-            for unit_sum in sums:
-                unit_sum.finish(2)
+            rs_o.start(1)
 
         at(0, chunk0_out)
-        at(2, chunk2_out)
-        at(4, lambda: (ar_d[0].middles_swap(), ar_u[0].middles_swap()))
-        at(5, lambda: turn(rs_d[0], rs_u[0]))
-        at(7, lambda: rs_o.start(1))
-        at(8, lambda: (ar_d[0].middles_send(), ar_u[0].middles_send()))
-        at(9, lambda: close(rs_d[0], rs_u[0]))
-        at(11, lambda: turn(rs_d[1], rs_u[1]))
-        at(14, lambda: close(rs_d[1], rs_u[1]))
-        at(15, lambda: (relay_at(1, 1, 0), relay_at(2, 0, 0)))
-        at(16, lambda: turn(rs_o))
-        at(19, lambda: close(rs_o))
+        at(12, lambda: (turn(rs_d[0], rs_u[0]), chunk2_out(), ar_d[0].middles_swap(), ar_u[0].middles_swap()))
+        at(16, lambda: relay_far(0, 0))
+        at(17, lambda: (close(rs_d[0], rs_u[0]), ar_d[1].ends_send(), ar_u[1].ends_send()))
+        at(18, lambda: (ar_d[0].middles_send(), ar_u[0].middles_send()))
+        at(21, lambda: relay_far(0, 1))
+        at(22, lambda: turn(rs_d[1], rs_u[1]))
+
+    def products(slot, i, hot_low, hot_high, part=slice(None)):
+        at = pl.ds(pl.multiple_of(i * 128, 128), 128)
+        keys, values = kn[slot, i, part], vn[slot, i, part]
+        q_pair, d_pair = qn[i], d_att[:, at]
+        scores = [
+            mm(keys * low + hot_high[part], qta[2 * i]),
+            mm(keys * high + hot_low[part], qta[2 * i + 1]),
+        ]
+        slopes = [
+            mm(values * low + v_high, dta[2 * i]),
+            mm(values * high + v_low, dta[2 * i + 1]),
+        ]
+        d_keys = jnp.zeros((keys.shape[0], 128), F32)
+        d_values = jnp.zeros((keys.shape[0], 128), F32)
+        for j in range(2):
+            h = 2 * i + j
+            mask = low if j == 0 else high
+            probs = jnp.exp(scores[j])
+            d_scores = (probs * slopes[j]).astype(BF)
+            d_values = d_values + mm(probs.astype(BF), d_pair * mask)
+            d_keys = d_keys + mm(d_scores, q_pair * mask)
+            dqt[h] += mm(kt[slot, i, 64 * j : 64 * (j + 1), part], d_scores)
+        dk[part, at] = d_keys.astype(BF)
+        dv[part, at] = d_values.astype(BF)
+
+    def enter(step):
+        for copy in loads(step):
+            copy.wait()
+        hot = key_codes(lens, block_at(step), rows)
+        return hot * low, hot * high
+
+    hots = enter(0)
+    for copy in loads(1):
+        copy.start()
+    for half in range(2):
+        part = slice(half * (rows // 2), (half + 1) * (rows // 2))
+
+        def one_pair(i, carry):
+            hooks(half * PAIRS + i)
+            products(0, i, *hots, part)
+            return carry
+
+        lax.fori_loop(0, PAIRS, one_pair, 0)
+        if half == 0:
+            late[0].wait()
+        block = block_at(0)
+        dxs[block, part] = (mm_nt(dk[part], wp[1]) + mm_nt(dv[part], wp[2])).astype(BF)
+        send_dx(block, half)
+    gk[...] = mm(xt[0], dk[...])
+    gv[...] = mm(xt[0], dv[...])
+    sums[3:4] = jnp.sum(dv[...].astype(F32), axis=0, keepdims=True)
+    late[1].start()
+    late[2].start()
 
     def one_step(step, carry):
         slot = step % 2
-        for copy in loads(step):
-            copy.wait()
-
-        @pl.when(step < seq - 1)
+        hots = enter(step)
+        for copy in loads(step + 1):
+            copy.start()
+        block = block_at(step)
+
+        def one_pair(i, carry):
+            hooks((step + 1) * PAIRS + i)
+            products(slot, i, *hots)
+            return carry
+
+        lax.fori_loop(0, PAIRS, one_pair, 0)
+        dxs[block] = (mm_nt(dk[...], wp[1]) + mm_nt(dv[...], wp[2])).astype(BF)
+
+        @pl.when((step == 1) | (not fast))
         def _():
-            for copy in loads(step + 1):
-                copy.start()
-
-        block = block_at(step)
-        hot = key_codes(lens, block, rows)
-        hot_low, hot_high = hot * low, hot * high
-
-        def one_pair(i, carry):
-            hooks(step * PAIRS + i)
-            at = pl.ds(pl.multiple_of(i * 128, 128), 128)
-            keys, values = kn[slot, i], vn[slot, i]
-            q_pair, d_pair = qn[i], d_att[:, at]
-            scores = [
-                mm(keys * low + hot_high, qta[2 * i]),
-                mm(keys * high + hot_low, qta[2 * i + 1]),
-            ]
-            slopes = [
-                mm(values * low + v_high, dta[2 * i]),
-                mm(values * high + v_low, dta[2 * i + 1]),
-            ]
-            d_keys = jnp.zeros((rows, 128), F32)
-            d_values = jnp.zeros((rows, 128), F32)
-            for j in range(2):
-                h = 2 * i + j
-                half = low if j == 0 else high
-                probs = jnp.exp(scores[j])
-                d_scores = (probs * slopes[j]).astype(BF)
-                d_values = d_values + mm(probs.astype(BF), d_pair * half)
-                d_keys = d_keys + mm(d_scores, q_pair * half)
-                dqt[h] += mm(kt[slot, i, 64 * j : 64 * (j + 1)], d_scores)
-            dk[:, at] = d_keys.astype(BF)
-            dv[:, at] = d_values.astype(BF)
-            return carry
-
-        lax.fori_loop(0, PAIRS, one_pair, 0)
-
-        @pl.when(step == 0)
-        def _():
-            late[0].wait()
-
-        dx = mm_nt(dk[...], wp[1]) + mm_nt(dv[...], wp[2])
-
-        @pl.when(step < seq - 1)
-        def _():
-            dxs[block] = dx.astype(BF)
-
-            @pl.when(me == 0)
-            def _():
-                dx_copy(1, block).start()
-
-            @pl.when(me == seq - 1)
-            def _():
-                dx_copy(0, block).start()
-
-        @pl.when(step == seq - 1)
-        def _():
-            dx_own[...] = dx
+            send_dx(block, 0)
+            send_dx(block, 1)
 
         gk[...] += mm(xt[slot], dk[...])
         gv[...] += mm(xt[slot], dv[...])
         sums[3:4] += jnp.sum(dv[...].astype(F32), axis=0, keepdims=True)
         return carry
 
-    lax.fori_loop(0, seq, one_step, 0)
+    lax.fori_loop(1, seq - 1, one_step, 0)
+
     last = (seq - 1) % 2
-    dq = ((dqt[...] * (HEAD**-0.5)).reshape(width, rows).T).astype(BF)
-    dx_own[...] += mm_nt(dq, wp[0])
-    sums[2:3] = jnp.sum(dq.astype(F32), axis=0, keepdims=True)
-    gq = mm(xt[last], dq)
+    hots = enter(seq - 1)
     lane_w = lax.broadcasted_iota(jnp.int32, (width, 128), 1)
     lo = lane_w < 64
-    for i in range(PAIRS):
-        at = slice(128 * i, 128 * (i + 1))
-        k_turned = pltpu.roll(gk[:, at], 64, 1)
-        tiles = (
-            jnp.where(lo, gq[:, at], k_turned), jnp.where(lo, gv[:, at], gq[:, at]), jnp.where(lo, k_turned, gv[:, at])
-        )
-        for j, tile in enumerate(tiles):
-            tile = tile.astype(BF)
-            place = 3 * i + j
-            if not fast:
-                gw_o[:, 128 * place : 128 * (place + 1)] = tile
-                continue
-            to = slice(128 * (place % 9), 128 * (place % 9 + 1))
-            for d in range(GROUPS):
-                stage_q[place // 9, d // 4, (d // 2) % 2, d % 2, :, to] = tile[part_w * d : part_w * (d + 1)]
-        if fast and i == 2:
-            rs_q[0].start(0)
-    if fast:
-        rs_q[1].start(0)
-        for unit in (ar_d[1], ar_u[1], ar_d[2], ar_u[2], ar_o):
-            unit.ends_send()
-    relay_at(1, 1, 1)
-    relay_at(2, 0, 1)
-    relay_at(1, 0, 2)
-    relay_at(2, 1, 2)
-    if fast:
-        for unit in rs_q:
+
+    def one_couple(c, carry):
+        if fast:
+
+            @pl.when(c == 0)
+            def _():
+                turn(rs_o)
+                ar_ff[0].middles_swap()
+                ar_ff[1].middles_swap()
+
+            @pl.when(c == 1)
+            def _():
+                close(rs_d[1], rs_u[1], rs_o)
+                for unit in ar_ff[2:]:
+                    unit.ends_send()
+                for half in range(2):
+                    send_dx(block_at(2), half)
+                    relay_near(half)
+
+            @pl.when(c >= 1)
+            def _():
+                for unit in couple(c - 1):
+                    unit.finish(0)
+                    unit.start(1)
+
+            @pl.when(c >= 2)
+            def _():
+                for unit in couple(c - 2):
+                    unit.finish(1)
+                    unit.start(2)
+                ar_ff[0].middles_send()
+
+        products(last, 2 * c, *hots)
+        if fast:
+
+            @pl.when(c == 1)
+            def _():
+                relay_far(1, 0)
+
+            @pl.when(c == 2)
+            def _():
+                ar_ff[1].middles_send()
+                relay_far(1, 1)
+
+        products(last, 2 * c + 1, *hots)
+        at = pl.ds(pl.multiple_of(c * 256, 256), 256)
+        turned = dqt[pl.ds(4 * c, 4)].reshape(256, rows) * (HEAD**-0.5)
+        dq_part = turned.T.astype(BF)
+        dq[:, at] = dq_part
+        x_t = xt[last]
+        gq_part = mm(x_t, dq_part)
+        gk_part = gk[:, at] + mm(x_t, dk[:, at])
+        gv_part = gv[:, at] + mm(x_t, dv[:, at])
+        for k in range(2):
+            cut = slice(128 * k, 128 * (k + 1))
+            q_tile, v_tile = gq_part[:, cut], gv_part[:, cut]
+            k_tile = pltpu.roll(gk_part[:, cut], 64, 1)
+            tiles = jnp.where(lo, q_tile, k_tile), jnp.where(lo, v_tile, q_tile), jnp.where(lo, k_tile, v_tile)
+            for j, tile in enumerate(tiles):
+                tile = tile.astype(BF)
+                for d in range(GROUPS):
+                    piece = tile[part_w * d : part_w * (d + 1)]
+                    stage_q[2 * c + k, d // 4, (d // 2) % 2, d % 2, :, 128 * j : 128 * (j + 1)] = piece
+        if fast:
+            for unit in couple(c):
+                unit.start(0)
+        return carry
+
+    lax.fori_loop(0, PAIRS // 2, one_couple, 0)
+    if not fast:
+        relay_far(0, 0)
+        relay_far(0, 1)
+        relay_far(1, 0)
+        relay_far(1, 1)
+        relay_near(0)
+        relay_near(1)
+    dx_own[...] = mm_nt(dk[...], wp[1]) + mm_nt(dv[...], wp[2]) + mm_nt(dq[...], wp[0])
+    sums[3:4] += jnp.sum(dv[...].astype(F32), axis=0, keepdims=True)
+    sums[2:3] = jnp.sum(dq[...].astype(F32), axis=0, keepdims=True)
+    if fast:
+        for unit in couple(2):
             unit.finish(0)
             unit.start(1)
+        for unit in couple(1):
+            unit.finish(1)
+            unit.start(2)
+        for unit in couple(0):
+            unit.finish(2)
+        for unit in couple(2):
+            unit.finish(1)
+            unit.start(2)
+        for unit in (*couple(1), *couple(2)):
+            unit.finish(2)
+        for unit in ar_q:
+            unit.ends_send()
+        for unit in ar_ff[2:]:
+            unit.middles_swap()
+        ar_ff[2].middles_send()
+        ar_ff[3].middles_send()
 
     late[1].wait()
     late[2].wait()
     for way, there in ((0, has_right), (1, has_left)):
         @pl.when(there)
         def _():
-            dx_copy(way, me).wait_recv()
+            for half in range(2):
+                dx_copy(way, me, half).wait_recv()
             dx_own[...] += rx[me + way].astype(F32)
 
     values = tok[...].astype(F32)
@@ -951,6 +1071,30 @@
     sums[0:1] = jnp.sum(d_normed * unit_rows, axis=0, keepdims=True)
     sums[1:2] = jnp.sum(d_normed, axis=0, keepdims=True)
     sums[4:8] = vec[0:4]
+    rows8 = sums[...]
+    for d in range(GROUPS):
+        y, x, core = d // 4, (d // 2) % 2, d % 2
+        stage_v[y, x, core, 0:8, 0:part_w] = rows8[:, part_w * d : part_w * (d + 1)]
+        stage_v[y, x, core, 8 : 8 + CHUNKS] = vec_up[0:CHUNKS, 128 * d : 128 * (d + 1)]
+    if fast:
+        rs_v.start(0)
+    if fast:
+        ar_ff[4].middles_send()
+        ar_q[0].middles_swap()
+        rs_v.finish(0)
+        rs_v.start(1)
+        ar_q[1].middles_swap()
+        ar_q[0].middles_send()
+        rs_v.finish(1)
+        rs_v.start(2)
+        ar_q[2].middles_swap()
+        ar_q[1].middles_send()
+        rs_v.finish(2)
+        ar_v.ends_send()
+        ar_q[3].middles_swap()
+        ar_q[2].middles_send()
+        ar_q[4].middles_swap()
+        ar_q[3].middles_send()
     scaled = d_normed * gain[...].reshape(1, -1)
     tok_o[...] = (
         d_mid[...]
@@ -961,36 +1105,12 @@
             - unit_rows * jnp.mean(scaled * unit_rows, axis=-1, keepdims=True)
         )
     ).astype(BF)
-    rows8 = sums[...]
-    for d in range(GROUPS):
-        y, x, core = d // 4, (d // 2) % 2, d % 2
-        stage_v[y, x, core, 0:8, 0:part_w] = rows8[:, part_w * d : part_w * (d + 1)]
-        stage_v[y, x, core, 8 : 8 + CHUNKS] = vec_up[0:CHUNKS, 128 * d : 128 * (d + 1)]
-    if fast:
-        rs_v.start(0)
-        for unit in (ar_d[1], ar_u[1], ar_d[2], ar_u[2], ar_o):
-            unit.middles_swap()
-        rs_v.finish(0)
-        rs_v.start(1)
-        for unit in rs_q:
-            unit.finish(1)
-            unit.start(2)
-        rs_v.finish(1)
-        rs_v.start(2)
-        for unit in (ar_d[1], ar_u[1], ar_d[2], ar_u[2], ar_o):
-            unit.middles_send()
-        rs_v.finish(2)
-        ar_v.ends_send()
-        for unit in rs_q:
-            unit.finish(2)
-        for unit in ar_q:
-            unit.ends_send()
+    if fast:
+        ar_q[5].middles_swap()
         ar_v.middles_swap()
-        for unit in ar_q:
-            unit.middles_swap()
+        ar_q[4].middles_send()
+        ar_q[5].middles_send()
         ar_v.middles_send()
-        for unit in ar_q:
-            unit.middles_send()
         for unit in (*ar_d, *ar_u, ar_o, ar_v, *ar_q):
             unit.finish()
         keep = [
@@ -1003,18 +1123,20 @@
             copy.start()
         for unit in (*rs_d, *rs_u, rs_o):
             unit.wait_sends((1, 2))
-        for unit in (*rs_q, rs_v):
+        for unit in (*couple(0), *couple(1), *couple(2), rs_v):
             unit.wait_sends((0, 1, 2))
         for copy in keep:
             copy.wait()
     else:
         stage_v_o[...] = stage_v[...]
+        gw_o[...] = stage_q[...]
 
     for place, first, second in ((0, 1, 1), (1, 1, 0), (2, 0, 1), (3, 0, 0)):
         @pl.when(me == place)
         def _():
             for step, way in enumerate((first, first, second)):
-                dx_copy(way, block_at(step)).wait_send()
+                for half in range(2):
+                    dx_copy(way, block_at(step), half).wait_send()
 
 
 def attend_back(fast, kn, vn, kt, xt, qn, qt, d_att, d_att_t, delta, lse, wp, lens, tokens, d_mid, gain, vec, vec_up, *ready):
@@ -1022,7 +1144,6 @@
     width = wp.shape[1]
     span = GROUPS * 128
     part = width // GROUPS
-    half = 3 * width // 2
     any_spec = pl.BlockSpec(memory_space=pl.ANY)
     vmem = pl.BlockSpec(memory_space=pltpu.VMEM)
     sds = jax.ShapeDtypeStruct
@@ -1032,11 +1153,11 @@
     if fast:
         outs += [
             sds((CHUNKS, 128, width), BF), sds((CHUNKS, part, span), BF), sds((part, width), BF),
-            sds((2, part, half), BF), sds((16, 128), F32),
+            sds((PAIRS, part, 384), BF), sds((16, 128), F32),
         ]
         out_specs += [any_spec] * 5
     else:
-        outs += [sds((width, 3 * width), BF), sds((*cube, 16, 128), F32)]
+        outs += [sds((PAIRS, *cube, part, 384), BF), sds((*cube, 16, 128), F32)]
         out_specs += [vmem] * 2
     scratch = [
         pltpu.VMEM((2, PAIRS, rows, 128), BF),
@@ -1050,35 +1171,36 @@
         pltpu.VMEM((width, width), F32),
         pltpu.VMEM((rows, width), BF),
         pltpu.VMEM((rows, width), BF),
+        pltpu.VMEM((rows, width), BF),
         pltpu.VMEM((3, width, width), BF),
         pltpu.VMEM((rows, width), BF),
         pltpu.VMEM((rows, width), F32),
         pltpu.VMEM((rows, width), F32),
         pltpu.VMEM((seq, rows, width), BF),
         pltpu.VMEM((seq + 1, rows, width), BF),
-        pltpu.VMEM((2, *cube, part, half) if fast else (8, 128), BF),
+        pltpu.VMEM((PAIRS, *cube, part, 384), BF),
         pltpu.VMEM((*cube, 16, 128), F32),
         pltpu.VMEM((8, width), F32),
         pltpu.SemaphoreType.DMA((2, 4)),
         pltpu.SemaphoreType.DMA((34,)),
         pltpu.SemaphoreType.DMA((5,)),
-        pltpu.SemaphoreType.DMA((2, 4)),
-        pltpu.SemaphoreType.DMA((2, 4)),
+        pltpu.SemaphoreType.DMA((2, 4, 2)),
+        pltpu.SemaphoreType.DMA((2, 4, 2)),
     ]
     if fast:
-        d, u, o, q = (128, width), (part, span), (part, width), (part, half)
+        d, u, o, q = (128, width), (part, span), (part, width), (part, 384)
         scratch += [
             pltpu.VMEM(shape, BF)
             for shape in (
                 (2, 2, 2, *d), (2, 2, 2, *u), (2, 2, *o), (2, 2, *d), (2, 2, *u), (2, *o), (3, *d), (3, *u), o,
-                (2, 2, 2, *q), (2, 2, *q), (2, *q),
+                (PAIRS, 2, 2, *q), (PAIRS, 2, *q), (PAIRS, *q),
             )
         ]
         scratch += [pltpu.VMEM((2, 2, 16, 128), F32), pltpu.VMEM((2, 16, 128), F32), pltpu.VMEM((16, 128), F32)]
-        for shape in ((3, *d), (3, *u), o, (2, *q)):
+        for shape in ((3, *d), (3, *u), o, (PAIRS, *q)):
             scratch += [pltpu.VMEM(shape, BF)] * 3
         scratch += [pltpu.VMEM((16, 128), F32)] * 3
-        scratch += [pltpu.SemaphoreType.DMA(shape) for shape in ((8, 3), (8, 3), (10, 3), (10, 3))]
+        scratch += [pltpu.SemaphoreType.DMA(shape) for shape in ((12, 3), (12, 3), (14, 3), (14, 3))]
     return pl.pallas_call(
         partial(attend_back_kernel, fast),
         out_shape=outs,
@@ -1099,15 +1221,14 @@
 def unpack_kernel(fin_d, fin_u, fin_o, fin_q, fin_v, down_o, up_o, out_o, qkv_o, *vec_o):
     chunks, _, _ = fin_d.shape
     part, span = fin_u.shape[1:]
-    half = fin_q.shape[2]
     for c in range(chunks):
         down_o[128 * c : 128 * (c + 1)] = fin_d[c].astype(F32)
         for d in range(GROUPS):
             at = chunk_columns(up_o.shape[1], c, d)
             up_o[:, at : at + 128] = fin_u[c, :, 128 * d : 128 * (d + 1)].astype(F32)
     out_o[...] = fin_o[...].astype(F32)
-    for c in range(2):
-        qkv_o[:, half * c : half * (c + 1)] = fin_q[c].astype(F32)
+    for i in range(PAIRS):
+        qkv_o[:, 384 * i : 384 * (i + 1)] = fin_q[i].astype(F32)
     for r in range(8):
         vec_o[r][...] = fin_v[r : r + 1, :part].reshape(part)
     vec_o[8][...] = jnp.concatenate([fin_v[8 + c : 9 + c] for c in range(chunks)], axis=1).reshape(128 * chunks)
@@ -1120,7 +1241,7 @@
     sds = jax.ShapeDtypeStruct
     outs = [
         sds((128 * chunks, width), F32), sds((part, span * chunks), F32), sds((part, width), F32),
-        sds((part, 2 * fin_q.shape[2]), F32),
+        sds((part, PAIRS * fin_q.shape[2]), F32),
     ]
     outs += [sds((part,), F32)] * 8 + [sds((128 * chunks,), F32)]
     return pl.pallas_call(
@@ -1162,6 +1283,7 @@
 
         g_down, g_up, g_out = sums
         g_qkv, packed = found
+        g_qkv = jnp.moveaxis(g_qkv.reshape(PAIRS, width, 384), 0, 1).reshape(width, 3 * width)
         g_down = jnp.moveaxis(g_down.reshape(CHUNKS, GROUPS, 128, width), 0, 1).reshape(ff, width)
         g_up = jnp.transpose(g_up.reshape(CHUNKS, width, GROUPS, 128), (1, 2, 0, 3)).reshape(width, ff)
         down, up, out, qkv = summed(g_down), summed(g_up), summed(g_out.reshape(width, width)), summed(g_qkv)

time: 241 us -> 221 us (0.917); the launches traced: 241 us -> 218 us
  Pallas kernels: 238 us -> 215 us
    pallas_call x1, Pallas kernels: 130 us -> 113 us  [attend_back(): pl.pallas_call(partial(attend_back_kernel, fast), out_shape=outs, in_spec...]
    pallas_call x1, Pallas kernels: 69.3 us -> 64.9 us  [gather_attend(): pl.pallas_call(gather_kernel, out_shape=outs, in_specs=[any_spec, pl.Bloc...]
where the time goes in v3:
time: 221 us; the launch traced here: 218 us
  Pallas kernels  215 us (97%)
    pallas_call x1, Pallas kernels, attend_back(): pl.pallas_call(partial(attend_back_kernel, fast), out_shape=outs, in_spec...  113 us
    pallas_call x1, Pallas kernels, gather_attend(): pl.pallas_call(gather_kernel, out_shape=outs, in_specs=[any_spec, pl.Bloc...  64.9 us
    pallas_call x1, Pallas kernels, feed_forward(): pl.pallas_call(partial(feed_forward_kernel, fast), out_shape=outs, in_spe...  34.2 us

profile of v3, /device:TPU:0, one launch (start us, length us, event | category | flops | bytes accessed | tf_op | source)
XLA Modules:
  0.0 217.9 jit_solution(10247231835729721432)
XLA Ops:
  0.6 64.9 %gather_attend.1 = (bf16[4,6,512,128]{3,2,1,0:T(8,128)(2,1)}, bf16[4,6,512,128]{3,2,1,0:T(8,128)(2,1)}, bf16[4,6,128,512]{3,2,1,0:T(8,128)(2,1)}, bf16[4,768,512...) custom-call(bf16[512,768]{1,0:T(8,128)(2,1)} %bitcast.4, ...), custom_call_target="tpu_custom_call" | custom-call | tf_op jit(solution)/shard_map/gather_attend/pallas_call | solution.py:290
  65.6 34.2 %feed_forward.1 = (bf16[512,768]{1,0:T(8,128)(2,1)}, f32[512,768]{1,0:T(8,128)}, bf16[512,768]{1,0:T(8,128)(2,1)}, bf16[768,512]{1,0:T(8,128)(2,1)}, f32[16,512]...) custom-call(bf16[512,768]{1,0:T(8,128)(2,1)} %bitcast.5, ...), custom_call_target="tpu_custom_call" | custom-call | tf_op jit(solution)/shard_map/feed_forward/pallas_call | solution.py:633
  99.8 0.0 copy-start
  99.8 112.6 %attend_back.1 = (bf16[512,768]{1,0:T(8,128)(2,1)}, bf16[3,128,768]{2,1,0:T(8,128)(2,1)}, bf16[3,96,1024]{2,1,0:T(8,128)(2,1)}, bf16[96,768]{1,0:T(8,128)(2,1)},...) custom-call(bf16[4,6,512,128]{3,2,1,0:T(8,128)(2,1)} %get-tuple-element.59.refs_0_, ...), custom_call_target="tpu_custom_call" | custom-call | tf_op jit(solution)/shard_map/attend_back/pallas_call | solution.py:1204
  212.4 0.0 copy-start.1
  212.4 3.4 %unpack.1 = (f32[384,768]{1,0:T(8,128)}, f32[96,3072]{1,0:T(8,128)}, f32[96,768]{1,0:T(8,128)}, f32[96,2304]{1,0:T(8,128)}, f32[96]{0:T(128)}, /*index=5*/f32[96...) custom-call(bf16[3,128,768]{2,1,0:T(8,128)(2,1)} %get-tuple-element., ...), custom_call_target="tpu_custom_call" | custom-call | tf_op jit(solution)/shard_map/unpack/pallas_call | solution.py:1247
  215.8 0.0 copy-done
  215.8 0.9 copy.33
  216.7 0.0 copy-done.1
  216.7 0.9 copy.34
Async XLA Ops:
  99.8 116.1 %copy-start = (bf16[512,768]{1,0:T(8,128)(2,1)S(1)}, bf16[512,768]{1,0:T(8,128)(2,1)}, u32[]{:S(2)}) copy-start(bf16[512,768]{1,0:T(8,128)(2,1)} %get-tuple-element.58) | copy-start | bytes 2359300
  212.4 4.3 %copy-start.1 = (bf16[512,768]{1,0:T(8,128)(2,1)S(1)}, bf16[512,768]{1,0:T(8,128)(2,1)}, u32[]{:S(2)}) copy-start(bf16[512,768]{1,0:T(8,128)(2,1)} %get-tuple-element.78) | copy-start | bytes 2359300

commit v4 on v1

v4 whole, which is shorter than its diff:
```python
from functools import partial

import jax
import jax.numpy as jnp
from jax import lax
from jax.experimental import pallas as pl
from jax.experimental.pallas import tpu as pltpu
from jax.sharding import PartitionSpec as P

HEADS = 12
HEAD = 64
PAIRS = 6
EPS = 1e-05
ROOT_HALF = 0.7071067811865476
BIG = 1e30
MESH = pl.DeviceIdType.MESH
F32 = jnp.float32
BF = jnp.bfloat16
MIB = 1024 * 1024


def normalize(values, gain, shift):
    average = jnp.mean(values, axis=-1, keepdims=True)
    centred = values - average
    variance = jnp.mean(centred * centred, axis=-1, keepdims=True)
    return centred * lax.rsqrt(variance + EPS) * gain + shift


def gelu_exact(values):
    return 0.5 * values * (1.0 + jax.scipy.special.erf(values * ROOT_HALF))


def mm(a, b):
    return jnp.dot(a, b, preferred_element_type=F32)


def mm_nt(a, b):
    return lax.dot_general(a, b, (((1,), (1,)), ((), ())), preferred_element_type=F32)


def cell_bounds(lens_ref, index):
    start = jnp.zeros(index.shape, jnp.int32)
    end = jnp.zeros(index.shape, jnp.int32)
    at = jnp.int32(0)
    for c in range(lens_ref.shape[1]):
        after = at + lens_ref[0, c]
        start = jnp.where(index == c, at, start)
        end = jnp.where(index == c, after, end)
        at = after
    return start, end


def key_codes(lens_ref, block, rows):
    lane = lax.broadcasted_iota(jnp.int32, (1, 128), 1) % 64
    start, end = cell_bounds(lens_ref, lane)
    ones = ((lane >= 8) & (lane < 11)).astype(F32)
    slot = lax.broadcasted_iota(jnp.int32, (rows, 128), 0) + block * rows
    hot = jnp.where((slot >= start) & (slot < end), 1.0, 0.0)
    return (hot + ones).astype(BF)


def query_codes(lens_ref, block, rows):
    cell = lax.broadcasted_iota(jnp.int32, (64, 1), 0)
    start, end = cell_bounds(lens_ref, cell)
    slot = lax.broadcasted_iota(jnp.int32, (64, rows), 1) + block * rows
    inside = (slot >= start) & (slot < end)
    return jnp.where(inside | (cell >= 8), 0.0, -BIG)


def lane_halves():
    lane = lax.broadcasted_iota(jnp.int32, (1, 128), 1)
    low = jnp.where(lane < 64, 1.0, 0.0).astype(BF)
    high = jnp.where(lane < 64, 0.0, 1.0).astype(BF)
    return low, high


def sort_weights(w_ref, wp):
    depth = w_ref.shape[0]
    lane = lax.broadcasted_iota(jnp.int32, (depth, 128), 1)
    low = lane < 64
    for i in range(PAIRS):
        t0, t1, t2 = (w_ref[:, 384 * i + 128 * j : 384 * i + 128 * (j + 1)].astype(F32) for j in range(3))
        at = slice(128 * i, 128 * (i + 1))
        wp[0, :, at] = jnp.where(low, t0, t1).astype(BF)
        wp[1, :, at] = pltpu.roll(jnp.where(low, t2, t0), 64, 1).astype(BF)
        wp[2, :, at] = jnp.where(low, t1, t2).astype(BF)


def gather_kernel(
    tok, lens, gain, shift, w_h, bq, bv,
    kn_o, vn_o, kt_o, xt_o, qn_o, qt_o, wp_o, att_f, att_o, lse_o,
    xr, w, wp, kn, vn, kt, xt, qn, qt, qta, vta, acc, top, send, recv, in_sem, out_sem,
):
    rows, width = tok.shape
    span = rows // 2
    seq = lax.axis_size("seq")
    me = lax.axis_index("seq")
    has_left, has_right = me > 0, me < seq - 1
    at_end = (me == 0) | (me == seq - 1)

    barrier = pltpu.get_barrier_semaphore()

    @pl.when(has_left)
    def _():
        pl.semaphore_signal(barrier, inc=1, device_id={"seq": me - 1}, device_id_type=MESH)

    @pl.when(has_right)
    def _():
        pl.semaphore_signal(barrier, inc=1, device_id={"seq": me + 1}, device_id_type=MESH)

    own_tokens = pltpu.make_async_copy(tok, xr.at[me], in_sem.at[0])
    own_tokens.start()
    weights = pltpu.make_async_copy(w_h, w, in_sem.at[1])
    weights.start()

    @pl.when(at_end)
    def _():
        pl.semaphore_wait(barrier, 1)

    @pl.when(~at_end)
    def _():
        pl.semaphore_wait(barrier, 2)

    def copy(way, hop, half, block):
        at = pl.ds(half * span, span)
        return pltpu.make_async_remote_copy(
            src_ref=tok.at[at] if hop == 0 else xr.at[block, at],
            dst_ref=xr.at[block, at],
            send_sem=send.at[way, hop, half],
            recv_sem=recv.at[way, hop, half],
            device_id={"seq": me - 1 if way == 0 else me + 1},
            device_id_type=MESH,
        )

    def can_send(way):
        return has_left if way == 0 else has_right

    def holds(way, hop):
        return me + hop < seq if way == 0 else me - hop >= 0

    def block_of(way, hop):
        return me + hop if way == 0 else me - hop

    for half in range(2):
        for way in range(2):
            @pl.when(can_send(way))
            def _():
                copy(way, 0, half, me).start()

    def normed(raw):
        return normalize(raw.astype(F32), gain[...].reshape(1, -1), shift[...].reshape(1, -1)).astype(BF)

    row16 = lax.broadcasted_iota(jnp.int32, (16, span), 0)
    for h in range(HEADS):
        vta[h, 64:] = jnp.where(row16 == 0, 1.0, 0.0).astype(BF)
    acc[...] = jnp.zeros_like(acc)
    top[...] = jnp.full_like(top, -3e38)
    codes = query_codes(lens, me, rows).astype(BF)
    low, high = lane_halves()
    own_tokens.wait()
    weights.wait()
    sort_weights(w, wp)
    keep_w = pltpu.make_async_copy(wp, wp_o, out_sem.at[0])
    keep_w.start()
    q = ((mm(normed(xr[me]), wp[0]) + bq[...].reshape(1, -1)).astype(BF).astype(F32) * (HEAD**-0.5)).astype(BF)
    for i in range(PAIRS):
        pair = q[:, 128 * i : 128 * (i + 1)]
        qn[i] = pair
        turned = pair.T
        qt[i] = turned
        qta[2 * i, :64] = turned[:64]
        qta[2 * i, 64:] = codes
        qta[2 * i + 1, :64] = codes
        qta[2 * i + 1, 64:] = turned[64:]
    keep_q = pltpu.make_async_copy(qn, qn_o, out_sem.at[1])
    keep_q.start()
    keep_qt = pltpu.make_async_copy(qt, qt_o, out_sem.at[2])
    keep_qt.start()

    def keeps(step):
        block = block_at(step)
        return [
            pltpu.make_async_copy(kn.at[block], kn_o.at[block], out_sem.at[3 + 4 * step]),
            pltpu.make_async_copy(vn.at[block], vn_o.at[block], out_sem.at[4 + 4 * step]),
            pltpu.make_async_copy(kt.at[block], kt_o.at[block], out_sem.at[5 + 4 * step]),
            pltpu.make_async_copy(xt.at[block], xt_o.at[block], out_sem.at[6 + 4 * step]),
        ]

    def block_at(step):
        from_end = jnp.where(me == 0, step, seq - 1 - step)
        from_mid = jnp.where(step == 0, me, jnp.where(step == 1, me + 1, jnp.where(step == 2, me - 1, jnp.where(me == 1, seq - 1, 0))))
        return jnp.where(at_end, from_end, from_mid)

    def half_step(turn, carry):
        step, half = turn // 2, turn % 2
        for hop in range(1, 4):
            for part in range(2):
                due = turn == jnp.where(at_end, 2 * hop + part, 4 * hop - 2 + part)
                for way in range(2):
                    @pl.when(due & holds(way, hop))
                    def _():
                        copy(way, hop - 1, part, block_of(way, hop)).wait_recv()

                        @pl.when(can_send(way))
                        def _():
                            copy(way, hop, part, block_of(way, hop)).start()

        block = block_at(step)
        at = pl.ds(pl.multiple_of(half * span, span), span)
        x = normed(xr[block, at])
        keys = mm(x, wp[1]).astype(BF)
        values = (mm(x, wp[2]) + bv[...].reshape(1, -1)).astype(BF)
        hot = key_codes(lens, 2 * block + half, span)
        hot_low, hot_high = hot * low, hot * high
        xt[block, :, at] = x.T
        for i in range(PAIRS):
            cut = slice(128 * i, 128 * (i + 1))
            kn[block, i, at] = keys[:, cut]
            kt[block, i, :, at] = keys[:, cut].T
            vn[block, i, at] = values[:, cut]
            turned = values[:, cut].T
            vta[2 * i, :64] = turned[:64]
            vta[2 * i + 1, :64] = turned[64:]

        def one_pair(i, carry):
            pair = kn[block, i, at]
            scores = [
                mm(pair * low + hot_high, qta[2 * i]),
                mm(pair * high + hot_low, qta[2 * i + 1]),
            ]
            for j in range(2):
                h = 2 * i + j
                before = top[h]
                now = jnp.maximum(before, jnp.max(scores[j], axis=0, keepdims=True))
                raised = jnp.exp(scores[j] - now).astype(BF)
                top[h] = now
                acc[h] = acc[h] * jnp.exp(before - now) + mm(vta[h], raised)
            return carry

        lax.fori_loop(0, PAIRS, one_pair, 0)
        for s in range(4):
            @pl.when(turn == 2 * s + 1)
            def _():
                for c in keeps(s):
                    c.start()

        return carry

    lax.fori_loop(0, 2 * seq, half_step, 0)

    lse_o[...] = jnp.zeros_like(lse_o)
    for h in range(HEADS):
        total = acc[h, 64:65]
        lse_o[h : h + 1] = top[h] + jnp.log(total)
        att_f[64 * h : 64 * (h + 1)] = acc[h, :64] / total
    att_o[...] = att_f[...].T.astype(BF)

    for way in range(2):
        for hop in range(3):
            for half in range(2):
                @pl.when(can_send(way) & holds(way, hop))
                def _():
                    copy(way, hop, half, block_of(way, hop)).wait_send()

    keep_w.wait()
    keep_q.wait()
    keep_qt.wait()
    for step in range(4):
        for c in keeps(step):
            c.wait()


def gather_attend(tokens, lens, gain, shift, w, bq, bv, seq):
    rows, width = tokens.shape
    any_spec = pl.BlockSpec(memory_space=pl.ANY)
    vmem = pl.BlockSpec(memory_space=pltpu.VMEM)
    sds = jax.ShapeDtypeStruct
    outs = [
        sds((seq, PAIRS, rows, 128), BF),
        sds((seq, PAIRS, rows, 128), BF),
        sds((seq, PAIRS, 128, rows), BF),
        sds((seq, width, rows), BF),
        sds((PAIRS, rows, 128), BF),
        sds((PAIRS, 128, rows), BF),
        sds((3, width, width), BF),
        sds((width, rows), F32),
        sds((rows, width), BF),
        sds((16, rows), F32),
    ]
    return pl.pallas_call(
        gather_kernel,
        out_shape=outs,
        in_specs=[any_spec, pl.BlockSpec(memory_space=pltpu.SMEM), vmem, vmem, any_spec, vmem, vmem],
        out_specs=[any_spec] * 7 + [vmem] * 3,
        scratch_shapes=[
            pltpu.VMEM((seq, rows, width), BF),
            pltpu.VMEM((width, 3 * width), BF),
            pltpu.VMEM((3, width, width), BF),
            pltpu.VMEM((seq, PAIRS, rows, 128), BF),
            pltpu.VMEM((seq, PAIRS, rows, 128), BF),
            pltpu.VMEM((seq, PAIRS, 128, rows), BF),
            pltpu.VMEM((seq, width, rows), BF),
            pltpu.VMEM((PAIRS, rows, 128), BF),
            pltpu.VMEM((PAIRS, 128, rows), BF),
            pltpu.VMEM((HEADS, 128, rows), BF),
            pltpu.VMEM((HEADS, 80, rows // 2), BF),
            pltpu.VMEM((HEADS, 80, rows), F32),
            pltpu.VMEM((HEADS, 1, rows), F32),
            pltpu.SemaphoreType.DMA((2, 4, 2)),
            pltpu.SemaphoreType.DMA((2, 4, 2)),
            pltpu.SemaphoreType.DMA((2,)),
            pltpu.SemaphoreType.DMA((20,)),
        ],
        compiler_params=pltpu.CompilerParams(
            collective_id=0, has_side_effects=True, vmem_limit_bytes=58 * MIB
        ),
        name="gather_attend",
    )(tokens, lens, gain, shift, w, bq, bv)


def three_parts(values):
    high = values.astype(BF).astype(F32)
    middle = (values - high).astype(BF).astype(F32)
    return high, middle, values - high - middle


def add_parts(total, other, parts=1, step=32):
    depth = total.shape[-2] // step

    def some(k, carry):
        at = (pl.ds(pl.multiple_of(k % depth * step, step), step),)
        if len(total.shape) == 3:
            at = (k // depth, *at)
        total[at] = total[at] + other[at]
        return carry

    lax.fori_loop(0, parts * depth, some, 0)


def dp_place():
    dp = lax.axis_index("dp")
    core, x, y = dp % 2, (dp // 2) % 2, dp // 4
    return (core, x, y), (dp + 1 - 2 * core, dp + 2 - 4 * x, dp + 4 - 8 * y)


class DpSum:
    def __init__(self, first, stage, one, two, three, send, recv):
        self.first, self.stage, self.one, self.two, self.three = first, stage, one, two, three
        (self.core, self.x, self.y), (self.to_core, self.to_x, self.to_y) = dp_place()
        self.send, self.recv = send, recv
        self.step = min(32, three.shape[-2])

    def copy(self, phase):
        x_first = self.first == "x"
        if phase == 0:
            src, dst, to = self.stage.at[:, :, 1 - self.core], self.one, self.to_core
        elif phase == 1:
            src = self.one.at[:, 1 - self.x] if x_first else self.one.at[1 - self.y]
            dst, to = self.two, self.to_x if x_first else self.to_y
        else:
            src = self.two.at[1 - self.y] if x_first else self.two.at[1 - self.x]
            dst, to = self.three, self.to_y if x_first else self.to_x
        return pltpu.make_async_remote_copy(
            src_ref=src, dst_ref=dst, send_sem=self.send.at[phase], recv_sem=self.recv.at[phase],
            device_id={"dp": to}, device_id_type=MESH,
        )

    def start(self, phase):
        self.copy(phase).start()

    def finish(self, phase):
        self.copy(phase).wait_recv()
        x_first = self.first == "x"
        if phase == 0:
            for y in range(2):
                add_parts(self.one.at[y], self.stage.at[y, :, self.core], 2, self.step)
        elif phase == 1:
            add_parts(self.two, self.one.at[:, self.x] if x_first else self.one.at[self.y], 2, self.step)
        else:
            add_parts(self.three, self.two.at[self.y] if x_first else self.two.at[self.x], 1, self.step)

    def wait_sends(self, phases):
        for phase in phases:
            self.copy(phase).wait_send()


class SeqSum:
    def __init__(self, part, total, swapped, send, recv):
        self.part, self.total, self.swapped = part, total, swapped
        self.send, self.recv = send, recv
        me = lax.axis_index("seq")
        self.end = (me == 0) | (me == 3)
        self.partner = jnp.where(me < 2, 1 - me, 5 - me)
        self.other = 3 - me

    def copy(self, phase):
        src, dst, to = (
            (self.part, self.total, self.partner),
            (self.part, self.swapped, self.other),
            (self.total, self.total, self.partner),
        )[phase]
        return pltpu.make_async_remote_copy(
            src_ref=src, dst_ref=dst, send_sem=self.send.at[phase], recv_sem=self.recv.at[phase],
            device_id={"seq": to}, device_id_type=MESH,
        )

    def ends_send(self):
        @pl.when(self.end)
        def _():
            self.copy(0).start()

    def middles_swap(self):
        @pl.when(~self.end)
        def _():
            self.copy(0).wait_recv()
            add_parts(self.part, self.total, 1, min(32, self.part.shape[-2]))
            self.copy(1).start()

    def middles_send(self):
        @pl.when(~self.end)
        def _():
            self.copy(1).wait_recv()
            depth = min(32, self.part.shape[-2])

            def some(k, carry):
                at = pl.ds(pl.multiple_of(k * depth, depth), depth)
                self.total[at] = self.part[at] + self.swapped[at]
                return carry

            lax.fori_loop(0, self.part.shape[-2] // depth, some, 0)
            self.copy(2).start()

    def finish(self):
        @pl.when(self.end)
        def _():
            self.copy(0).wait_send()
            self.copy(2).wait_recv()

        @pl.when(~self.end)
        def _():
            self.copy(1).wait_send()
            self.copy(2).wait_send()


CHUNKS = 3
GROUPS = 8


def chunk_columns(ff, c, d):
    return (ff // GROUPS) * d + 128 * c


def place_of(d):
    return d // 4, (d // 2) % 2, d % 2


def layer_back_kernel(fast, *refs):
    (
        kn_h, vn_h, kt_h, xt_h, qn_h, qt_h, wp_h, att_h, att_f_h, tok_h, cot_h, w_out_h, w_up_h, w_down_h,
        lse, lens, gain_one, b_out, gain, shift, b_up, b_down, *refs,
    ) = refs
    layer_o, tok_o, *refs = refs
    if fast:
        fin_d_o, fin_u_o, fin_o_o, fin_q_o, fin_v_o, *refs = refs
    else:
        gd_o, gu_o, go_o, gq_o, stage_v_o, *refs = refs
    (
        stage_d, stage_u, stage_o, stage_v, sums, vec_up, d_att, dta, d_mid, rx,
        ff_sem, in_sem, load_sem, out_sem, dsend, drecv, *refs,
    ) = refs
    rows, width = tok_h.shape
    ff = w_up_h.shape[1]
    span = GROUPS * 128
    part_w = width // GROUPS
    seq = lax.axis_size("seq")
    me = lax.axis_index("seq")
    has_left, has_right = me > 0, me < seq - 1
    at_end = (me == 0) | (me == seq - 1)
    half_rows = rows // 2

    barrier = pltpu.get_barrier_semaphore()

    @pl.when(has_left)
    def _():
        pl.semaphore_signal(barrier, inc=1, device_id={"seq": me - 1}, device_id_type=MESH)

    @pl.when(has_right)
    def _():
        pl.semaphore_signal(barrier, inc=1, device_id={"seq": me + 1}, device_id_type=MESH)

    if fast:
        for to in dp_place()[1]:
            pl.semaphore_signal(barrier, inc=1, device_id={"dp": to}, device_id_type=MESH)
    greeted = 3 if fast else 0

    def meet():
        @pl.when(at_end)
        def _():
            pl.semaphore_wait(barrier, greeted + 1)

        @pl.when(~at_end)
        def _():
            pl.semaphore_wait(barrier, greeted + 2)

    if fast:
        (
            one_d, one_u, one_o, two_d, two_u, two_o, three_d, three_u, three_o,
            one_q, two_q, three_q, one_v, two_v, three_v,
            zx_d, fin_d, zx_u, fin_u, zx_o, fin_o, zx_q, fin_q, zx_v, fin_v,
            psend, precv, zsend, zrecv,
        ) = refs
        rs_d = [
            DpSum("x", stage_d.at[c], one_d.at[c], two_d.at[c], three_d.at[c], psend.at[c], precv.at[c])
            for c in range(CHUNKS)
        ]
        rs_u = [
            DpSum("y", stage_u.at[c], one_u.at[c], two_u.at[c], three_u.at[c], psend.at[3 + c], precv.at[3 + c])
            for c in range(CHUNKS)
        ]
        rs_o = DpSum("x", stage_o, one_o, two_o, three_o, psend.at[6], precv.at[6])
        rs_v = DpSum("x", stage_v, one_v, two_v, three_v, psend.at[7], precv.at[7])

        def couple(c):
            found = []
            for k in range(2):
                tile = 2 * c + k
                staged = stage_u.at[c, :, :, :, :, pl.ds(384 * k, 384)]
                found.append(
                    DpSum(
                        "xy"[k], staged, one_q.at[tile], two_q.at[tile], three_q.at[tile],
                        psend.at[8 + tile], precv.at[8 + tile],
                    )
                )
            return found

        ar_d = [
            SeqSum(three_d.at[c], fin_d.at[c], zx_d.at[c], zsend.at[c], zrecv.at[c]) for c in range(CHUNKS)
        ]
        ar_u = [
            SeqSum(three_u.at[c], fin_u.at[c], zx_u.at[c], zsend.at[3 + c], zrecv.at[3 + c])
            for c in range(CHUNKS)
        ]
        ar_o = SeqSum(three_o, fin_o, zx_o, zsend.at[6], zrecv.at[6])
        ar_v = SeqSum(three_v, fin_v, zx_v, zsend.at[7], zrecv.at[7])
        ar_q = [
            SeqSum(three_q.at[c], fin_q.at[c], zx_q.at[c], zsend.at[8 + c], zrecv.at[8 + c])
            for c in range(PAIRS)
        ]

    def turn(*found):
        for unit_sum in found:
            unit_sum.finish(1)
            unit_sum.start(2)

    def close(*found):
        for unit_sum in found:
            unit_sum.finish(2)

    def per_row(ref):
        return ref[...].reshape(1, -1)

    stage_v[...] = jnp.zeros_like(stage_v)
    sums[...] = jnp.zeros_like(sums)

    def feed_forward(tok, att, att_f, cot, w_out, wu, wd, d_norm, bias):
        first = [
            pltpu.make_async_copy(src, dst, ff_sem.at[2, k // GROUPS, k % GROUPS])
            for k, (src, dst) in enumerate(((tok_h, tok), (att_h, att), (w_out_h, w_out), (cot_h, cot), (att_f_h, att_f)))
        ]

        def loads(c):
            found = []
            for d in range(GROUPS):
                at = pl.ds(chunk_columns(ff, c, d), 128)
                to = pl.ds(128 * d, 128)
                found.append(pltpu.make_async_copy(w_up_h.at[:, at], wu.at[c % 2, :, to], ff_sem.at[0, c, d]))
                found.append(pltpu.make_async_copy(w_down_h.at[at], wd.at[c % 2, to], ff_sem.at[1, c, d]))
            return found

        for copy in (*first[:3], *loads(0), *first[3:], *loads(1)):
            copy.start()
        meet()
        for copy in first[:3]:
            copy.wait()
        middle = tok[...].astype(F32) + mm(att[...], w_out[...]) + per_row(b_out)
        average = jnp.mean(middle, axis=-1, keepdims=True)
        centred = middle - average
        scale = lax.rsqrt(jnp.mean(centred * centred, axis=-1, keepdims=True) + EPS)
        unit = centred * scale
        normed = (unit * per_row(gain) + per_row(shift)).astype(BF)
        normed_t = normed.T
        for copy in first[3:]:
            copy.wait()
        d_out = cot[...]
        for c in range(CHUNKS):
            for d in range(GROUPS):
                at = chunk_columns(ff, c, d)
                bias[c : c + 1, 128 * d : 128 * (d + 1)] = b_up[at : at + 128].reshape(1, 128)
        d_mid[...] = middle + per_row(b_down)
        d_norm[...] = jnp.zeros_like(d_norm)

        def one_chunk(c, carry):
            for copy in loads(c):
                copy.wait()
            slot = c % 2
            upper = mm(normed, wu[slot]) + bias[pl.ds(c, 1)]
            cdf = 0.5 * (1.0 + lax.erf(upper * ROOT_HALF))
            hidden = (upper * cdf).astype(BF)
            slope = cdf + upper * (jnp.exp(-0.5 * upper * upper) * 0.3989422804014327)
            d_upper = (mm_nt(d_out, wd[slot]) * slope).astype(BF)
            vec_up[pl.ds(c, 1)] = jnp.sum(d_upper.astype(F32), axis=0, keepdims=True)
            if fast:

                @pl.when(c == 1)
                def _():
                    for unit_sum in (rs_d[0], rs_u[0]):
                        unit_sum.finish(0)
                        unit_sum.start(1)

                @pl.when(c == 2)
                def _():
                    for unit_sum in (rs_d[1], rs_u[1]):
                        unit_sum.finish(0)

            g_down = mm(hidden.T, d_out).astype(BF)
            g_up = mm(normed_t, d_upper).astype(BF)
            for d in range(GROUPS):
                stage_d[(c, *place_of(d))] = g_down[128 * d : 128 * (d + 1)]
                stage_u[(c, *place_of(d))] = g_up[96 * d : 96 * (d + 1)]
            if fast:
                for k in range(CHUNKS):

                    @pl.when(c == k)
                    def _():
                        rs_d[k].start(0)
                        rs_u[k].start(0)
                        if k == 2:
                            turn(rs_d[0], rs_u[0])
                            rs_d[1].start(1)
                            rs_u[1].start(1)

            d_mid[...] += mm(hidden, wd[slot])
            d_norm[...] += mm_nt(d_upper, wu[slot])

            @pl.when(c == 0)
            def _():
                for copy in loads(2):
                    copy.start()

            return carry

        lax.fori_loop(0, CHUNKS, one_chunk, 0)
        d_normed = d_norm[...]
        tok[...] = d_mid[...].astype(BF)
        keep_layer = pltpu.make_async_copy(tok, layer_o, out_sem.at[5])
        keep_layer.start()
        sums[7:8] = jnp.sum(d_out.astype(F32), axis=0, keepdims=True)
        sums[5:6] = jnp.sum(d_normed * unit, axis=0, keepdims=True)
        sums[6:7] = jnp.sum(d_normed, axis=0, keepdims=True)
        scaled = d_normed * per_row(gain)
        d_middle = d_out.astype(F32) + scale * (
            scaled
            - jnp.mean(scaled, axis=-1, keepdims=True)
            - unit * jnp.mean(scaled * unit, axis=-1, keepdims=True)
        )
        d_mid[...] = d_middle
        d_branch = d_middle.astype(BF)
        sums[4:5] = jnp.sum(d_branch.astype(F32), axis=0, keepdims=True)
        g_out = mm(att_f[...].astype(BF), d_branch).astype(BF)
        for d in range(GROUPS):
            stage_o[place_of(d)] = g_out[96 * d : 96 * (d + 1)]
        if fast:
            rs_o.start(0)
            for unit_sum in (rs_d[2], rs_u[2]):
                unit_sum.finish(0)
            close(rs_d[0], rs_u[0])
            ar_d[0].ends_send()
            ar_u[0].ends_send()
        d_attended = mm_nt(d_branch, w_out[...]).astype(BF)
        d_att[...] = d_attended
        turned = d_attended.T
        product = turned.astype(F32) * att_f[...]
        row16 = lax.broadcasted_iota(jnp.int32, (16, rows), 0)
        for h in range(HEADS):
            own, other = 64 * (h % 2), 64 * (1 - h % 2)
            dta[h, own : own + 64] = turned[64 * h : 64 * (h + 1)]
            delta = jnp.sum(product[64 * h : 64 * (h + 1)], axis=0, keepdims=True)
            extra = jnp.zeros((16, rows), F32)
            for r, part in enumerate(three_parts(-delta)):
                extra = jnp.where(row16 == r, part, extra)
            dta[h, other : other + 16] = extra.astype(BF)
            dta[h, other + 16 : other + 64] = jnp.zeros((48, rows), BF)
        if fast:
            rs_o.finish(0)
        else:
            keep = [
                pltpu.make_async_copy(stage_d, gd_o, out_sem.at[0]),
                pltpu.make_async_copy(stage_u, gu_o, out_sem.at[1]),
                pltpu.make_async_copy(stage_o, go_o, out_sem.at[2]),
            ]
            for copy in keep:
                copy.start()
            for copy in keep:
                copy.wait()
        keep_layer.wait()

    pl.run_scoped(
        feed_forward,
        pltpu.VMEM((rows, width), BF),
        pltpu.VMEM((rows, width), BF),
        pltpu.VMEM((width, rows), F32),
        pltpu.VMEM((rows, width), BF),
        pltpu.VMEM((width, width), BF),
        pltpu.VMEM((2, width, span), BF),
        pltpu.VMEM((2, span, width), BF),
        pltpu.VMEM((rows, width), F32),
        pltpu.VMEM((8, span), F32),
    )

    def block_at(step):
        b0 = jnp.where(me < 2, seq - 1, 0)
        b1 = jnp.where(me < 2, seq - 2, 1)
        b2 = jnp.where(me == 0, 1, jnp.where(me == 1, 0, jnp.where(me == 2, 3, 2)))
        return jnp.where(step == 0, b0, jnp.where(step == 1, b1, jnp.where(step == 2, b2, me)))

    def dx_stage(step, half):
        return stage_d.at[step // 2, step % 2, half]

    def dx_copy(way, step, block, half):
        return pltpu.make_async_remote_copy(
            src_ref=dx_stage(step, half), dst_ref=rx.at[block + way, half],
            send_sem=dsend.at[way, block, half], recv_sem=drecv.at[way, block, half],
            device_id={"seq": me - 1 if way == 0 else me + 1}, device_id_type=MESH,
        )

    def store_dx(step, half, value):
        for k in range(2):
            stage_d[step // 2, step % 2, half, k] = value[128 * k : 128 * (k + 1)]

    def relay_at(place, way, step, half):
        @pl.when(me == place)
        def _():
            block = block_at(step)
            dx_copy(way, step, block, half).wait_recv()
            add_parts(dx_stage(step, half), rx.at[block + way, half], 2)
            dx_copy(way, step, block, half).start()

    def relay_far(step, half):
        relay_at(1, 1, step, half)
        relay_at(2, 0, step, half)

    def relay_near(half):
        relay_at(1, 0, 2, half)
        relay_at(2, 1, 2, half)

    def send_dx(step, half):
        block = block_at(step)

        @pl.when(me == 0)
        def _():
            dx_copy(1, step, block, half).start()

        @pl.when(me == seq - 1)
        def _():
            dx_copy(0, step, block, half).start()

    def attention(kn, vn, kt, xt, qta, dqt, gk, gv, dk, dv, dq, wp, qn, hot_ref):
        def loads(step):
            block, slot = block_at(step), step % 2
            return [
                pltpu.make_async_copy(kn_h.at[block], kn.at[slot], in_sem.at[slot, 0]),
                pltpu.make_async_copy(vn_h.at[block], vn.at[slot], in_sem.at[slot, 1]),
                pltpu.make_async_copy(kt_h.at[block], kt.at[slot], in_sem.at[slot, 2]),
            ]

        def load_x(step):
            return pltpu.make_async_copy(xt_h.at[block_at(step)], xt, in_sem.at[0, 3])

        fills = [pltpu.make_async_copy(qn_h, qn, load_sem.at[HEADS])]
        for h in range(HEADS):
            own = pl.ds(64 * (h % 2), 64)
            fills.append(pltpu.make_async_copy(qt_h.at[h // 2, own], qta.at[h, own], load_sem.at[h]))
        load_wp = pltpu.make_async_copy(wp_h, wp, load_sem.at[HEADS + 1])
        for copy in (*loads(0), *fills, load_x(0), load_wp):
            copy.start()
        low, high = lane_halves()
        codes = query_codes(lens, me, rows)[:16]
        row16 = lax.broadcasted_iota(jnp.int32, (16, rows), 0)
        for h in range(HEADS):
            other = 64 * (1 - h % 2)
            extra = codes
            for r, part in enumerate(three_parts(-lse[h : h + 1])):
                extra = jnp.where(row16 == 8 + r, part, extra)
            qta[h, other : other + 16] = extra.astype(BF)
            qta[h, other + 16 : other + 64] = jnp.zeros((48, rows), BF)
        dqt[...] = jnp.zeros_like(dqt)
        lane = lax.broadcasted_iota(jnp.int32, (1, 128), 1)
        v_low = jnp.where(lane < 3, 1.0, 0.0).astype(BF)
        v_high = jnp.where((lane >= 64) & (lane < 67), 1.0, 0.0).astype(BF)
        if fast:
            for unit_sum in rs_d:
                unit_sum.wait_sends((0,))
        for copy in fills:
            copy.wait()

        def hooks(g):
            if not fast:
                return

            def at(when, action):
                @pl.when(g == when)
                def _():
                    action()

            def second():
                turn(rs_d[1], rs_u[1])
                for unit_sum in (rs_d[2], rs_u[2], rs_o):
                    unit_sum.start(1)

            at(5, second)
            at(6, lambda: (ar_d[0].middles_swap(), ar_u[0].middles_swap()))
            at(12, lambda: (close(rs_d[1], rs_u[1]), ar_d[1].ends_send(), ar_u[1].ends_send()))
            at(14, lambda: relay_far(0, 0))
            at(16, lambda: (ar_d[0].middles_send(), ar_u[0].middles_send()))
            at(17, lambda: turn(rs_d[2], rs_u[2]))
            at(20, lambda: relay_far(0, 1))
            at(21, lambda: (turn(rs_o), close(rs_d[2], rs_u[2])))
            at(23, lambda: (close(rs_o), [unit.ends_send() for unit in (ar_d[2], ar_u[2], ar_o)]))

        def products(slot, i, part=slice(None)):
            at = pl.ds(pl.multiple_of(i * 128, 128), 128)
            keys, values = kn[slot, i, part], vn[slot, i, part]
            q_pair, d_pair = qn[i], d_att[:, at]
            hot = hot_ref[part]
            scores = [
                mm(keys * low + hot * high, qta[2 * i]),
                mm(keys * high + hot * low, qta[2 * i + 1]),
            ]
            slopes = [
                mm(values * low + v_high, dta[2 * i]),
                mm(values * high + v_low, dta[2 * i + 1]),
            ]
            d_keys = jnp.zeros((keys.shape[0], 128), F32)
            d_values = jnp.zeros((keys.shape[0], 128), F32)
            for j in range(2):
                h = 2 * i + j
                mask = low if j == 0 else high
                probs = jnp.exp(scores[j])
                d_scores = (probs * slopes[j]).astype(BF)
                d_values = d_values + mm(probs.astype(BF), d_pair * mask)
                d_keys = d_keys + mm(d_scores, q_pair * mask)
                dqt[h] += mm(kt[slot, i, 64 * j : 64 * (j + 1), part], d_scores)
            dk[part, at] = d_keys.astype(BF)
            dv[part, at] = d_values.astype(BF)

        def enter(step):
            for copy in loads(step):
                copy.wait()
            hot_ref[...] = key_codes(lens, block_at(step), rows)

        enter(0)
        for copy in loads(1):
            copy.start()

        def one_half(half, carry):
            part = pl.ds(pl.multiple_of(half * half_rows, half_rows), half_rows)

            def one_pair(i, carry):
                hooks(half * PAIRS + i)
                products(0, i, part)
                return carry

            lax.fori_loop(0, PAIRS, one_pair, 0)

            @pl.when(half == 0)
            def _():
                load_wp.wait()

            store_dx(0, half, (mm_nt(dk[part], wp[1]) + mm_nt(dv[part], wp[2])).astype(BF))
            send_dx(0, half)
            return carry

        lax.fori_loop(0, 2, one_half, 0)
        load_x(0).wait()
        gk[...] = mm(xt[...], dk[...])
        gv[...] = mm(xt[...], dv[...])
        load_x(1).start()
        sums[3:4] = jnp.sum(dv[...].astype(F32), axis=0, keepdims=True)

        def one_step(step, carry):
            slot = step % 2
            enter(step)
            for copy in loads(step + 1):
                copy.start()

            def one_pair(i, carry):
                hooks((step + 1) * PAIRS + i)
                products(slot, i)
                return carry

            lax.fori_loop(0, PAIRS, one_pair, 0)
            dx = (mm_nt(dk[...], wp[1]) + mm_nt(dv[...], wp[2])).astype(BF)
            for half in range(2):
                store_dx(step, half, dx[half * half_rows : (half + 1) * half_rows])
                send_dx(step, half)
            load_x(step).wait()
            gk[...] += mm(xt[...], dk[...])
            gv[...] += mm(xt[...], dv[...])
            load_x(step + 1).start()
            sums[3:4] += jnp.sum(dv[...].astype(F32), axis=0, keepdims=True)
            return carry

        lax.fori_loop(1, seq - 1, one_step, 0)

        last = (seq - 1) % 2
        enter(seq - 1)
        load_x(seq - 1).wait()
        lane_w = lax.broadcasted_iota(jnp.int32, (width, 128), 1)
        lo = lane_w < 64
        if fast:
            for unit_sum in rs_u:
                unit_sum.wait_sends((0,))

        def one_couple(c, carry):
            if fast:

                @pl.when(c == 0)
                def _():
                    relay_near(0)
                    ar_d[1].middles_swap()
                    ar_u[1].middles_swap()

                @pl.when(c == 1)
                def _():
                    relay_near(1)
                    relay_far(1, 0)

                @pl.when(c == 2)
                def _():
                    relay_far(1, 1)
                    ar_d[1].middles_send()
                    ar_u[1].middles_send()

                @pl.when(c >= 1)
                def _():
                    for unit in couple(c - 1):
                        unit.finish(0)
                        unit.start(1)

                @pl.when(c >= 2)
                def _():
                    turn(*couple(c - 2))


            def one_pair(k, carry):
                products(last, 2 * c + k)
                return carry

            lax.fori_loop(0, 2, one_pair, 0)
            at = pl.ds(pl.multiple_of(c * 256, 256), 256)
            turned = dqt[pl.ds(4 * c, 4)].reshape(256, rows) * (HEAD**-0.5)
            dq_part = turned.T.astype(BF)
            dq[:, at] = dq_part
            x_t = xt[...]
            gq_part = mm(x_t, dq_part)
            gk_part = gk[:, at] + mm(x_t, dk[:, at])
            gv_part = gv[:, at] + mm(x_t, dv[:, at])
            for k in range(2):
                cut = slice(128 * k, 128 * (k + 1))
                q_tile, v_tile = gq_part[:, cut], gv_part[:, cut]
                k_tile = pltpu.roll(gk_part[:, cut], 64, 1)
                tiles = jnp.where(lo, q_tile, k_tile), jnp.where(lo, v_tile, q_tile), jnp.where(lo, k_tile, v_tile)
                for j, tile in enumerate(tiles):
                    tile = tile.astype(BF)
                    to = slice(384 * k + 128 * j, 384 * k + 128 * (j + 1))
                    for d in range(GROUPS):
                        stage_u[(c, *place_of(d), slice(None), to)] = tile[part_w * d : part_w * (d + 1)]
            if fast:
                for unit in couple(c):
                    unit.start(0)
            return carry

        lax.fori_loop(0, PAIRS // 2, one_couple, 0)
        if not fast:
            for step in range(2):
                for half in range(2):
                    relay_far(step, half)
            relay_near(0)
            relay_near(1)
        dx_own = gk.at[pl.ds(0, rows)]
        dx_own[...] = mm_nt(dk[...], wp[1]) + mm_nt(dv[...], wp[2]) + mm_nt(dq[...], wp[0])
        sums[3:4] += jnp.sum(dv[...].astype(F32), axis=0, keepdims=True)
        sums[2:3] = jnp.sum(dq[...].astype(F32), axis=0, keepdims=True)
        load_tok = pltpu.make_async_copy(tok_h, dv, load_sem.at[HEADS + 2])
        load_tok.start()
        if fast:
            for unit in couple(2):
                unit.finish(0)
                unit.start(1)
            turn(*couple(1))
            close(*couple(0))
            ar_d[2].middles_swap()
            turn(*couple(2))
            ar_u[2].middles_swap()
            close(*couple(1), *couple(2))
            ar_o.middles_swap()
            for unit in ar_q:
                unit.ends_send()
            ar_d[2].middles_send()
            ar_u[2].middles_send()

        load_tok.wait()
        for way, there in ((0, has_right), (1, has_left)):
            @pl.when(there)
            def _():
                for half in range(2):
                    dx_copy(way, 0, me, half).wait_recv()

                def some(k, carry):
                    at = pl.ds(pl.multiple_of(k * 32, 32), 32)
                    piece = rx[me + way, k // 8, k // 4 % 2, pl.ds(pl.multiple_of(k % 4 * 32, 32), 32)]
                    dx_own[at] += piece.astype(F32)
                    return carry

                lax.fori_loop(0, rows // 32, some, 0)

        values = dv[...].astype(F32)
        centred = values - jnp.mean(values, axis=-1, keepdims=True)
        scale = lax.rsqrt(jnp.mean(centred * centred, axis=-1, keepdims=True) + EPS)
        unit_rows = centred * scale
        d_normed = dx_own[...]
        sums[0:1] = jnp.sum(d_normed * unit_rows, axis=0, keepdims=True)
        sums[1:2] = jnp.sum(d_normed, axis=0, keepdims=True)
        rows8 = sums[...]
        for d in range(GROUPS):
            y, x, core = place_of(d)
            stage_v[y, x, core, 0:8, 0:part_w] = rows8[:, part_w * d : part_w * (d + 1)]
            stage_v[y, x, core, 8 : 8 + CHUNKS] = vec_up[0:CHUNKS, 128 * d : 128 * (d + 1)]
        if fast:
            rs_v.start(0)
        if fast:
            ar_o.middles_send()
            ar_q[0].middles_swap()
            rs_v.finish(0)
            rs_v.start(1)
            ar_q[1].middles_swap()
            ar_q[0].middles_send()
            rs_v.finish(1)
            rs_v.start(2)
            ar_q[2].middles_swap()
            ar_q[1].middles_send()
            rs_v.finish(2)
            ar_v.ends_send()
            ar_q[3].middles_swap()
            ar_q[2].middles_send()
            ar_q[4].middles_swap()
            ar_q[3].middles_send()
        scaled = d_normed * per_row(gain_one)
        dk[...] = (
            d_mid[...]
            + scale
            * (
                scaled
                - jnp.mean(scaled, axis=-1, keepdims=True)
                - unit_rows * jnp.mean(scaled * unit_rows, axis=-1, keepdims=True)
            )
        ).astype(BF)
        keep = [pltpu.make_async_copy(dk, tok_o, out_sem.at[6])]
        keep[0].start()
        if fast:
            ar_q[5].middles_swap()
            ar_v.middles_swap()
            ar_q[4].middles_send()
            ar_q[5].middles_send()
            ar_v.middles_send()
            for unit in (*ar_d, *ar_u, ar_o, ar_v, *ar_q):
                unit.finish()
            done = ((fin_d, fin_d_o), (fin_u, fin_u_o), (fin_o, fin_o_o), (fin_q, fin_q_o), (fin_v, fin_v_o))
            for unit in (*rs_d, *rs_u):
                unit.wait_sends((1, 2))
            for unit in (rs_o, rs_v, *couple(0), *couple(1), *couple(2)):
                unit.wait_sends((0, 1, 2))
        else:
            done = ((stage_u, gq_o), (stage_v, stage_v_o))
        keep += [pltpu.make_async_copy(src, dst, out_sem.at[k]) for k, (src, dst) in enumerate(done)]
        for copy in keep[1:]:
            copy.start()
        for copy in keep:
            copy.wait()

        for place, first, second in ((0, 1, 1), (1, 1, 0), (2, 0, 1), (3, 0, 0)):
            @pl.when(me == place)
            def _():
                for step, way in enumerate((first, first, second)):
                    for half in range(2):
                        dx_copy(way, step, block_at(step), half).wait_send()

    pl.run_scoped(
        attention,
        pltpu.VMEM((2, PAIRS, rows, 128), BF),
        pltpu.VMEM((2, PAIRS, rows, 128), BF),
        pltpu.VMEM((2, PAIRS, 128, rows), BF),
        pltpu.VMEM((width, rows), BF),
        pltpu.VMEM((HEADS, 128, rows), BF),
        pltpu.VMEM((HEADS, HEAD, rows), F32),
        pltpu.VMEM((width, width), F32),
        pltpu.VMEM((width, width), F32),
        pltpu.VMEM((rows, width), BF),
        pltpu.VMEM((rows, width), BF),
        pltpu.VMEM((rows, width), BF),
        pltpu.VMEM((3, width, width), BF),
        pltpu.VMEM((PAIRS, rows, 128), BF),
        pltpu.VMEM((rows, 128), BF),
    )


def layer_back(fast, *args):
    kn, wp = args[0], args[6]
    seq, _, rows, _ = kn.shape
    width = wp.shape[1]
    span = GROUPS * 128
    part = width // GROUPS
    any_spec = pl.BlockSpec(memory_space=pl.ANY)
    vmem = pl.BlockSpec(memory_space=pltpu.VMEM)
    sds = jax.ShapeDtypeStruct
    cube = (2, 2, 2)
    outs = [sds((rows, width), BF), sds((rows, width), BF)]
    if fast:
        outs += [
            sds((CHUNKS, 128, width), BF), sds((CHUNKS, part, span), BF), sds((part, width), BF),
            sds((PAIRS, part, 384), BF), sds((16, 128), F32),
        ]
    else:
        outs += [
            sds((CHUNKS, *cube, 128, width), BF), sds((CHUNKS, *cube, part, span), BF), sds((*cube, part, width), BF),
            sds((CHUNKS, *cube, part, span), BF), sds((*cube, 16, 128), F32),
        ]
    scratch = [
        pltpu.VMEM((CHUNKS, *cube, 128, width), BF),
        pltpu.VMEM((CHUNKS, *cube, part, span), BF),
        pltpu.VMEM((*cube, part, width), BF),
        pltpu.VMEM((*cube, 16, 128), F32),
        pltpu.VMEM((8, width), F32),
        pltpu.VMEM((8, span), F32),
        pltpu.VMEM((rows, width), BF),
        pltpu.VMEM((HEADS, 128, rows), BF),
        pltpu.VMEM((rows, width), F32),
        pltpu.VMEM((seq + 1, 2, 2, 128, width), BF),
        pltpu.SemaphoreType.DMA((3, CHUNKS, GROUPS)),
        pltpu.SemaphoreType.DMA((2, 4)),
        pltpu.SemaphoreType.DMA((HEADS + 3,)),
        pltpu.SemaphoreType.DMA((7,)),
        pltpu.SemaphoreType.DMA((2, 4, 2)),
        pltpu.SemaphoreType.DMA((2, 4, 2)),
    ]
    if fast:
        d, u, o, q = (128, width), (part, span), (part, width), (part, 384)
        scratch += [
            pltpu.VMEM(shape, BF)
            for shape in (
                (CHUNKS, 2, 2, *d), (CHUNKS, 2, 2, *u), (2, 2, *o), (CHUNKS, 2, *d), (CHUNKS, 2, *u), (2, *o),
                (CHUNKS, *d), (CHUNKS, *u), o, (PAIRS, 2, 2, *q), (PAIRS, 2, *q), (PAIRS, *q),
            )
        ]
        scratch += [pltpu.VMEM((2, 2, 16, 128), F32), pltpu.VMEM((2, 16, 128), F32), pltpu.VMEM((16, 128), F32)]
        for shape in ((CHUNKS, *d), (CHUNKS, *u), o, (PAIRS, *q)):
            scratch += [pltpu.VMEM(shape, BF)] * 2
        scratch += [pltpu.VMEM((16, 128), F32)] * 2
        scratch += [pltpu.SemaphoreType.DMA((14, 3))] * 4
    return pl.pallas_call(
        partial(layer_back_kernel, fast),
        out_shape=outs,
        in_specs=[any_spec] * 14 + [vmem, pl.BlockSpec(memory_space=pltpu.SMEM)] + [vmem] * 6,
        out_specs=[any_spec] * len(outs),
        scratch_shapes=scratch,
        compiler_params=pltpu.CompilerParams(
            collective_id=1, has_side_effects=True, vmem_limit_bytes=62 * MIB
        ),
        name="layer_back",
    )(*args)


def unpack_kernel(fin_d, fin_u, fin_o, fin_q, fin_v, down_o, up_o, out_o, qkv_o, *vec_o):
    chunks, _, _ = fin_d.shape
    part, span = fin_u.shape[1:]
    for c in range(chunks):
        down_o[128 * c : 128 * (c + 1)] = fin_d[c].astype(F32)
        for d in range(GROUPS):
            at = chunk_columns(up_o.shape[1], c, d)
            up_o[:, at : at + 128] = fin_u[c, :, 128 * d : 128 * (d + 1)].astype(F32)
    out_o[...] = fin_o[...].astype(F32)
    for i in range(PAIRS):
        qkv_o[:, 384 * i : 384 * (i + 1)] = fin_q[i].astype(F32)
    for r in range(8):
        vec_o[r][...] = fin_v[r : r + 1, :part].reshape(part)
    vec_o[8][...] = jnp.concatenate([fin_v[8 + c : 9 + c] for c in range(chunks)], axis=1).reshape(128 * chunks)


def unpack(fin_d, fin_u, fin_o, fin_q, fin_v):
    vmem = pl.BlockSpec(memory_space=pltpu.VMEM)
    chunks, _, width = fin_d.shape
    part, span = fin_u.shape[1:]
    sds = jax.ShapeDtypeStruct
    outs = [
        sds((128 * chunks, width), F32), sds((part, span * chunks), F32), sds((part, width), F32),
        sds((part, PAIRS * fin_q.shape[2]), F32),
    ]
    outs += [sds((part,), F32)] * 8 + [sds((128 * chunks,), F32)]
    return pl.pallas_call(
        unpack_kernel, out_shape=outs, in_specs=[vmem] * 5, out_specs=[vmem] * len(outs), name="unpack",
    )(fin_d, fin_u, fin_o, fin_q, fin_v)


def local(
    tokens, cell_lengths, ln1_gain, ln1_shift, w_qkv, b_query, b_value, w_out, b_out,
    ln2_gain, ln2_shift, w_up, b_up, w_down, b_down, cotangent,
):
    bucket_count, local_slots, width = tokens.shape
    ff = w_up.shape[1]
    seq_count = lax.axis_size("seq")
    dp_count = lax.axis_size("dp")
    fast = dp_count == GROUPS
    rows = bucket_count * local_slots
    flat = tokens.reshape(rows, width)
    kn, vn, kt, xt, qn, qt, wp, att_t, attended, lse = gather_attend(
        flat, cell_lengths, ln1_gain, ln1_shift, w_qkv, b_query, b_value, seq_count
    )
    layer_out, tokens_grad, *found = layer_back(
        fast, kn, vn, kt, xt, qn, qt, wp, attended, att_t, flat, cotangent.reshape(rows, width), w_out, w_up, w_down,
        lse, cell_lengths, ln1_gain, b_out, ln2_gain, ln2_shift, b_up, b_down,
    )
    layer_out = layer_out.reshape(tokens.shape)
    tokens_grad = tokens_grad.reshape(tokens.shape)
    if fast:
        down, up, out, qkv, *vectors = unpack(*found)
    else:

        def summed(g):
            share = lax.psum_scatter(g, "dp", scatter_dimension=0, tiled=True)
            return lax.psum(share, "seq").astype(F32)

        g_down, g_up, g_out, g_qkv, packed = found
        g_qkv = g_qkv.reshape(CHUNKS, width, GROUPS * 128)[:, :, :768]
        g_qkv = jnp.moveaxis(g_qkv, 0, 1).reshape(width, 3 * width)
        g_down = jnp.moveaxis(g_down.reshape(CHUNKS, GROUPS, 128, width), 0, 1).reshape(ff, width)
        g_up = jnp.transpose(g_up.reshape(CHUNKS, width, GROUPS, 128), (1, 2, 0, 3)).reshape(width, ff)
        down, up, out, qkv = summed(g_down), summed(g_up), summed(g_out.reshape(width, width)), summed(g_qkv)
        packed = packed.reshape(GROUPS, 16, 128)
        vectors = [packed[:, r, : width // GROUPS].reshape(width) for r in range(8)]
        vectors.append(packed[:, 8 : 8 + CHUNKS].reshape(ff))
        together = jnp.concatenate([v.reshape(dp_count, -1) for v in vectors], axis=1)
        together = lax.psum(together, ("dp", "seq"))
        mine = lax.dynamic_index_in_dim(together, lax.axis_index("dp"), 0, keepdims=False)
        sizes = [v.shape[0] // dp_count for v in vectors]
        vectors = [mine[sum(sizes[:k]) : sum(sizes[: k + 1])] for k in range(len(sizes))]
    g1, s1, bq, bv, bo, g2, s2, bd, bu = vectors
    return layer_out, tokens_grad, g1, s1, qkv, bq, bv, out, bo, g2, s2, up, bu, down, bd


def solution(mesh):
    token_spec = P("dp", "seq", None)
    vector, matrix = P("dp"), P("dp", None)
    placed = (token_spec, P("dp", None)) + (P(),) * 13 + (token_spec,)
    return jax.shard_map(
        local,
        mesh=mesh,
        in_specs=placed,
        out_specs=(
            token_spec, token_spec, vector, vector, matrix, vector, vector, matrix, vector,
            vector, vector, matrix, vector, matrix, vector,
        ),
        check_vma=False,
    )
```

time: 484 us -> 209 us (0.43)
  waiting for transfers between devices: 227 us -> 0 us
  Pallas kernels: 124 us -> 205 us
  matrix products: 44.4 us -> 0 us
  blocking collectives: 44 us -> 0 us
  other arithmetic: 16 us -> 0 us
  between operations: 14.4 us -> 0.68 us
  local copies, waits for them, and re-layouts: 12.8 us -> 2.95 us
    reduce_scatter x5 -> x0, waiting for transfers between devices: 199 us -> none  [the longest x4 136 us: summed(): share = lax.psum_scatter(g, 'dp', scatter_dimension=0, tiled=True)]
    pallas_call x2 -> x3, Pallas kernels: 124 us -> 205 us  [the longest x1 137 us: layer_back(): pl.pallas_call(partial(layer_back_kernel, fast), out_shape=outs, in_specs...]
    dot_general x9 -> x0, matrix products: 44.4 us -> none  [mm(): return jnp.dot(a, b, preferred_element_type=F32)]
    psum x1 -> x0, blocking collectives: 44 us -> none  [local(): packed = lax.psum(packed, ('dp', 'seq'))]
    psum x1 -> x0, waiting for transfers between devices: 28.1 us -> none  [summed(): return lax.psum(share, 'seq').astype(F32)]
    reduce_sum x8 -> x0, other arithmetic: 7.26 us -> none  [the longest x2 2.3 us: normalize(): return centred * lax.rsqrt(variance + EPS) * gain + shift]
    convert_element_type x4 -> x0, other arithmetic: 5.95 us -> none  [summed(): return lax.psum(share, 'seq').astype(F32)]
    reshape x11 -> x0, local copies, waits for them, and re-layouts: 5.59 us -> none  [the longest x4 5.15 us: row(): return v.reshape(1, -1)]
  transfers between devices with their start and end apart: 6 -> 0, of which waited for: 5 -> 0; matrix products, arithmetic and copies ran while one was open for 8% -> 0% of each run, Pallas kernels for 11% -> 0%
where the time goes in v4:
time: 209 us
  Pallas kernels  205 us (98%)
  local copies, waits for them, and re-layouts  2.95 us (1%)
    pallas_call x1, Pallas kernels, layer_back(): pl.pallas_call(partial(layer_back_kernel, fast), out_shape=outs, in_specs...  137 us
    pallas_call x1, Pallas kernels, gather_attend(): pl.pallas_call(gather_kernel, out_shape=outs, in_specs=[any_spec, pl.Bloc...  65 us

profile of v4, /device:TPU:0, one launch (start us, length us, event | category | flops | bytes accessed | tf_op | source)
XLA Modules:
  0.0 208.6 jit_solution(8775654825809264290)
XLA Ops:
  0.6 65.0 %gather_attend.1 = (bf16[4,6,512,128]{3,2,1,0:T(8,128)(2,1)}, bf16[4,6,512,128]{3,2,1,0:T(8,128)(2,1)}, bf16[4,6,128,512]{3,2,1,0:T(8,128)(2,1)}, bf16[4,768,512...) custom-call(bf16[512,768]{1,0:T(8,128)(2,1)} %bitcast.4, ...), custom_call_target="tpu_custom_call" | custom-call | tf_op jit(solution)/shard_map/gather_attend/pallas_call | solution.py:290
  65.6 136.6 %layer_back.1 = (bf16[512,768]{1,0:T(8,128)(2,1)}, bf16[512,768]{1,0:T(8,128)(2,1)}, bf16[3,128,768]{2,1,0:T(8,128)(2,1)}, bf16[3,96,1024]{2,1,0:T(8,128)(2,1)},...) custom-call(bf16[4,6,512,128]{3,2,1,0:T(8,128)(2,1)} %get-tuple-element.45.refs_0_, ...), custom_call_target="tpu_custom_call" | custom-call | tf_op jit(solution)/shard_map/layer_back/pallas_call | solution.py:1170
  202.3 0.0 copy-start
  202.3 3.4 %unpack.1 = (f32[384,768]{1,0:T(8,128)}, f32[96,3072]{1,0:T(8,128)}, f32[96,768]{1,0:T(8,128)}, f32[96,2304]{1,0:T(8,128)}, f32[96]{0:T(128)}, /*index=5*/f32[96...) custom-call(bf16[3,128,768]{2,1,0:T(8,128)(2,1)} %get-tuple-element., ...), custom_call_target="tpu_custom_call" | custom-call | tf_op jit(solution)/shard_map/unpack/pallas_call | solution.py:1209
  205.7 2.1 copy.33
  207.8 0.0 copy-done
  207.8 0.9 copy.34
Async XLA Ops:
  202.3 5.5 %copy-start = (bf16[512,768]{1,0:T(8,128)(2,1)S(1)}, bf16[512,768]{1,0:T(8,128)(2,1)}, u32[]{:S(2)}) copy-start(bf16[512,768]{1,0:T(8,128)(2,1)} %get-tuple-element.56) | copy-start | bytes 2359300

commit v5 on v4

--- a/solution.py
+++ b/solution.py
@@ -88,8 +88,8 @@
 
 def gather_kernel(
     tok, lens, gain, shift, w_h, bq, bv,
-    kn_o, vn_o, kt_o, xt_o, qn_o, qt_o, wp_o, att_f, att_o, lse_o,
-    xr, w, wp, kn, vn, kt, xt, qn, qt, qta, vta, acc, top, send, recv, in_sem, out_sem,
+    kn_o, vn_o, kt_o, xt_o, qn_o, qt_o, wp_o, att_o, lse_o,
+    xr, w, wp, kn, vn, kt, xt, qn, qt, qta, vta, acc, top, att_t, send, recv, in_sem, out_sem,
 ):
     rows, width = tok.shape
     span = rows // 2
@@ -121,13 +121,13 @@
     def _():
         pl.semaphore_wait(barrier, 2)
 
-    def copy(way, hop, half, block):
-        at = pl.ds(half * span, span)
+    def copy(way, hop, quarter, block):
+        at = pl.ds(quarter * (rows // 4), rows // 4)
         return pltpu.make_async_remote_copy(
             src_ref=tok.at[at] if hop == 0 else xr.at[block, at],
             dst_ref=xr.at[block, at],
-            send_sem=send.at[way, hop, half],
-            recv_sem=recv.at[way, hop, half],
+            send_sem=send.at[way, hop, quarter],
+            recv_sem=recv.at[way, hop, quarter],
             device_id={"seq": me - 1 if way == 0 else me + 1},
             device_id_type=MESH,
         )
@@ -141,11 +141,11 @@
     def block_of(way, hop):
         return me + hop if way == 0 else me - hop
 
-    for half in range(2):
+    for quarter in range(4):
         for way in range(2):
             @pl.when(can_send(way))
             def _():
-                copy(way, 0, half, me).start()
+                copy(way, 0, quarter, me).start()
 
     def normed(raw):
         return normalize(raw.astype(F32), gain[...].reshape(1, -1), shift[...].reshape(1, -1)).astype(BF)
@@ -160,7 +160,7 @@
     own_tokens.wait()
     weights.wait()
     sort_weights(w, wp)
-    keep_w = pltpu.make_async_copy(wp, wp_o, out_sem.at[0])
+    keep_w = pltpu.make_async_copy(wp, wp_o, out_sem.at[4, 0])
     keep_w.start()
     q = ((mm(normed(xr[me]), wp[0]) + bq[...].reshape(1, -1)).astype(BF).astype(F32) * (HEAD**-0.5)).astype(BF)
     for i in range(PAIRS):
@@ -172,18 +172,20 @@
         qta[2 * i, 64:] = codes
         qta[2 * i + 1, :64] = codes
         qta[2 * i + 1, 64:] = turned[64:]
-    keep_q = pltpu.make_async_copy(qn, qn_o, out_sem.at[1])
+    keep_q = pltpu.make_async_copy(qn, qn_o, out_sem.at[4, 1])
     keep_q.start()
-    keep_qt = pltpu.make_async_copy(qt, qt_o, out_sem.at[2])
+    keep_qt = pltpu.make_async_copy(qt, qt_o, out_sem.at[4, 2])
     keep_qt.start()
+
+    def keep_att(i):
+        at = pl.ds(128 * i, 128)
+        return pltpu.make_async_copy(att_t.at[at], att_o.at[at], out_sem.at[5, i])
 
     def keeps(step):
         block = block_at(step)
         return [
-            pltpu.make_async_copy(kn.at[block], kn_o.at[block], out_sem.at[3 + 4 * step]),
-            pltpu.make_async_copy(vn.at[block], vn_o.at[block], out_sem.at[4 + 4 * step]),
-            pltpu.make_async_copy(kt.at[block], kt_o.at[block], out_sem.at[5 + 4 * step]),
-            pltpu.make_async_copy(xt.at[block], xt_o.at[block], out_sem.at[6 + 4 * step]),
+            pltpu.make_async_copy(src.at[block], dst.at[block], out_sem.at[step, k])
+            for k, (src, dst) in enumerate(((kn, kn_o), (vn, vn_o), (kt, kt_o), (xt, xt_o)))
         ]
 
     def block_at(step):
@@ -191,26 +193,23 @@
         from_mid = jnp.where(step == 0, me, jnp.where(step == 1, me + 1, jnp.where(step == 2, me - 1, jnp.where(me == 1, seq - 1, 0))))
         return jnp.where(at_end, from_end, from_mid)
 
-    def half_step(turn, carry):
-        step, half = turn // 2, turn % 2
-        for hop in range(1, 4):
-            for part in range(2):
-                due = turn == jnp.where(at_end, 2 * hop + part, 4 * hop - 2 + part)
-                for way in range(2):
-                    @pl.when(due & holds(way, hop))
-                    def _():
-                        copy(way, hop - 1, part, block_of(way, hop)).wait_recv()
-
-                        @pl.when(can_send(way))
-                        def _():
-                            copy(way, hop, part, block_of(way, hop)).start()
-
+    def arrive(due, way, hop, quarter):
+        @pl.when(due & holds(way, hop))
+        def _():
+            block = block_of(way, hop)
+            copy(way, hop - 1, quarter, block).wait_recv()
+
+            @pl.when(can_send(way))
+            def _():
+                copy(way, hop, quarter, block).start()
+
+    def attend(step, part, span):
         block = block_at(step)
-        at = pl.ds(pl.multiple_of(half * span, span), span)
+        at = pl.ds(pl.multiple_of(part * span, span), span)
         x = normed(xr[block, at])
         keys = mm(x, wp[1]).astype(BF)
         values = (mm(x, wp[2]) + bv[...].reshape(1, -1)).astype(BF)
-        hot = key_codes(lens, 2 * block + half, span)
+        hot = key_codes(lens, block * (rows // span) + part, span)
         hot_low, hot_high = hot * low, hot * high
         xt[block, :, at] = x.T
         for i in range(PAIRS):
@@ -219,8 +218,13 @@
             kt[block, i, :, at] = keys[:, cut].T
             vn[block, i, at] = values[:, cut]
             turned = values[:, cut].T
-            vta[2 * i, :64] = turned[:64]
-            vta[2 * i + 1, :64] = turned[64:]
+            vta[2 * i, :64, :span] = turned[:64]
+            vta[2 * i + 1, :64, :span] = turned[64:]
+
+        @pl.when(part == rows // span - 1)
+        def _():
+            for c in keeps(step):
+                c.start()
 
         def one_pair(i, carry):
             pair = kn[block, i, at]
@@ -234,37 +238,53 @@
                 now = jnp.maximum(before, jnp.max(scores[j], axis=0, keepdims=True))
                 raised = jnp.exp(scores[j] - now).astype(BF)
                 top[h] = now
-                acc[h] = acc[h] * jnp.exp(before - now) + mm(vta[h], raised)
+                acc[h] = acc[h] * jnp.exp(before - now) + mm(vta[h, :, :span], raised)
             return carry
 
         lax.fori_loop(0, PAIRS, one_pair, 0)
-        for s in range(4):
-            @pl.when(turn == 2 * s + 1)
-            def _():
-                for c in keeps(s):
-                    c.start()
-
+
+    def half_step(turn, carry):
+        for hop in range(1, 3):
+            for quarter in range(4):
+                first = jnp.where(at_end, 2 * hop, 2 * hop if hop == 1 else -2)
+                for way in range(2):
+                    arrive(turn == first + quarter // 2, way, hop, quarter)
+        attend(turn // 2, turn % 2, rows // 2)
         return carry
 
-    lax.fori_loop(0, 2 * seq, half_step, 0)
-
-    lse_o[...] = jnp.zeros_like(lse_o)
-    for h in range(HEADS):
-        total = acc[h, 64:65]
-        lse_o[h : h + 1] = top[h] + jnp.log(total)
-        att_f[64 * h : 64 * (h + 1)] = acc[h, :64] / total
-    att_o[...] = att_f[...].T.astype(BF)
+    def last_step(turn, carry):
+        for hop in range(2, 4):
+            for quarter in range(4):
+                due = (turn == quarter) & (at_end if hop == 3 else ~at_end)
+                for way in range(2):
+                    arrive(due, way, hop, quarter)
+        attend(seq - 1, turn, rows // 4)
+        return carry
+
+    lax.fori_loop(0, 2 * (seq - 1), half_step, 0)
+    lax.fori_loop(0, 4, last_step, 0)
+
+    for i in range(PAIRS):
+        for j in range(2):
+            h = 2 * i + j
+            total = acc[h, 64:65]
+            lse_o[h : h + 1] = top[h] + jnp.log(total)
+            att_t[64 * h : 64 * (h + 1)] = (acc[h, :64] * (1.0 / total)).astype(BF)
+        keep_att(i).start()
+    lse_o[HEADS:] = jnp.zeros((16 - HEADS, rows), F32)
 
     for way in range(2):
         for hop in range(3):
-            for half in range(2):
+            for quarter in range(4):
                 @pl.when(can_send(way) & holds(way, hop))
                 def _():
-                    copy(way, hop, half, block_of(way, hop)).wait_send()
+                    copy(way, hop, quarter, block_of(way, hop)).wait_send()
 
     keep_w.wait()
     keep_q.wait()
     keep_qt.wait()
+    for i in range(PAIRS):
+        keep_att(i).wait()
     for step in range(4):
         for c in keeps(step):
             c.wait()
@@ -283,15 +303,14 @@
         sds((PAIRS, rows, 128), BF),
         sds((PAIRS, 128, rows), BF),
         sds((3, width, width), BF),
-        sds((width, rows), F32),
-        sds((rows, width), BF),
+        sds((width, rows), BF),
         sds((16, rows), F32),
     ]
     return pl.pallas_call(
         gather_kernel,
         out_shape=outs,
         in_specs=[any_spec, pl.BlockSpec(memory_space=pltpu.SMEM), vmem, vmem, any_spec, vmem, vmem],
-        out_specs=[any_spec] * 7 + [vmem] * 3,
+        out_specs=[any_spec] * 8 + [vmem],
         scratch_shapes=[
             pltpu.VMEM((seq, rows, width), BF),
             pltpu.VMEM((width, 3 * width), BF),
@@ -306,10 +325,11 @@
             pltpu.VMEM((HEADS, 80, rows // 2), BF),
             pltpu.VMEM((HEADS, 80, rows), F32),
             pltpu.VMEM((HEADS, 1, rows), F32),
-            pltpu.SemaphoreType.DMA((2, 4, 2)),
-            pltpu.SemaphoreType.DMA((2, 4, 2)),
+            pltpu.VMEM((width, rows), BF),
+            pltpu.SemaphoreType.DMA((2, 4, 4)),
+            pltpu.SemaphoreType.DMA((2, 4, 4)),
             pltpu.SemaphoreType.DMA((2,)),
-            pltpu.SemaphoreType.DMA((20,)),
+            pltpu.SemaphoreType.DMA((6, 6)),
         ],
         compiler_params=pltpu.CompilerParams(
             collective_id=0, has_side_effects=True, vmem_limit_bytes=58 * MIB
@@ -456,7 +476,7 @@
 
 def layer_back_kernel(fast, *refs):
     (
-        kn_h, vn_h, kt_h, xt_h, qn_h, qt_h, wp_h, att_h, att_f_h, tok_h, cot_h, w_out_h, w_up_h, w_down_h,
+        kn_h, vn_h, kt_h, xt_h, qn_h, qt_h, wp_h, att_h, tok_h, cot_h, w_out_h, w_up_h, w_down_h,
         lse, lens, gain_one, b_out, gain, shift, b_up, b_down, *refs,
     ) = refs
     layer_o, tok_o, *refs = refs
@@ -465,7 +485,7 @@
     else:
         gd_o, gu_o, go_o, gq_o, stage_v_o, *refs = refs
     (
-        stage_d, stage_u, stage_o, stage_v, sums, vec_up, d_att, dta, d_mid, rx,
+        stage_d, stage_u, stage_o, stage_v, sums, vec_up, d_att, dta, d_mid, rx, kn, vn, kt, qta, qn,
         ff_sem, in_sem, load_sem, out_sem, dsend, drecv, *refs,
     ) = refs
     rows, width = tok_h.shape
@@ -562,13 +582,32 @@
     stage_v[...] = jnp.zeros_like(stage_v)
     sums[...] = jnp.zeros_like(sums)
 
-    def feed_forward(tok, att, att_f, cot, w_out, wu, wd, d_norm, bias):
+    def block_at(step):
+        b0 = jnp.where(me < 2, seq - 1, 0)
+        b1 = jnp.where(me < 2, seq - 2, 1)
+        b2 = jnp.where(me == 0, 1, jnp.where(me == 1, 0, jnp.where(me == 2, 3, 2)))
+        return jnp.where(step == 0, b0, jnp.where(step == 1, b1, jnp.where(step == 2, b2, me)))
+
+    def loads(step):
+        block, slot = block_at(step), step % 2
+        return [
+            pltpu.make_async_copy(kn_h.at[block], kn.at[slot], in_sem.at[slot, 0]),
+            pltpu.make_async_copy(vn_h.at[block], vn.at[slot], in_sem.at[slot, 1]),
+            pltpu.make_async_copy(kt_h.at[block], kt.at[slot], in_sem.at[slot, 2]),
+        ]
+
+    fills = [pltpu.make_async_copy(qn_h, qn, load_sem.at[HEADS])]
+    for h in range(HEADS):
+        own = pl.ds(64 * (h % 2), 64)
+        fills.append(pltpu.make_async_copy(qt_h.at[h // 2, own], qta.at[h, own], load_sem.at[h]))
+
+    def feed_forward(tok, att_t, cot, w_out, wu, wd, d_norm, bias):
         first = [
             pltpu.make_async_copy(src, dst, ff_sem.at[2, k // GROUPS, k % GROUPS])
-            for k, (src, dst) in enumerate(((tok_h, tok), (att_h, att), (w_out_h, w_out), (cot_h, cot), (att_f_h, att_f)))
+            for k, (src, dst) in enumerate(((att_h, att_t), (w_out_h, w_out), (tok_h, tok), (cot_h, cot)))
         ]
 
-        def loads(c):
+        def weights(c):
             found = []
             for d in range(GROUPS):
                 at = pl.ds(chunk_columns(ff, c, d), 128)
@@ -577,12 +616,21 @@
                 found.append(pltpu.make_async_copy(w_down_h.at[at], wd.at[c % 2, to], ff_sem.at[1, c, d]))
             return found
 
-        for copy in (*first[:3], *loads(0), *first[3:], *loads(1)):
+        for copy in (*first[:3], *weights(0), *first[3:], *weights(1), *loads(0), *fills):
             copy.start()
+        codes = query_codes(lens, me, rows)[:16]
+        row16 = lax.broadcasted_iota(jnp.int32, (16, rows), 0)
+        for h in range(HEADS):
+            other = 64 * (1 - h % 2)
+            extra = codes
+            for r, part in enumerate(three_parts(-lse[h : h + 1])):
+                extra = jnp.where(row16 == 8 + r, part, extra)
+            qta[h, other : other + 16] = extra.astype(BF)
+            qta[h, other + 16 : other + 64] = jnp.zeros((48, rows), BF)
         meet()
         for copy in first[:3]:
             copy.wait()
-        middle = tok[...].astype(F32) + mm(att[...], w_out[...]) + per_row(b_out)
+        middle = tok[...].astype(F32) + mm(att_t[...].T, w_out[...]) + per_row(b_out)
         average = jnp.mean(middle, axis=-1, keepdims=True)
         centred = middle - average
         scale = lax.rsqrt(jnp.mean(centred * centred, axis=-1, keepdims=True) + EPS)
@@ -600,7 +648,7 @@
         d_norm[...] = jnp.zeros_like(d_norm)
 
         def one_chunk(c, carry):
-            for copy in loads(c):
+            for copy in weights(c):
                 copy.wait()
             slot = c % 2
             upper = mm(normed, wu[slot]) + bias[pl.ds(c, 1)]
@@ -644,7 +692,7 @@
 
             @pl.when(c == 0)
             def _():
-                for copy in loads(2):
+                for copy in weights(2):
                     copy.start()
 
             return carry
@@ -666,20 +714,18 @@
         d_mid[...] = d_middle
         d_branch = d_middle.astype(BF)
         sums[4:5] = jnp.sum(d_branch.astype(F32), axis=0, keepdims=True)
-        g_out = mm(att_f[...].astype(BF), d_branch).astype(BF)
+        g_out = mm(att_t[...], d_branch).astype(BF)
         for d in range(GROUPS):
             stage_o[place_of(d)] = g_out[96 * d : 96 * (d + 1)]
         if fast:
             rs_o.start(0)
-            for unit_sum in (rs_d[2], rs_u[2]):
-                unit_sum.finish(0)
             close(rs_d[0], rs_u[0])
             ar_d[0].ends_send()
             ar_u[0].ends_send()
         d_attended = mm_nt(d_branch, w_out[...]).astype(BF)
         d_att[...] = d_attended
         turned = d_attended.T
-        product = turned.astype(F32) * att_f[...]
+        product = turned.astype(F32) * att_t[...].astype(F32)
         row16 = lax.broadcasted_iota(jnp.int32, (16, rows), 0)
         for h in range(HEADS):
             own, other = 64 * (h % 2), 64 * (1 - h % 2)
@@ -690,9 +736,7 @@
                 extra = jnp.where(row16 == r, part, extra)
             dta[h, other : other + 16] = extra.astype(BF)
             dta[h, other + 16 : other + 64] = jnp.zeros((48, rows), BF)
-        if fast:
-            rs_o.finish(0)
-        else:
+        if not fast:
             keep = [
                 pltpu.make_async_copy(stage_d, gd_o, out_sem.at[0]),
                 pltpu.make_async_copy(stage_u, gu_o, out_sem.at[1]),
@@ -707,8 +751,7 @@
     pl.run_scoped(
         feed_forward,
         pltpu.VMEM((rows, width), BF),
-        pltpu.VMEM((rows, width), BF),
-        pltpu.VMEM((width, rows), F32),
+        pltpu.VMEM((width, rows), BF),
         pltpu.VMEM((rows, width), BF),
         pltpu.VMEM((width, width), BF),
         pltpu.VMEM((2, width, span), BF),
@@ -717,12 +760,6 @@
         pltpu.VMEM((8, span), F32),
     )
 
-    def block_at(step):
-        b0 = jnp.where(me < 2, seq - 1, 0)
-        b1 = jnp.where(me < 2, seq - 2, 1)
-        b2 = jnp.where(me == 0, 1, jnp.where(me == 1, 0, jnp.where(me == 2, 3, 2)))
-        return jnp.where(step == 0, b0, jnp.where(step == 1, b1, jnp.where(step == 2, b2, me)))
-
     def dx_stage(step, half):
         return stage_d.at[step // 2, step % 2, half]
 
@@ -764,35 +801,14 @@
         def _():
             dx_copy(0, step, block, half).start()
 
-    def attention(kn, vn, kt, xt, qta, dqt, gk, gv, dk, dv, dq, wp, qn, hot_ref):
-        def loads(step):
-            block, slot = block_at(step), step % 2
-            return [
-                pltpu.make_async_copy(kn_h.at[block], kn.at[slot], in_sem.at[slot, 0]),
-                pltpu.make_async_copy(vn_h.at[block], vn.at[slot], in_sem.at[slot, 1]),
-                pltpu.make_async_copy(kt_h.at[block], kt.at[slot], in_sem.at[slot, 2]),
-            ]
-
+    def attention(xt, dqt, gk, gv, dk, dv, dq, wp, hot_ref):
         def load_x(step):
             return pltpu.make_async_copy(xt_h.at[block_at(step)], xt, in_sem.at[0, 3])
 
-        fills = [pltpu.make_async_copy(qn_h, qn, load_sem.at[HEADS])]
-        for h in range(HEADS):
-            own = pl.ds(64 * (h % 2), 64)
-            fills.append(pltpu.make_async_copy(qt_h.at[h // 2, own], qta.at[h, own], load_sem.at[h]))
         load_wp = pltpu.make_async_copy(wp_h, wp, load_sem.at[HEADS + 1])
-        for copy in (*loads(0), *fills, load_x(0), load_wp):
+        for copy in (load_x(0), load_wp):
             copy.start()
         low, high = lane_halves()
-        codes = query_codes(lens, me, rows)[:16]
-        row16 = lax.broadcasted_iota(jnp.int32, (16, rows), 0)
-        for h in range(HEADS):
-            other = 64 * (1 - h % 2)
-            extra = codes
-            for r, part in enumerate(three_parts(-lse[h : h + 1])):
-                extra = jnp.where(row16 == 8 + r, part, extra)
-            qta[h, other : other + 16] = extra.astype(BF)
-            qta[h, other + 16 : other + 64] = jnp.zeros((48, rows), BF)
         dqt[...] = jnp.zeros_like(dqt)
         lane = lax.broadcasted_iota(jnp.int32, (1, 128), 1)
         v_low = jnp.where(lane < 3, 1.0, 0.0).astype(BF)
@@ -815,10 +831,10 @@
             def second():
                 turn(rs_d[1], rs_u[1])
                 for unit_sum in (rs_d[2], rs_u[2], rs_o):
+                    unit_sum.finish(0)
                     unit_sum.start(1)
 
-            at(5, second)
-            at(6, lambda: (ar_d[0].middles_swap(), ar_u[0].middles_swap()))
+            at(6, lambda: (second(), ar_d[0].middles_swap(), ar_u[0].middles_swap()))
             at(12, lambda: (close(rs_d[1], rs_u[1]), ar_d[1].ends_send(), ar_u[1].ends_send()))
             at(14, lambda: relay_far(0, 0))
             at(16, lambda: (ar_d[0].middles_send(), ar_u[0].middles_send()))
@@ -1041,20 +1057,6 @@
         if fast:
             ar_o.middles_send()
             ar_q[0].middles_swap()
-            rs_v.finish(0)
-            rs_v.start(1)
-            ar_q[1].middles_swap()
-            ar_q[0].middles_send()
-            rs_v.finish(1)
-            rs_v.start(2)
-            ar_q[2].middles_swap()
-            ar_q[1].middles_send()
-            rs_v.finish(2)
-            ar_v.ends_send()
-            ar_q[3].middles_swap()
-            ar_q[2].middles_send()
-            ar_q[4].middles_swap()
-            ar_q[3].middles_send()
         scaled = d_normed * per_row(gain_one)
         dk[...] = (
             d_mid[...]
@@ -1068,7 +1070,21 @@
         keep = [pltpu.make_async_copy(dk, tok_o, out_sem.at[6])]
         keep[0].start()
         if fast:
+            ar_q[1].middles_swap()
+            rs_v.finish(0)
+            rs_v.start(1)
+            ar_q[2].middles_swap()
+            ar_q[0].middles_send()
+            rs_v.finish(1)
+            rs_v.start(2)
+            ar_q[3].middles_swap()
+            ar_q[1].middles_send()
+            rs_v.finish(2)
+            ar_v.ends_send()
+            ar_q[4].middles_swap()
+            ar_q[2].middles_send()
             ar_q[5].middles_swap()
+            ar_q[3].middles_send()
             ar_v.middles_swap()
             ar_q[4].middles_send()
             ar_q[5].middles_send()
@@ -1097,11 +1113,7 @@
 
     pl.run_scoped(
         attention,
-        pltpu.VMEM((2, PAIRS, rows, 128), BF),
-        pltpu.VMEM((2, PAIRS, rows, 128), BF),
-        pltpu.VMEM((2, PAIRS, 128, rows), BF),
         pltpu.VMEM((width, rows), BF),
-        pltpu.VMEM((HEADS, 128, rows), BF),
         pltpu.VMEM((HEADS, HEAD, rows), F32),
         pltpu.VMEM((width, width), F32),
         pltpu.VMEM((width, width), F32),
@@ -1109,7 +1121,6 @@
         pltpu.VMEM((rows, width), BF),
         pltpu.VMEM((rows, width), BF),
         pltpu.VMEM((3, width, width), BF),
-        pltpu.VMEM((PAIRS, rows, 128), BF),
         pltpu.VMEM((rows, 128), BF),
     )
 
@@ -1146,6 +1157,11 @@
         pltpu.VMEM((HEADS, 128, rows), BF),
         pltpu.VMEM((rows, width), F32),
         pltpu.VMEM((seq + 1, 2, 2, 128, width), BF),
+        pltpu.VMEM((2, PAIRS, rows, 128), BF),
+        pltpu.VMEM((2, PAIRS, rows, 128), BF),
+        pltpu.VMEM((2, PAIRS, 128, rows), BF),
+        pltpu.VMEM((HEADS, 128, rows), BF),
+        pltpu.VMEM((PAIRS, rows, 128), BF),
         pltpu.SemaphoreType.DMA((3, CHUNKS, GROUPS)),
         pltpu.SemaphoreType.DMA((2, 4)),
         pltpu.SemaphoreType.DMA((HEADS + 3,)),
@@ -1170,7 +1186,7 @@
     return pl.pallas_call(
         partial(layer_back_kernel, fast),
         out_shape=outs,
-        in_specs=[any_spec] * 14 + [vmem, pl.BlockSpec(memory_space=pltpu.SMEM)] + [vmem] * 6,
+        in_specs=[any_spec] * 13 + [vmem, pl.BlockSpec(memory_space=pltpu.SMEM)] + [vmem] * 6,
         out_specs=[any_spec] * len(outs),
         scratch_shapes=scratch,
         compiler_params=pltpu.CompilerParams(
@@ -1180,7 +1196,12 @@
     )(*args)
 
 
-def unpack_kernel(fin_d, fin_u, fin_o, fin_q, fin_v, down_o, up_o, out_o, qkv_o, *vec_o):
+def unpack_kernel(fin_d, fin_u, fin_o, fin_q, fin_v, layer, grad, layer_o, grad_o, down_o, up_o, out_o, qkv_o, *refs):
+    *vec_o, held, sem = refs
+    inward = [pltpu.make_async_copy(src, held.at[k], sem.at[0, k]) for k, src in enumerate((layer, grad))]
+    outward = [pltpu.make_async_copy(held.at[k], dst, sem.at[1, k]) for k, dst in enumerate((layer_o, grad_o))]
+    for copy in inward:
+        copy.start()
     chunks, _, _ = fin_d.shape
     part, span = fin_u.shape[1:]
     for c in range(chunks):
@@ -1188,27 +1209,36 @@
         for d in range(GROUPS):
             at = chunk_columns(up_o.shape[1], c, d)
             up_o[:, at : at + 128] = fin_u[c, :, 128 * d : 128 * (d + 1)].astype(F32)
+    for k in range(2):
+        inward[k].wait()
+        outward[k].start()
     out_o[...] = fin_o[...].astype(F32)
     for i in range(PAIRS):
         qkv_o[:, 384 * i : 384 * (i + 1)] = fin_q[i].astype(F32)
     for r in range(8):
         vec_o[r][...] = fin_v[r : r + 1, :part].reshape(part)
     vec_o[8][...] = jnp.concatenate([fin_v[8 + c : 9 + c] for c in range(chunks)], axis=1).reshape(128 * chunks)
-
-
-def unpack(fin_d, fin_u, fin_o, fin_q, fin_v):
+    for copy in outward:
+        copy.wait()
+
+
+def unpack(fin_d, fin_u, fin_o, fin_q, fin_v, layer, grad):
     vmem = pl.BlockSpec(memory_space=pltpu.VMEM)
+    any_spec = pl.BlockSpec(memory_space=pl.ANY)
     chunks, _, width = fin_d.shape
     part, span = fin_u.shape[1:]
     sds = jax.ShapeDtypeStruct
     outs = [
+        sds(layer.shape, BF), sds(grad.shape, BF),
         sds((128 * chunks, width), F32), sds((part, span * chunks), F32), sds((part, width), F32),
         sds((part, PAIRS * fin_q.shape[2]), F32),
     ]
     outs += [sds((part,), F32)] * 8 + [sds((128 * chunks,), F32)]
     return pl.pallas_call(
-        unpack_kernel, out_shape=outs, in_specs=[vmem] * 5, out_specs=[vmem] * len(outs), name="unpack",
-    )(fin_d, fin_u, fin_o, fin_q, fin_v)
+        unpack_kernel, out_shape=outs, in_specs=[vmem] * 5 + [any_spec] * 2,
+        out_specs=[any_spec] * 2 + [vmem] * (len(outs) - 2),
+        scratch_shapes=[pltpu.VMEM((2, *layer.shape), BF), pltpu.SemaphoreType.DMA((2, 2))], name="unpack",
+    )(fin_d, fin_u, fin_o, fin_q, fin_v, layer, grad)
 
 
 def local(
@@ -1222,17 +1252,15 @@
     fast = dp_count == GROUPS
     rows = bucket_count * local_slots
     flat = tokens.reshape(rows, width)
-    kn, vn, kt, xt, qn, qt, wp, att_t, attended, lse = gather_attend(
+    kn, vn, kt, xt, qn, qt, wp, att_t, lse = gather_attend(
         flat, cell_lengths, ln1_gain, ln1_shift, w_qkv, b_query, b_value, seq_count
     )
     layer_out, tokens_grad, *found = layer_back(
-        fast, kn, vn, kt, xt, qn, qt, wp, attended, att_t, flat, cotangent.reshape(rows, width), w_out, w_up, w_down,
+        fast, kn, vn, kt, xt, qn, qt, wp, att_t, flat, cotangent.reshape(rows, width), w_out, w_up, w_down,
         lse, cell_lengths, ln1_gain, b_out, ln2_gain, ln2_shift, b_up, b_down,
     )
-    layer_out = layer_out.reshape(tokens.shape)
-    tokens_grad = tokens_grad.reshape(tokens.shape)
     if fast:
-        down, up, out, qkv, *vectors = unpack(*found)
+        layer_out, tokens_grad, down, up, out, qkv, *vectors = unpack(*found, layer_out, tokens_grad)
     else:
 
         def summed(g):
@@ -1253,6 +1281,8 @@
         mine = lax.dynamic_index_in_dim(together, lax.axis_index("dp"), 0, keepdims=False)
         sizes = [v.shape[0] // dp_count for v in vectors]
         vectors = [mine[sum(sizes[:k]) : sum(sizes[: k + 1])] for k in range(len(sizes))]
+    layer_out = layer_out.reshape(tokens.shape)
+    tokens_grad = tokens_grad.reshape(tokens.shape)
     g1, s1, bq, bv, bo, g2, s2, bd, bu = vectors
     return layer_out, tokens_grad, g1, s1, qkv, bq, bv, out, bo, g2, s2, up, bu, down, bd
 

time: 209 us -> 200 us (0.957)
  Pallas kernels: 205 us -> 198 us
  local copies, waits for them, and re-layouts: 2.95 us -> 0 us
    pallas_call x1, Pallas kernels: 137 us -> 130 us  [layer_back(): pl.pallas_call(partial(layer_back_kernel, fast), out_shape=outs, in_specs...]
    unnamed x4 -> x0, local copies, waits for them, and re-layouts: 2.95 us -> none
    pallas_call x1, Pallas kernels: 3.43 us -> 5.53 us  [unpack(): pl.pallas_call(unpack_kernel, out_shape=outs, in_specs=[vmem] * 5 + [any_...]
where the time goes in v5:
time: 200 us; the launch traced here: 199 us
  Pallas kernels  198 us (99%)
    pallas_call x1, Pallas kernels, layer_back(): pl.pallas_call(partial(layer_back_kernel, fast), out_shape=outs, in_specs...  130 us
    pallas_call x1, Pallas kernels, gather_attend(): pl.pallas_call(gather_kernel, out_shape=outs, in_specs=[any_spec, pl.Bloc...  63.4 us
    pallas_call x1, Pallas kernels, unpack(): pl.pallas_call(unpack_kernel, out_shape=outs, in_specs=[vmem] * 5 + [any_...  5.53 us

profile of v5, /device:TPU:0, one launch (start us, length us, event | category | flops | bytes accessed | tf_op | source)
XLA Modules:
  0.0 199.3 jit_solution(2739679856145590982)
XLA Ops:
  0.6 63.4 %gather_attend.1 = (bf16[4,6,512,128]{3,2,1,0:T(8,128)(2,1)}, bf16[4,6,512,128]{3,2,1,0:T(8,128)(2,1)}, bf16[4,6,128,512]{3,2,1,0:T(8,128)(2,1)}, bf16[4,768,512...) custom-call(bf16[512,768]{1,0:T(8,128)(2,1)} %bitcast.4, ...), custom_call_target="tpu_custom_call" | custom-call | tf_op jit(solution)/shard_map/gather_attend/pallas_call | solution.py:309
  64.0 129.6 %layer_back.1 = (bf16[512,768]{1,0:T(8,128)(2,1)}, bf16[512,768]{1,0:T(8,128)(2,1)}, bf16[3,128,768]{2,1,0:T(8,128)(2,1)}, bf16[3,96,1024]{2,1,0:T(8,128)(2,1)},...) custom-call(bf16[4,6,512,128]{3,2,1,0:T(8,128)(2,1)} %get-tuple-element.46.refs_0_, ...), custom_call_target="tpu_custom_call" | custom-call | tf_op jit(solution)/shard_map/layer_back/pallas_call | solution.py:1186
  193.6 5.5 %unpack.1 = (bf16[512,768]{1,0:T(8,128)(2,1)}, bf16[512,768]{1,0:T(8,128)(2,1)}, f32[384,768]{1,0:T(8,128)}, f32[96,3072]{1,0:T(8,128)}, f32[96,768]{1,0:T(8,128...) custom-call(bf16[3,128,768]{2,1,0:T(8,128)(2,1)} %get-tuple-element., ...), custom_call_target="tpu_custom_call" | custom-call | tf_op jit(solution)/shard_map/unpack/pallas_call | solution.py:1237

commit v6 on v5

--- a/solution.py
+++ b/solution.py
@@ -88,8 +88,8 @@
 
 def gather_kernel(
     tok, lens, gain, shift, w_h, bq, bv,
-    kn_o, vn_o, kt_o, xt_o, qn_o, qt_o, wp_o, att_o, lse_o,
-    xr, w, wp, kn, vn, kt, xt, qn, qt, qta, vta, acc, top, att_t, send, recv, in_sem, out_sem,
+    kn_o, vn_o, kt_o, xt_o, qn_o, qt_o, wp_o, att_o, lse_h,
+    xr, w, wp, kn, vn, kt, xt, qn, qt, qta, vta, acc, top, att_t, lse_o, send, recv, in_sem, out_sem,
 ):
     rows, width = tok.shape
     span = rows // 2
@@ -272,6 +272,8 @@
             att_t[64 * h : 64 * (h + 1)] = (acc[h, :64] * (1.0 / total)).astype(BF)
         keep_att(i).start()
     lse_o[HEADS:] = jnp.zeros((16 - HEADS, rows), F32)
+    keep_lse = pltpu.make_async_copy(lse_o, lse_h, out_sem.at[4, 4])
+    keep_lse.start()
 
     for way in range(2):
         for hop in range(3):
@@ -285,6 +287,7 @@
     keep_qt.wait()
     for i in range(PAIRS):
         keep_att(i).wait()
+    keep_lse.wait()
     for step in range(4):
         for c in keeps(step):
             c.wait()
@@ -310,7 +313,7 @@
         gather_kernel,
         out_shape=outs,
         in_specs=[any_spec, pl.BlockSpec(memory_space=pltpu.SMEM), vmem, vmem, any_spec, vmem, vmem],
-        out_specs=[any_spec] * 8 + [vmem],
+        out_specs=[any_spec] * 9,
         scratch_shapes=[
             pltpu.VMEM((seq, rows, width), BF),
             pltpu.VMEM((width, 3 * width), BF),
@@ -326,6 +329,7 @@
             pltpu.VMEM((HEADS, 80, rows), F32),
             pltpu.VMEM((HEADS, 1, rows), F32),
             pltpu.VMEM((width, rows), BF),
+            pltpu.VMEM((16, rows), F32),
             pltpu.SemaphoreType.DMA((2, 4, 4)),
             pltpu.SemaphoreType.DMA((2, 4, 4)),
             pltpu.SemaphoreType.DMA((2,)),
@@ -1089,18 +1093,20 @@
             ar_q[4].middles_send()
             ar_q[5].middles_send()
             ar_v.middles_send()
-            for unit in (*ar_d, *ar_u, ar_o, ar_v, *ar_q):
-                unit.finish()
-            done = ((fin_d, fin_d_o), (fin_u, fin_u_o), (fin_o, fin_o_o), (fin_q, fin_q_o), (fin_v, fin_v_o))
+            done = ((ar_d, fin_d, fin_d_o), (ar_u, fin_u, fin_u_o), ((ar_o,), fin_o, fin_o_o), (ar_q, fin_q, fin_q_o), ((ar_v,), fin_v, fin_v_o))
+            for k, (units, src, dst) in enumerate(done):
+                for unit in units:
+                    unit.finish()
+                keep.append(pltpu.make_async_copy(src, dst, out_sem.at[k]))
+                keep[-1].start()
             for unit in (*rs_d, *rs_u):
                 unit.wait_sends((1, 2))
             for unit in (rs_o, rs_v, *couple(0), *couple(1), *couple(2)):
                 unit.wait_sends((0, 1, 2))
         else:
-            done = ((stage_u, gq_o), (stage_v, stage_v_o))
-        keep += [pltpu.make_async_copy(src, dst, out_sem.at[k]) for k, (src, dst) in enumerate(done)]
-        for copy in keep[1:]:
-            copy.start()
+            for k, (src, dst) in enumerate(((stage_u, gq_o), (stage_v, stage_v_o))):
+                keep.append(pltpu.make_async_copy(src, dst, out_sem.at[k]))
+                keep[-1].start()
         for copy in keep:
             copy.wait()
 
@@ -1196,25 +1202,46 @@
     )(*args)
 
 
-def unpack_kernel(fin_d, fin_u, fin_o, fin_q, fin_v, layer, grad, layer_o, grad_o, down_o, up_o, out_o, qkv_o, *refs):
-    *vec_o, held, sem = refs
-    inward = [pltpu.make_async_copy(src, held.at[k], sem.at[0, k]) for k, src in enumerate((layer, grad))]
-    outward = [pltpu.make_async_copy(held.at[k], dst, sem.at[1, k]) for k, dst in enumerate((layer_o, grad_o))]
+def unpack_kernel(
+    fin_d, fin_u, fin_o, fin_q, fin_v, layer, grad, layer_o, grad_o, down_o, up_o, out_o, qkv_o, *refs
+):
+    *vec_o, a_d, a_u, a_o, a_q, down, up, out, qkv, held, in_sem, out_sem = refs
+    inward = [
+        pltpu.make_async_copy(src, dst, in_sem.at[k])
+        for k, (src, dst) in enumerate(
+            ((fin_u, a_u), (fin_d, a_d), (fin_q, a_q), (fin_o, a_o), (layer, held.at[0]), (grad, held.at[1]))
+        )
+    ]
+    outward = [
+        pltpu.make_async_copy(src, dst, out_sem.at[k])
+        for k, (src, dst) in enumerate(
+            ((up, up_o), (down, down_o), (qkv, qkv_o), (out, out_o), (held.at[0], layer_o), (held.at[1], grad_o))
+        )
+    ]
     for copy in inward:
         copy.start()
-    chunks, _, _ = fin_d.shape
-    part, span = fin_u.shape[1:]
+    chunks, _, _ = a_d.shape
+    part = a_u.shape[1]
+    inward[0].wait()
     for c in range(chunks):
-        down_o[128 * c : 128 * (c + 1)] = fin_d[c].astype(F32)
         for d in range(GROUPS):
-            at = chunk_columns(up_o.shape[1], c, d)
-            up_o[:, at : at + 128] = fin_u[c, :, 128 * d : 128 * (d + 1)].astype(F32)
-    for k in range(2):
+            at = chunk_columns(up.shape[1], c, d)
+            up[:, at : at + 128] = a_u[c, :, 128 * d : 128 * (d + 1)].astype(F32)
+    outward[0].start()
+    inward[1].wait()
+    for c in range(chunks):
+        down[128 * c : 128 * (c + 1)] = a_d[c].astype(F32)
+    outward[1].start()
+    inward[2].wait()
+    for i in range(PAIRS):
+        qkv[:, 384 * i : 384 * (i + 1)] = a_q[i].astype(F32)
+    outward[2].start()
+    inward[3].wait()
+    out[...] = a_o[...].astype(F32)
+    outward[3].start()
+    for k in (4, 5):
         inward[k].wait()
         outward[k].start()
-    out_o[...] = fin_o[...].astype(F32)
-    for i in range(PAIRS):
-        qkv_o[:, 384 * i : 384 * (i + 1)] = fin_q[i].astype(F32)
     for r in range(8):
         vec_o[r][...] = fin_v[r : r + 1, :part].reshape(part)
     vec_o[8][...] = jnp.concatenate([fin_v[8 + c : 9 + c] for c in range(chunks)], axis=1).reshape(128 * chunks)
@@ -1228,16 +1255,21 @@
     chunks, _, width = fin_d.shape
     part, span = fin_u.shape[1:]
     sds = jax.ShapeDtypeStruct
-    outs = [
-        sds(layer.shape, BF), sds(grad.shape, BF),
-        sds((128 * chunks, width), F32), sds((part, span * chunks), F32), sds((part, width), F32),
-        sds((part, PAIRS * fin_q.shape[2]), F32),
-    ]
+    large = [(128 * chunks, width), (part, span * chunks), (part, width), (part, PAIRS * fin_q.shape[2])]
+    outs = [sds(layer.shape, BF), sds(grad.shape, BF)] + [sds(shape, F32) for shape in large]
     outs += [sds((part,), F32)] * 8 + [sds((128 * chunks,), F32)]
     return pl.pallas_call(
-        unpack_kernel, out_shape=outs, in_specs=[vmem] * 5 + [any_spec] * 2,
-        out_specs=[any_spec] * 2 + [vmem] * (len(outs) - 2),
-        scratch_shapes=[pltpu.VMEM((2, *layer.shape), BF), pltpu.SemaphoreType.DMA((2, 2))], name="unpack",
+        unpack_kernel, out_shape=outs, in_specs=[any_spec] * 4 + [vmem] + [any_spec] * 2,
+        out_specs=[any_spec] * 6 + [vmem] * 9,
+        scratch_shapes=[
+            *(pltpu.VMEM(ref.shape, BF) for ref in (fin_d, fin_u, fin_o, fin_q)),
+            *(pltpu.VMEM(shape, F32) for shape in large),
+            pltpu.VMEM((2, *layer.shape), BF),
+            pltpu.SemaphoreType.DMA((6,)),
+            pltpu.SemaphoreType.DMA((6,)),
+        ],
+        compiler_params=pltpu.CompilerParams(vmem_limit_bytes=60 * MIB),
+        name="unpack",
     )(fin_d, fin_u, fin_o, fin_q, fin_v, layer, grad)
 
 

time: 200 us -> 198 us (0.990)
  no operation moved by 1% of the time
where the time goes in v6:
time: 198 us; the launch traced here: 197 us
  Pallas kernels  197 us (99%)
    pallas_call x1, Pallas kernels, layer_back(): pl.pallas_call(partial(layer_back_kernel, fast), out_shape=outs, in_specs...  129 us
    pallas_call x1, Pallas kernels, gather_attend(): pl.pallas_call(gather_kernel, out_shape=outs, in_specs=[any_spec, pl.Bloc...  62.8 us
    pallas_call x1, Pallas kernels, unpack(): pl.pallas_call(unpack_kernel, out_shape=outs, in_specs=[any_spec] * 4 + [...  4.88 us

profile of v6, /device:TPU:0, one launch (start us, length us, event | category | flops | bytes accessed | tf_op | source)
XLA Modules:
  0.0 197.4 jit_solution(10012298998858551870)
XLA Ops:
  0.6 62.8 %gather_attend.1 = (bf16[4,6,512,128]{3,2,1,0:T(8,128)(2,1)}, bf16[4,6,512,128]{3,2,1,0:T(8,128)(2,1)}, bf16[4,6,128,512]{3,2,1,0:T(8,128)(2,1)}, bf16[4,768,512...) custom-call(bf16[512,768]{1,0:T(8,128)(2,1)} %bitcast.4, ...), custom_call_target="tpu_custom_call" | custom-call | tf_op jit(solution)/shard_map/gather_attend/pallas_call | solution.py:312
  63.5 128.9 %layer_back.1 = (bf16[512,768]{1,0:T(8,128)(2,1)}, bf16[512,768]{1,0:T(8,128)(2,1)}, bf16[3,128,768]{2,1,0:T(8,128)(2,1)}, bf16[3,96,1024]{2,1,0:T(8,128)(2,1)},...) custom-call(bf16[4,6,512,128]{3,2,1,0:T(8,128)(2,1)} %get-tuple-element.46.refs_0_, ...), custom_call_target="tpu_custom_call" | custom-call | tf_op jit(solution)/shard_map/layer_back/pallas_call | solution.py:1192
  192.4 4.9 %unpack.1 = (bf16[512,768]{1,0:T(8,128)(2,1)}, bf16[512,768]{1,0:T(8,128)(2,1)}, f32[384,768]{1,0:T(8,128)}, f32[96,3072]{1,0:T(8,128)}, f32[96,768]{1,0:T(8,128...) custom-call(bf16[3,128,768]{2,1,0:T(8,128)(2,1)} %get-tuple-element., ...), custom_call_target="tpu_custom_call" | custom-call | tf_op jit(solution)/shard_map/unpack/pallas_call | solution.py:1261

commit v7 on v6

--- a/solution.py
+++ b/solution.py
@@ -128,7 +128,7 @@
             dst_ref=xr.at[block, at],
             send_sem=send.at[way, hop, quarter],
             recv_sem=recv.at[way, hop, quarter],
-            device_id={"seq": me - 1 if way == 0 else me + 1},
+            device_id={"seq": jnp.maximum(me - 1, 0) if way == 0 else jnp.minimum(me + 1, seq - 1)},
             device_id_type=MESH,
         )
 
@@ -771,7 +771,7 @@
         return pltpu.make_async_remote_copy(
             src_ref=dx_stage(step, half), dst_ref=rx.at[block + way, half],
             send_sem=dsend.at[way, block, half], recv_sem=drecv.at[way, block, half],
-            device_id={"seq": me - 1 if way == 0 else me + 1}, device_id_type=MESH,
+            device_id={"seq": jnp.maximum(me - 1, 0) if way == 0 else jnp.minimum(me + 1, seq - 1)}, device_id_type=MESH,
         )
 
     def store_dx(step, half, value):

time: 198 us -> 198 us (level)
  no operation moved by 1% of the time
where the time goes in v7:
time: 198 us; the launch traced here: 197 us
  Pallas kernels  197 us (99%)
    pallas_call x1, Pallas kernels, layer_back(): pl.pallas_call(partial(layer_back_kernel, fast), out_shape=outs, in_specs...  129 us
    pallas_call x1, Pallas kernels, gather_attend(): pl.pallas_call(gather_kernel, out_shape=outs, in_specs=[any_spec, pl.Bloc...  62.8 us
    pallas_call x1, Pallas kernels, unpack(): pl.pallas_call(unpack_kernel, out_shape=outs, in_specs=[any_spec] * 4 + [...  4.88 us

profile of v7, /device:TPU:0, one launch (start us, length us, event | category | flops | bytes accessed | tf_op | source)
XLA Modules:
  0.0 197.4 jit_solution(16165700729572239067)
XLA Ops:
  0.6 62.8 %gather_attend.1 = (bf16[4,6,512,128]{3,2,1,0:T(8,128)(2,1)}, bf16[4,6,512,128]{3,2,1,0:T(8,128)(2,1)}, bf16[4,6,128,512]{3,2,1,0:T(8,128)(2,1)}, bf16[4,768,512...) custom-call(bf16[512,768]{1,0:T(8,128)(2,1)} %bitcast.4, ...), custom_call_target="tpu_custom_call" | custom-call | tf_op jit(solution)/shard_map/gather_attend/pallas_call | solution.py:312
  63.5 128.9 %layer_back.1 = (bf16[512,768]{1,0:T(8,128)(2,1)}, bf16[512,768]{1,0:T(8,128)(2,1)}, bf16[3,128,768]{2,1,0:T(8,128)(2,1)}, bf16[3,96,1024]{2,1,0:T(8,128)(2,1)},...) custom-call(bf16[4,6,512,128]{3,2,1,0:T(8,128)(2,1)} %get-tuple-element.46.refs_0_, ...), custom_call_target="tpu_custom_call" | custom-call | tf_op jit(solution)/shard_map/layer_back/pallas_call | solution.py:1192
  192.4 4.9 %unpack.1 = (bf16[512,768]{1,0:T(8,128)(2,1)}, bf16[512,768]{1,0:T(8,128)(2,1)}, f32[384,768]{1,0:T(8,128)}, f32[96,3072]{1,0:T(8,128)}, f32[96,768]{1,0:T(8,128...) custom-call(bf16[3,128,768]{2,1,0:T(8,128)(2,1)} %get-tuple-element., ...), custom_call_target="tpu_custom_call" | custom-call | tf_op jit(solution)/shard_map/unpack/pallas_call | solution.py:1261
